TPU v7x, 32 devices: a whole 2x2x4 slice. The times are simulated.
32 devices in a mesh: page: 8 (over z, x), blk: 4 (over y, core).
Axes of the slice: x: 2, y: 2, z: 4, core: 2. Of those that a mesh axis runs over, the one named last changes fastest.
Arguments:
- tokens: bfloat16 [24, 512, 768], P('page', 'blk'), may hold values from -6 to 6
- lengths: int32 [24], P('page'), may hold values from 40 to 512, as said below
- boxes: int32 [24, 512, 4], P('page', 'blk'), may hold values from 0 to 1000
- qkv_weight: bfloat16 [768, 2304], replicated, may hold values from -0.21875 to 0.21875
- qkv_bias: float32 [2304], replicated, may hold values from -3 to 3
- box_weight: bfloat16 [64, 128], replicated, may hold values from -0.5 to 0.5
- out_weight: bfloat16 [768, 768], replicated, may hold values from -1.5 to 1.5
- out_bias: float32 [768], replicated, may hold values from -2 to 2
- norm1_gain: float32 [768], replicated, may hold values from 0.1 to 1.9
- norm1_bias: float32 [768], replicated, may hold values from -2 to 2
- up_weight: bfloat16 [768, 3072], replicated, may hold values from -0.21875 to 0.21875
- up_bias: float32 [3072], replicated, may hold values from -3 to 3
- down_weight: bfloat16 [3072, 768], replicated, may hold values from -0.109375 to 0.109375
- down_bias: float32 [768], replicated, may hold values from -2 to 2
- norm2_gain: float32 [768], replicated, may hold values from 0.1 to 1.9
- norm2_bias: float32 [768], replicated, may hold values from -2 to 2
- cotangent: bfloat16 [24, 512, 768], P('page', 'blk'), may hold values from -6 to 6
Outputs:
- layer_output: bfloat16 [24, 512, 768], P('page', 'blk')
- input_grad: bfloat16 [24, 512, 768], P('page', 'blk')
- qkv_weight_grad: float32 [768, 2304], P('page')
- qkv_bias_grad: float32 [2304], P('page')
- box_weight_grad: float32 [8192], P('page')
- out_weight_grad: float32 [768, 768], P('page')
- out_bias_grad: float32 [768], P('page')
- norm1_gain_grad: float32 [768], P('page')
- norm1_bias_grad: float32 [768], P('page')
- up_weight_grad: float32 [768, 3072], P('page')
- up_bias_grad: float32 [3072], P('page')
- down_weight_grad: float32 [3072, 768], P('page')
- down_bias_grad: float32 [768], P('page')
- norm2_gain_grad: float32 [768], P('page')
- norm2_bias_grad: float32 [768], P('page')
Inputs may be any that keep to these rules, and one draw needn't show every extreme that they name: `lengths`: real tokens of each page; in each aligned run of 3 pages one page is longer than 384, and some page is 512 long.
All inputs are finite; a program needn't handle non-finite values.
Results may differ from a plain program's by a relative error of at most 0.018.
Values may be sent and summed in bfloat16 or wider, within the bound.
A program may use at most 192 MiB of HBM per device.

v0:
```python
import functools

import jax
import jax.numpy as jnp
import numpy as np
from jax import lax
from jax.experimental import pallas as pl
from jax.experimental.pallas import tpu as pltpu
from jax.sharding import PartitionSpec as P

norm_eps = 1e-12

MESH = pl.DeviceIdType.MESH
LANES = 128
SMALL_ROWS = 16
low = jnp.bfloat16
f32 = jnp.float32
ORDERS = ((0, 1, 2), (1, 2, 0), (2, 0, 1))


def flip(page, way):
    x, z = page % 2, page // 2
    if way == 0:
        return z * 2 + (1 - x)
    if way == 1:
        return (z + 1 - 2 * (z % 2)) * 2 + x
    return (3 - z) * 2 + x


def core_of(blk):
    return blk + 1 - 2 * (blk % 2)


def side_of(blk):
    return (blk + 2) % 4


def shard_at(page, order, code):
    for place, way in enumerate(ORDERS[order]):
        if code >> (2 - place) & 1:
            page = flip(page, way)
    return page


def greet(others):
    barrier = pltpu.get_barrier_semaphore()
    for other in others:
        pl.semaphore_signal(barrier, inc=1, device_id=other, device_id_type=MESH)
    pl.semaphore_wait(barrier, len(others))


def remote(src, dst, send_sem, recv_sem, to):
    return pltpu.make_async_remote_copy(
        src_ref=src, dst_ref=dst, send_sem=send_sem, recv_sem=recv_sem, device_id=to,
        device_id_type=MESH,
    )


def dot(a, b):
    return jnp.dot(a, b, preferred_element_type=f32)


def dot_nt(a, b):
    return lax.dot_general(a, b, (((1,), (1,)), ((), ())), preferred_element_type=f32)


def dot_tn(a, b):
    return lax.dot_general(a, b, (((0,), (0,)), ((), ())), preferred_element_type=f32)


def sin_cos(theta):
    turns = jnp.floor(theta * 0.6366197723675814 + 0.5)
    rest = theta - turns * 1.5703125
    rest = rest - turns * 4.837512969970703125e-4
    rest = rest - turns * 7.54978995489188216e-8
    square = rest * rest
    sine = ((-1.9515295891e-4 * square + 8.3321608736e-3) * square - 1.6666654611e-1) * square
    sine = sine * rest + rest
    cosine = (2.443315711809948e-5 * square - 1.388731625493765e-3) * square + 4.166664568298827e-2
    cosine = cosine * square * square - 0.5 * square + 1.0
    quarter = turns.astype(jnp.int32)
    odd = (quarter & 1) == 1
    sine_at = jnp.where(odd, cosine, sine)
    cosine_at = jnp.where(odd, sine, cosine)
    sine_at = jnp.where((quarter & 2) == 2, -sine_at, sine_at)
    cosine_at = jnp.where(((quarter + 1) & 2) == 2, -cosine_at, cosine_at)
    return sine_at, cosine_at


def lane_halves(shape):
    return lax.broadcasted_iota(jnp.int32, shape, 1) < LANES // 2


def turned(both):
    swapped = pltpu.roll(both, LANES // 2, 1)
    left = lane_halves(both.shape)
    return jnp.where(left, -swapped, both), jnp.where(left, both, swapped)


def rotate_key(proj, cosine2, sine2):
    return proj * cosine2 + pltpu.roll(proj, LANES // 2, 1) * sine2


def attend_kernel(
    tokens, boxes, lengths, freq, qkv_w, qkv_b, box2,
    x_out, q_out, k_out, v_out, sc_out, p_out, ctx_out,
    x, box, w_q, w_kv, q, k, v, sc, probs, ctx,
    own_sem, w_sem, out_sem, p_sem, ctx_sem,
    mate_send, mate_recv, side_send, side_recv, pass_send, pass_recv, ctx_send, ctx_recv,
):
    page, blk = lax.axis_index("page"), lax.axis_index("blk")
    core, side_at = blk % 2, blk // 2
    mate, side = (page, core_of(blk)), (page, side_of(blk))
    pages = tokens.shape[0]
    half = w_q.shape[1]
    pairs = half // LANES
    chip = 2 * tokens.shape[1]
    keys = 2 * chip
    scale = 0.125

    def of_half(part):
        return pl.ds(pl.multiple_of(part * 2 * half + core * half, LANES), half)

    loads = [
        pltpu.make_async_copy(qkv_w.at[:, of_half(0)], w_q, w_sem.at[0]),
        pltpu.make_async_copy(qkv_w.at[:, of_half(1)], w_kv.at[:, :half], w_sem.at[1]),
        pltpu.make_async_copy(qkv_w.at[:, of_half(2)], w_kv.at[:, half:], w_sem.at[2]),
    ]
    own = []
    for pg in range(pages):
        own.append(pltpu.make_async_copy(tokens.at[pg], x.at[pg, core], own_sem.at[pg, 0]))
        own.append(pltpu.make_async_copy(boxes.at[pg], box.at[pg, core], own_sem.at[pg, 1]))
    for copy in own:
        copy.start()
    for copy in loads:
        copy.start()
    greet((mate, side))
    to_mate, to_side = [], []
    for pg in range(pages):
        for which, (src, dst) in enumerate(((tokens, x), (boxes, box))):
            to_side.append(
                remote(src.at[pg], dst.at[pg, 2 + core], side_send.at[pg, which], side_recv.at[pg, which], side)
            )
            to_side[-1].start()
            to_mate.append(
                remote(src.at[pg], dst.at[pg, core], mate_send.at[pg, which], mate_recv.at[pg, which], mate)
            )
            to_mate[-1].start()
    for copy in loads:
        copy.wait()

    @pl.loop(0, pages)
    def _(pg):
        passed = []
        for which, (src, dst) in enumerate(((tokens, x), (boxes, box))):
            remote(
                src.at[pg], dst.at[pg, 2 + core], side_send.at[pg, which], side_recv.at[pg, which], side
            ).wait_recv()
            copy = remote(
                dst.at[pg, 2 + core], dst.at[pg, 2 + core], pass_send.at[pg, which],
                pass_recv.at[pg, which], mate,
            )
            copy.start()
            passed.append(copy)
            pltpu.make_async_copy(src.at[pg], dst.at[pg, core], own_sem.at[pg, which]).wait()
            remote(
                src.at[pg], dst.at[pg, core], mate_send.at[pg, which], mate_recv.at[pg, which], mate
            ).wait_recv()
        for copy in passed:
            copy.wait_recv()
        pltpu.make_async_copy(x.at[pg], x_out.at[pg], out_sem.at[pg, 0]).start()
        for at in range(4):
            rows = box[pg, at]
            spread = [
                jnp.broadcast_to(rows[c : c + 1], (freq.shape[0] // 4, LANES)) for c in range(4)
            ]
            sine, cosine = sin_cos(jnp.concatenate(spread, 0) * freq[...])
            sc[pg, at * LANES : (at + 1) * LANES] = jnp.concatenate([sine, cosine], 0).T
        pltpu.make_async_copy(sc.at[pg], sc_out.at[pg], out_sem.at[pg, 1]).start()
        x_all = x[pg].reshape(keys, x.shape[-1])
        q_all = (dot(x_all[:chip], w_q[...]) + qkv_b[:, of_half(0)]).astype(low)
        bias = jnp.concatenate([qkv_b[:, of_half(1)], qkv_b[:, of_half(2)]], 1)
        kv_all = (dot(x_all, w_kv[...]) + bias).astype(low)
        for hp in range(pairs):
            q[pg, hp] = q_all[:, hp * LANES : (hp + 1) * LANES]
            k[pg, hp] = kv_all[:, hp * LANES : (hp + 1) * LANES]
            v[pg, hp] = kv_all[:, half + hp * LANES : half + (hp + 1) * LANES]
        for which, (src, dst) in enumerate(((q, q_out), (k, k_out), (v, v_out))):
            pltpu.make_async_copy(src.at[pg], dst.at[pg], out_sem.at[pg, 2 + which]).start()
        place = lax.broadcasted_iota(jnp.int32, (keys, chip), 0) + side_at * chip
        place = jnp.where(place >= keys, place - keys, place)
        valid = place < lengths[pg]

        @pl.loop(0, pairs)
        def _(hp):
            both = sc[pg]
            cosine2, sine2 = turned(both)
            basis = both.astype(low)
            basis_q = (both[:chip] * scale).astype(low)
            left = lane_halves((chip, LANES))
            cosine_q = jnp.where(left, -cosine2[:chip], cosine2[:chip]) * scale
            sine_q = jnp.where(left, sine2[:chip], -sine2[:chip]) * scale
            q_pair, k_pair = q[pg, hp], k[pg, hp]
            q_proj = dot(q_pair, box2[...])
            k_proj = dot(k_pair, box2[...])
            v_t = v[pg, hp].T
            outs = []
            for e in range(2):
                at = slice(e * LANES, (e + 1) * LANES)
                q_pos = rotate_key(q_proj[:, at], cosine_q, sine_q).astype(low)
                k_pos = rotate_key(k_proj[:, at], cosine2, sine2).astype(low)
                mine = left if e == 0 else jnp.logical_not(left)
                q_own = jnp.where(mine, q_pair.astype(f32) * scale, 0.0).astype(low)
                scores = dot_nt(
                    jnp.concatenate([basis, k_pos], 1), jnp.concatenate([q_pos, basis_q], 1)
                )
                scores = scores + dot_nt(k_pair, q_own)
                scores = jnp.where(valid, scores, -1e30)
                top = jnp.max(scores, axis=0, keepdims=True)
                grown = jnp.exp(scores - top)
                total = jnp.sum(grown, axis=0, keepdims=True)
                p = (grown * (1.0 / total)).astype(low)
                probs[pg, hp, e] = p
                outs.append(dot(v_t[e * LANES // 2 : (e + 1) * LANES // 2], p))
            pltpu.make_async_copy(probs.at[pg, hp], p_out.at[pg, hp], p_sem.at[pg, hp]).start()
            context = jnp.concatenate(outs, 0).T.astype(low)
            lanes = pl.ds(pl.multiple_of(hp * LANES, LANES), LANES)
            ctx[pg, 0, :, lanes] = context[: chip // 2]
            ctx[pg, 1, :, lanes] = context[chip // 2 :]

        mine = pl.ds(pl.multiple_of(core * half, LANES), half)
        pltpu.make_async_copy(ctx.at[pg, core], ctx_out.at[pg, :, mine], ctx_sem.at[pg]).start()
        remote(
            ctx.at[pg, 1 - core], ctx_out.at[pg, :, mine], ctx_send.at[pg], ctx_recv.at[pg], mate
        ).start()
        for copy in passed:
            copy.wait_send()

    mine = pl.ds(pl.multiple_of(core * half, LANES), half)
    for pg in range(pages):
        for which, (src, dst) in enumerate(((x, x_out), (sc, sc_out), (q, q_out), (k, k_out), (v, v_out))):
            pltpu.make_async_copy(src.at[pg], dst.at[pg], out_sem.at[pg, which]).wait()
        for hp in range(pairs):
            pltpu.make_async_copy(probs.at[pg, hp], p_out.at[pg, hp], p_sem.at[pg, hp]).wait()
        pltpu.make_async_copy(ctx.at[pg, core], ctx_out.at[pg, :, mine], ctx_sem.at[pg]).wait()
        remote(
            ctx.at[pg, 1 - core], ctx_out.at[pg, :, mine], ctx_send.at[pg], ctx_recv.at[pg], mate
        ).wait()
    for copy in to_side + to_mate:
        copy.wait_send()


def any_spec():
    return pl.BlockSpec(memory_space=pl.ANY)


def vmem_spec():
    return pl.BlockSpec(memory_space=pltpu.VMEM)


def attend(tokens, boxes, lengths, qkv_w, qkv_b, box_weight):
    pages, block, width = tokens.shape
    head_dim, pos = box_weight.shape
    half = width // 2
    pairs = half // LANES
    chip, keys = 2 * block, 4 * block
    count = pos // 8
    freqs = 10000.0 ** (-np.arange(count) / count)
    freq = jnp.asarray(np.tile(np.tile(freqs, 4)[:, None], (1, LANES)), f32)
    boxes_t = jnp.pad(boxes.astype(f32).transpose(0, 2, 1), ((0, 0), (0, 4), (0, 0)))
    zero = jnp.zeros_like(box_weight)
    box2 = jnp.concatenate(
        [jnp.concatenate([box_weight, zero], 1), jnp.concatenate([zero, box_weight], 1)], 0
    )
    struct = jax.ShapeDtypeStruct
    vmem, dma = pltpu.VMEM, pltpu.SemaphoreType.DMA
    return pl.pallas_call(
        attend_kernel,
        out_shape=(
            struct((pages, 4, block, width), low),
            struct((pages, pairs, chip, LANES), low),
            struct((pages, pairs, keys, LANES), low),
            struct((pages, pairs, keys, LANES), low),
            struct((pages, keys, LANES), f32),
            struct((pages, pairs, 2, keys, chip), low),
            struct((pages, block, width), low),
        ),
        in_specs=[any_spec(), any_spec(), pl.BlockSpec(memory_space=pltpu.SMEM), vmem_spec(), any_spec(), vmem_spec(), vmem_spec()],
        out_specs=(any_spec(),) * 7,
        scratch_shapes=[
            vmem((pages, 4, block, width), low),
            vmem((pages, 4, 8, LANES), f32),
            vmem((width, half), low),
            vmem((width, 2 * half), low),
            vmem((pages, pairs, chip, LANES), low),
            vmem((pages, pairs, keys, LANES), low),
            vmem((pages, pairs, keys, LANES), low),
            vmem((pages, keys, LANES), f32),
            vmem((pages, pairs, 2, keys, chip), low),
            vmem((pages, 2, block, half), low),
            dma((pages, 2)), dma((3,)), dma((pages, 5)), dma((pages, pairs)), dma((pages,)),
            dma((pages, 2)), dma((pages, 2)), dma((pages, 2)), dma((pages, 2)),
            dma((pages, 2)), dma((pages, 2)), dma((pages,)), dma((pages,)),
        ],
        compiler_params=pltpu.CompilerParams(
            collective_id=1, has_side_effects=True, vmem_limit_bytes=56 * 2**20
        ),
        name="attend",
    )(tokens, boxes_t, lengths, freq, qkv_w, qkv_b.reshape(1, -1), box2)


def norm_of(resid):
    center = resid - jnp.mean(resid, axis=-1, keepdims=True)
    spread = jnp.mean(center * center, axis=-1, keepdims=True)
    inverse = lax.rsqrt(spread + norm_eps)
    return center * inverse, inverse


def norm_back(grad, normed, inverse):
    mean = jnp.mean(grad, axis=-1, keepdims=True)
    along = jnp.mean(grad * normed, axis=-1, keepdims=True)
    return inverse * (grad - mean - normed * along)


def column_sum(values):
    return jnp.sum(values, axis=0, keepdims=True)


def feed_kernel(
    ctx, tokens, cotangent, out_w, up_w, down_w, out_b, gain1, shift1, up_b, down_b, gain2, shift2,
    output, dresid1, dctx, packed, g_up_b, g_rows,
    w_out, w_up, w_down, act, slope, norm1, inverse1, hidden, hidden_t, grow, staged, w_sem, up_sem, down_sem, pack_sem,
):
    chunks, chunk = w_up.shape[0], w_up.shape[2]
    width = ctx.shape[1]
    up_pieces = chunk // LANES
    shard = width // 8
    out_load = pltpu.make_async_copy(out_w, w_out, w_sem)
    out_load.start()

    def up_load(j):
        return pltpu.make_async_copy(
            up_w.at[:, pl.ds(pl.multiple_of(j * chunk, LANES), chunk)], w_up.at[j], up_sem.at[j]
        )

    def down_load(j):
        return pltpu.make_async_copy(
            down_w.at[pl.ds(pl.multiple_of(j * chunk, LANES), chunk)], w_down.at[j], down_sem.at[j]
        )

    for j in range(chunks):
        up_load(j).start()
        down_load(j).start()
    out_load.wait()
    resid = tokens[...].astype(f32) + dot(ctx[...], w_out[...]) + out_b[...]
    normed, inverse = norm_of(resid)
    norm1[...] = normed
    inverse1[...] = jnp.broadcast_to(inverse, inverse1.shape)
    first = normed * gain1[...] + shift1[...]
    hidden[...] = first.astype(low)
    hidden_t[...] = first.astype(low).T
    grow[...] = first + down_b[...]

    @pl.loop(0, chunks)
    def _(j):
        up_load(j).wait()
        upper = dot(hidden[...], w_up[j]) + up_b[pl.ds(j, 1)]
        cdf = 0.5 + 0.5 * lax.erf(upper * 0.7071067811865476)
        act_low = (upper * cdf).astype(low)
        act[j] = act_low
        slope[j] = cdf + upper * (jnp.exp(upper * upper * -0.5) * 0.3989422804014327)
        down_load(j).wait()
        grow[...] += dot(act_low, w_down[j])

    normed2, inverse2 = norm_of(grow[...])
    output[...] = (normed2 * gain2[...] + shift2[...]).astype(low)
    cot = cotangent[...].astype(f32)
    g_rows[0:1] = column_sum(cot * normed2)
    g_rows[1:2] = column_sum(cot)
    dresid2 = norm_back(cot * gain2[...], normed2, inverse2)
    dffn = dresid2.astype(low)
    g_rows[2:3] = column_sum(dffn.astype(f32))
    grow[...] = dresid2
    staged[...] = dffn

    @pl.loop(0, chunks)
    def _(j):
        dffn = staged[...]
        dupper = (dot_nt(dffn, w_down[j]) * slope[j]).astype(low)
        g_up_b[pl.ds(j, 1)] = column_sum(dupper.astype(f32))
        grow[...] += dot_nt(dupper, w_up[j])
        grad_up = dot(hidden_t[...], dupper).astype(low)
        for piece in range(up_pieces):
            part = grad_up[:, piece * LANES : (piece + 1) * LANES].reshape(8, shard, LANES)
            packed[j, :, piece * shard : (piece + 1) * shard] = part
        grad_down = dot_tn(act[j], dffn).astype(low)
        for piece in range(up_pieces):
            row = j * up_pieces + piece
            per = up_pieces * chunks // 8
            at = pl.ds(pl.multiple_of(up_pieces * shard + (row % per) * LANES, LANES), LANES)
            for column in range(6):
                packed[column, row // per, at] = grad_down[
                    piece * LANES : (piece + 1) * LANES, column * LANES : (column + 1) * LANES
                ]

    dhidden = grow[...]
    normed = norm1[...]
    g_rows[3:4] = column_sum(dhidden * normed)
    g_rows[4:5] = column_sum(dhidden)
    back = norm_back(dhidden * gain1[...], normed, inverse1[:, :1])
    dresid1[...] = back
    dattn = back.astype(low)
    g_rows[5:6] = column_sum(dattn.astype(f32))
    g_rows[6:8] = jnp.zeros((2, width), f32)
    dctx[...] = dot_nt(dattn, w_out[...]).astype(low)
    grad_out = dot_tn(ctx[...], dattn).astype(low)
    first_row = packed.shape[2] - shard
    for column in range(6):
        part = grad_out[:, column * LANES : (column + 1) * LANES].reshape(8, shard, LANES)
        packed[column, :, first_row:] = part


def feed(ctx, tokens, cotangent, out_w, up_w, down_w, out_b, gain1, shift1, up_b, down_b, gain2, shift2):
    rows, width = ctx.shape
    hidden_width = up_w.shape[1]
    chunks = 6
    chunk = hidden_width // chunks
    shard = width // 8
    packed_rows = (chunk // LANES) * shard + hidden_width // 8 + shard
    struct = jax.ShapeDtypeStruct
    vmem, dma = pltpu.VMEM, pltpu.SemaphoreType.DMA

    def row(vector):
        return vector.reshape(1, -1)

    return pl.pallas_call(
        feed_kernel,
        out_shape=(
            struct((rows, width), low),
            struct((rows, width), f32),
            struct((rows, width), low),
            struct((6, 8, packed_rows, LANES), low),
            struct((chunks, chunk), f32),
            struct((8, width), f32),
        ),
        in_specs=[vmem_spec()] * 3 + [any_spec()] * 3 + [vmem_spec()] * 7,
        out_specs=(vmem_spec(),) * 6,
        scratch_shapes=[
            vmem((width, width), low),
            vmem((chunks, width, chunk), low),
            vmem((chunks, chunk, width), low),
            vmem((chunks, rows, chunk), low),
            vmem((chunks, rows, chunk), f32),
            vmem((rows, width), f32),
            vmem((rows, LANES), f32),
            vmem((rows, width), low),
            vmem((width, rows), low),
            vmem((rows, width), f32),
            vmem((rows, width), low),
            dma, dma((chunks,)), dma((chunks,)), dma,
        ],
        compiler_params=pltpu.CompilerParams(vmem_limit_bytes=60 * 2**20),
        name="feed",
    )(
        ctx, tokens, cotangent, out_w, up_w, down_w, row(out_b), row(gain1), row(shift1),
        up_b.reshape(chunks, chunk), row(down_b), row(gain2), row(shift2),
    )


def attend_back_kernel(
    dctx_own, x_in, q_in, k_in, v_in, sc_in, p_in, qkv_w, box_w, dresid1,
    input_grad, packed, g_bias, g_box,
    x, q, k, v, sc, probs, dctx, dq, dkv, x_t, w_c, dx, dx_mate, dx_side, box_t,
    in_sem, p_sem, w_sem, own_sem, mate_send, mate_recv, core_send, core_recv, side_send, side_recv,
):
    page, blk = lax.axis_index("page"), lax.axis_index("blk")
    core = blk % 2
    mate, side = (page, core_of(blk)), (page, side_of(blk))
    pages, pairs, chip, _ = q.shape
    keys = k.shape[2]
    block = chip // 2
    half = pairs * LANES
    width = x.shape[-1]
    head = LANES // 2
    scale = 0.125

    def of_half(part, which):
        return pl.ds(pl.multiple_of(part * 2 * half + which * half, LANES), half)

    def loads(pg):
        names = ((x_in, x), (q_in, q), (k_in, k), (v_in, v), (sc_in, sc))
        return [
            pltpu.make_async_copy(src.at[pg], dst.at[pg], in_sem.at[pg, at])
            for at, (src, dst) in enumerate(names)
        ]

    def p_load(hp, pg):
        return pltpu.make_async_copy(p_in.at[pg, hp], probs.at[pg, hp], p_sem.at[pg, hp])

    w_loads = [
        pltpu.make_async_copy(qkv_w.at[:, of_half(part, core)], w_c.at[part], w_sem.at[part])
        for part in range(3)
    ]

    def own_copy(pg):
        return pltpu.make_async_copy(
            dctx_own.at[pg, :, of_half(0, core)], dctx.at[pg, core], own_sem.at[pg]
        )

    def mate_copy(pg):
        return remote(
            dctx_own.at[pg, :, of_half(0, 1 - core)], dctx.at[pg, core], mate_send.at[pg],
            mate_recv.at[pg], mate,
        )

    greet((mate, side))
    for pg in range(pages):
        mate_copy(pg).start()
        own_copy(pg).start()
        for copy in loads(pg):
            copy.start()
        p_load(0, pg).start()
    for copy in w_loads:
        copy.start()
    for hp in range(1, pairs):
        for pg in range(pages):
            p_load(hp, pg).start()
    for e in range(2):
        box_t[e] = jnp.zeros_like(box_t[e])
        box_t[e, :, e * head : (e + 1) * head] = box_w[...].astype(f32).T.astype(low)
    g_box[...] = jnp.zeros_like(g_box)
    for pg in range(pages):
        for copy in loads(pg):
            copy.wait()
        x_t[:, pg * keys : (pg + 1) * keys] = x[pg].reshape(keys, width).T
        own_copy(pg).wait()
        mate_copy(pg).wait_recv()

    @pl.loop(0, pairs)
    def _(hp):
        lanes = pl.ds(pl.multiple_of(hp * LANES, LANES), LANES)

        @pl.loop(0, pages)
        def _(pg):
            p_load(hp, pg).wait()
            both = sc[pg]
            cosine2, sine2 = turned(both)
            flat = both.T
            sine_t, cosine_t = flat[:head, :chip], flat[head:, :chip]
            basis = both.astype(low)
            basis_t = flat.astype(low)
            q_pair, k_pair, v_pair = q[pg, hp], k[pg, hp], v[pg, hp]
            q_t, k_t = q_pair.T, k_pair.T
            dc = dctx[pg, :, :, lanes].reshape(chip, LANES)
            left = lane_halves((chip, LANES))
            zero = jnp.zeros_like(dc)
            dk, dv, dqs = 0.0, 0.0, []
            for e in range(2):
                mine = left if e == 0 else jnp.logical_not(left)
                own_rows = slice(e * head, (e + 1) * head)
                p = probs[pg, hp, e]
                dc_own = jnp.where(mine, dc, zero)
                q_own = jnp.where(mine, q_pair, zero)
                dp = dot_nt(v_pair, dc_own)
                p_wide = p.astype(f32)
                delta = jnp.sum(p_wide * dp, axis=0, keepdims=True)
                ds = (p_wide * (dp - delta)).astype(low)
                dv = dv + dot(p, dc_own)
                dk_feat = dot(ds, jnp.concatenate([q_own, basis[:chip]], 1)) * scale
                dq_feat = dot(jnp.concatenate([k_t[own_rows], basis_t], 0), ds) * scale
                dk_proj = rotate_key(dk_feat[:, LANES:], cosine2, sine2).astype(low)
                a, b = dq_feat[head : 2 * head], dq_feat[2 * head :]
                dq_proj = jnp.concatenate(
                    [a * cosine_t - b * sine_t, a * sine_t + b * cosine_t], 0
                ).astype(low)
                dk = dk + dk_feat[:, :LANES] + dot(dk_proj, box_t[e])
                dqs.append(dq_feat[:head] + dot(box_w[...], dq_proj))
                g_box[...] += dot(k_t[own_rows], dk_proj) + dot_nt(q_t[own_rows], dq_proj)
            at = pl.ds(pl.multiple_of(pg * keys, LANES), keys)
            at_q = pl.ds(pl.multiple_of(pg * chip, LANES), chip)
            dq[hp, at_q] = jnp.concatenate(dqs, 0).T.astype(low)
            dkv[hp, at, :LANES] = dk.astype(low)
            dkv[hp, at, LANES:] = dv.astype(low)

        dkv_all = dkv[hp]
        dq_all = dq[hp]
        g_kv = column_sum(dkv_all.astype(f32))
        g_bias[0:1, lanes] = column_sum(dq_all.astype(f32))
        g_bias[1:2, lanes] = g_kv[:, :LANES]
        g_bias[2:3, lanes] = g_kv[:, LANES:]
        grad = dot(x_t[...], dkv_all).astype(low)
        x_q = jnp.concatenate([x_t[:, pg * keys : pg * keys + chip] for pg in range(pages)], 1)
        grad_q = dot(x_q, dq_all).astype(low)
        shard = width // 8
        packed[hp, :, :shard] = grad_q.reshape(8, shard, LANES)
        packed[hp, :, shard : 2 * shard] = grad[:, :LANES].reshape(8, shard, LANES)
        packed[hp, :, 2 * shard :] = grad[:, LANES:].reshape(8, shard, LANES)

    for copy in w_loads:
        copy.wait()

    def core_copy(pg, at):
        return remote(
            dx.at[pg, at, 1 - core], dx_mate.at[pg, at], core_send.at[pg, at], core_recv.at[pg, at],
            mate,
        )

    def side_copy(pg):
        return remote(dx.at[pg, 1, core], dx_side.at[pg], side_send.at[pg], side_recv.at[pg], side)

    @pl.loop(0, pages)
    def _(pg):
        for at in (1, 0):
            rows = pl.ds(pl.multiple_of(pg * keys + at * chip, LANES), chip)
            dks = jnp.concatenate([dkv[hp, rows, :LANES] for hp in range(pairs)], 1)
            dvs = jnp.concatenate([dkv[hp, rows, LANES:] for hp in range(pairs)], 1)
            total = dot_nt(dks, w_c[1]) + dot_nt(dvs, w_c[2])
            if at == 0:
                rows_q = pl.ds(pl.multiple_of(pg * chip, LANES), chip)
                dqs = jnp.concatenate([dq[hp, rows_q] for hp in range(pairs)], 1)
                total = total + dot_nt(dqs, w_c[0])
            dx[pg, at] = total.astype(low).reshape(2, block, width)
            core_copy(pg, at).start()

    @pl.loop(0, pages)
    def _(pg):
        core_copy(pg, 1).wait_recv()
        dx[pg, 1, core] = dx[pg, 1, core] + dx_mate[pg, 1]
        side_copy(pg).start()

    @pl.loop(0, pages)
    def _(pg):
        core_copy(pg, 0).wait_recv()
        side_copy(pg).wait_recv()
        total = dx[pg, 0, core].astype(f32) + dx_mate[pg, 0].astype(f32) + dx_side[pg].astype(f32)
        input_grad[pg] = (total + dresid1[pg]).astype(low)
        for at in range(2):
            core_copy(pg, at).wait_send()
        side_copy(pg).wait_send()
        mate_copy(pg).wait_send()


def attend_back(dctx, x, q, k, v, sc, probs, qkv_w, box_w, dresid1):
    pages, pairs, chip, _ = q.shape
    keys = k.shape[2]
    width = x.shape[-1]
    block = chip // 2
    half = pairs * LANES
    struct = jax.ShapeDtypeStruct
    vmem, dma = pltpu.VMEM, pltpu.SemaphoreType.DMA
    return pl.pallas_call(
        attend_back_kernel,
        out_shape=(
            struct((pages, block, width), low),
            struct((pairs, 8, 3 * width // 8, LANES), low),
            struct((8, half), f32),
            struct(box_w.shape, f32),
        ),
        in_specs=[any_spec()] * 8 + [vmem_spec()] * 2,
        out_specs=(vmem_spec(),) * 4,
        scratch_shapes=[
            vmem((pages, 4, block, width), low),
            vmem((pages, pairs, chip, LANES), low),
            vmem((pages, pairs, keys, LANES), low),
            vmem((pages, pairs, keys, LANES), low),
            vmem((pages, keys, LANES), f32),
            vmem((pages, pairs, 2, keys, chip), low),
            vmem((pages, 2, block, half), low),
            vmem((pairs, pages * chip, LANES), low),
            vmem((pairs, pages * keys, 2 * LANES), low),
            vmem((width, pages * keys), low),
            vmem((3, width, half), low),
            vmem((pages, 2, 2, block, width), low),
            vmem((pages, 2, block, width), low),
            vmem((pages, block, width), low),
            vmem((2, LANES, LANES), low),
            dma((pages, 5)), dma((pages, pairs)), dma((3,)), dma((pages,)), dma((pages,)), dma((pages,)),
            dma((pages, 2)), dma((pages, 2)), dma((pages,)), dma((pages,)),
        ],
        compiler_params=pltpu.CompilerParams(
            collective_id=2, has_side_effects=True, vmem_limit_bytes=60 * 2**20
        ),
        name="attend_back",
    )(dctx, x, q, k, v, sc, probs, qkv_w, box_w, dresid1)


def reduce_kernel(
    packed, small, packed_qkv, up_ref, down_ref, out_ref, qkv_ref, small_ref,
    held, from_core, got1, got2, got3, got_side, total, got_core,
    local_sem, small_sem, qkv_sem, core_send, core_recv, send1, recv1, send2, recv2, send3, recv3,
    side_send, side_recv, last_send, last_recv,
):
    page, blk = lax.axis_index("page"), lax.axis_index("blk")
    core = blk % 2
    mate = (page, core_of(blk))
    side = (page, side_of(blk))
    greet([(flip(page, way), blk) for way in range(3)] + [mate, side])
    wide = packed.shape[2]
    both = wide + SMALL_ROWS
    half = 3 * core

    def send(src, dst, sems, recv, to):
        copy = pltpu.make_async_remote_copy(
            src_ref=src, dst_ref=dst, send_sem=sems, recv_sem=recv, device_id=to,
            device_id_type=MESH,
        )
        copy.start()
        return copy

    codes = (6, 7, 4, 5, 2, 3, 0, 1)
    first, locals_ = {}, {}
    for code in codes:
        for order in range(3):
            shard = shard_at(page, order, code)
            other = 3 - half + order
            first[order, code] = (
                send(
                    packed.at[other, shard], from_core.at[order, code, :wide],
                    core_send.at[order, code, 0], core_recv.at[order, code, 0], mate,
                ),
                send(
                    small.at[other, shard], from_core.at[order, code, wide:],
                    core_send.at[order, code, 1], core_recv.at[order, code, 1], mate,
                ),
            )
            locals_[order, code] = (
                pltpu.make_async_copy(
                    packed.at[half + order, shard], held.at[order, code, :wide],
                    local_sem.at[order, code],
                ),
                pltpu.make_async_copy(
                    small.at[half + order, shard], held.at[order, code, wide:both],
                    small_sem.at[order, code],
                ),
                pltpu.make_async_copy(
                    packed_qkv.at[order, shard], held.at[order, code, both:],
                    qkv_sem.at[order, code],
                ),
            )
            for copy in locals_[order, code]:
                copy.start()
    sent = {}

    def partner(order, place):
        return (flip(page, ORDERS[order][place]), blk)

    for code in codes:
        for order in range(3):
            for copy in locals_[order, code]:
                copy.wait()
            for copy in first[order, code]:
                copy.wait_recv()
            held[order, code, :both] = held[order, code, :both] + from_core[order, code]
            if code >= 4:
                slot = code - 4
                sent[1, order, slot] = send(
                    held.at[order, code], got1.at[order, slot], send1.at[order, slot],
                    recv1.at[order, slot], partner(order, 0),
                )
    for slot in (2, 3, 0, 1):
        for order in range(3):
            sent[1, order, slot].wait_recv()
            held[order, slot] = held[order, slot] + got1[order, slot]
            if slot >= 2:
                sent[2, order, slot - 2] = send(
                    held.at[order, slot], got2.at[order, slot - 2], send2.at[order, slot - 2],
                    recv2.at[order, slot - 2], partner(order, 1),
                )
    for slot in (1, 0):
        for order in range(3):
            sent[2, order, slot].wait_recv()
            held[order, slot] = held[order, slot] + got2[order, slot]
            if slot == 1:
                sent[3, order] = send(
                    held.at[order, 1], got3.at[order], send3.at[order], recv3.at[order],
                    partner(order, 2),
                )
    for order in range(3):
        sent[3, order].wait_recv()
        held[order, 0] = held[order, 0] + got3[order]
        sent[4, order] = send(
            held.at[order, 0], got_side.at[order], side_send.at[order], side_recv.at[order], side
        )

    def write(part, order, which):
        rows = part[order].astype(jnp.float32)
        at = 0
        for piece in range(4):
            lanes = pl.ds(pl.multiple_of(which * 1536 + order * 512 + piece * LANES, LANES), LANES)
            up_ref[:, lanes] = rows[at : at + 96]
            at += 96
        lanes = pl.ds(pl.multiple_of(which * 384 + order * LANES, LANES), LANES)
        down_ref[:, lanes] = rows[at : at + 384]
        at += 384
        out_ref[:, lanes] = rows[at : at + 96]
        at += 96
        small_ref[pl.ds(which, 1), order] = rows[None, at : at + SMALL_ROWS]
        at += SMALL_ROWS
        for piece in range(3):
            lanes = pl.ds(pl.multiple_of(piece * 768 + which * 384 + order * LANES, LANES), LANES)
            qkv_ref[:, lanes] = rows[at : at + 96]
            at += 96

    for order in range(3):
        sent[4, order].wait_recv()
        total[order] = held[order, 0] + got_side[order]
        sent[5, order] = send(
            total.at[order], got_core.at[order], last_send.at[order], last_recv.at[order], mate
        )
        write(total, order, core)
    for order in range(3):
        sent[5, order].wait_recv()
        write(got_core, order, 1 - core)
    for copies in first.values():
        for copy in copies:
            copy.wait_send()
    for copy in sent.values():
        copy.wait_send()


def reduce_by_kernel(packed, packed_qkv, vectors):
    shards = lax.axis_size("page")
    small = jnp.concatenate([v.reshape(shards, -1) for v in vectors], axis=1).astype(low)
    width = small.shape[1]
    small = jnp.pad(small, ((0, 0), (0, 6 * SMALL_ROWS * LANES - width)))
    small = small.reshape(8, 6, SMALL_ROWS, LANES).transpose(1, 0, 2, 3)
    wide = packed.shape[2] + SMALL_ROWS
    rows = wide + packed_qkv.shape[2]
    struct = jax.ShapeDtypeStruct
    vmem, dma = pltpu.VMEM, pltpu.SemaphoreType.DMA
    up_s, down_s, out_s, qkv_s, small_s = pl.pallas_call(
        reduce_kernel,
        out_shape=(
            struct((96, 3072), f32),
            struct((384, 768), f32),
            struct((96, 768), f32),
            struct((96, 2304), f32),
            struct((2, 3, SMALL_ROWS, LANES), f32),
        ),
        in_specs=[any_spec()] * 3,
        out_specs=(vmem_spec(),) * 5,
        scratch_shapes=[
            vmem((3, 8, rows, LANES), low),
            vmem((3, 8, wide, LANES), low),
            vmem((3, 4, rows, LANES), low),
            vmem((3, 2, rows, LANES), low),
            vmem((3, rows, LANES), low),
            vmem((3, rows, LANES), low),
            vmem((3, rows, LANES), low),
            vmem((3, rows, LANES), low),
            dma((3, 8)), dma((3, 8)), dma((3, 8)), dma((3, 8, 2)), dma((3, 8, 2)),
            dma((3, 4)), dma((3, 4)),
            dma((3, 2)), dma((3, 2)),
            dma((3,)), dma((3,)),
            dma((3,)), dma((3,)),
            dma((3,)), dma((3,)),
        ],
        compiler_params=pltpu.CompilerParams(
            collective_id=3, has_side_effects=True, vmem_limit_bytes=56 * 2**20
        ),
        name="reduce_grads",
    )(packed, small, packed_qkv)
    flat = small_s.reshape(-1)
    sums, at = [], 0
    for vector in vectors:
        count = vector.shape[0] // shards
        sums.append(flat[at : at + count])
        at += count
    return (qkv_s, out_s, up_s, down_s), sums


def reduce_by_collectives(packed, packed_qkv, vectors):
    core = lax.axis_index("blk") % 2
    up = packed[:, :, :384].reshape(6, 8, 4, 96, LANES).transpose(1, 3, 0, 2, 4).reshape(768, 3072)
    down = packed[:, :, 384:768].transpose(1, 2, 0, 3).reshape(3072, 768)
    out = packed[:, :, 768:].transpose(1, 2, 0, 3).reshape(768, 768)
    own = packed_qkv.reshape(3, 8, 3, 96, LANES).transpose(1, 3, 2, 0, 4).reshape(768, 3, 384)
    qkv = jnp.zeros((768, 3, 2, 384), low)
    qkv = lax.dynamic_update_slice(qkv, own[:, :, None], (0, 0, core, 0)).reshape(768, 2304)
    grads = jax.tree.map(lambda g: g.astype(f32), (qkv, out, up, down, *vectors))
    page_sums = tuple(
        lax.psum_scatter(grad, "page", scatter_dimension=0, tiled=True) for grad in grads
    )
    sums = jax.tree.map(
        lambda part: part.astype(f32), lax.psum(jax.tree.map(lambda g: g.astype(low), page_sums), "blk")
    )
    return sums[:4], sums[4:]


def local(
    tokens, lengths, boxes, qkv_weight, qkv_bias, box_weight, out_weight, out_bias, norm1_gain,
    norm1_bias, up_weight, up_bias, down_weight, down_bias, norm2_gain, norm2_bias, cotangent,
):
    pages, block, width = tokens.shape
    rows = pages * block
    x, q, k, v, sc, probs, ctx = attend(tokens, boxes, lengths, qkv_weight, qkv_bias, box_weight)
    output, dresid1, dctx, packed, g_up_b, g_rows = feed(
        ctx.reshape(rows, width), tokens.reshape(rows, width), cotangent.reshape(rows, width),
        out_weight, up_weight, down_weight, out_bias, norm1_gain, norm1_bias, up_bias, down_bias,
        norm2_gain, norm2_bias,
    )
    input_grad, packed_qkv, g_bias, g_box = attend_back(
        dctx.reshape(pages, block, width), x, q, k, v, sc, probs, qkv_weight, box_weight,
        dresid1.reshape(pages, block, width),
    )
    core = lax.axis_index("blk") % 2
    own_bias = g_bias[:3].reshape(3, 1, width // 2)
    bias = lax.dynamic_update_slice(jnp.zeros((3, 2, width // 2), f32), own_bias, (0, core, 0))
    vectors = (
        bias.reshape(-1), g_box.reshape(-1), g_rows[5], g_rows[3], g_rows[4], g_up_b.reshape(-1),
        g_rows[2], g_rows[0], g_rows[1],
    )
    if lax.axis_size("page") == 8:
        weights, sums = reduce_by_kernel(packed, packed_qkv, vectors)
    else:
        weights, sums = reduce_by_collectives(packed, packed_qkv, vectors)
    qkv_w, out_w, up_w, down_w = weights
    qkv_b, box, out_b, gain1, shift1, up_b, down_b, gain2, shift2 = sums
    return (
        output.reshape(pages, block, width), input_grad, qkv_w, qkv_b, box, out_w, out_b, gain1,
        shift1, up_w, up_b, down_w, down_b, gain2, shift2,
    )


def solution(mesh):
    return jax.shard_map(
        local,
        mesh=mesh,
        in_specs=(
            P("page", "blk", None),
            P("page"),
            P("page", "blk", None),
            P(),
            P(),
            P(),
            P(),
            P(),
            P(),
            P(),
            P(),
            P(),
            P(),
            P(),
            P(),
            P(),
            P("page", "blk", None),
        ),
        out_specs=(
            P("page", "blk", None),
            P("page", "blk", None),
            P("page", None),
            P("page"),
            P("page"),
            P("page", None),
            P("page"),
            P("page"),
            P("page"),
            P("page", None),
            P("page"),
            P("page", None),
            P("page"),
            P("page"),
            P("page"),
        ),
        check_vma=False,
    )
```

profile of v0, /device:TPU:9, one launch (start us, length us, event | category | flops | bytes accessed | tf_op | source)
XLA Modules:
  0.0 256.3 jit_solution(13830033646376594199)
XLA Ops:
  0.6 0.7 convert_bitcast_fusion
  1.3 0.6 pad.10.boxes
  1.9 1.3 reshape.81.qkv_b
  3.3 1.4 fusion.2.box2
  4.7 0.0 copy-start.11
  4.7 0.0 copy-start.12
  4.7 0.0 copy-start.13
  4.7 32.4 %attend.1 = (bf16[3,4,128,768]{3,2,1,0:T(8,128)(2,1)}, bf16[3,3,256,128]{3,2,1,0:T(8,128)(2,1)}, bf16[3,3,512,128]{3,2,1,0:T(8,128)(2,1)}, bf16[3,3,512,128]{3,2...) custom-call(bf16[3,128,768]{2,1,0:T(8,128)(2,1)} %tokens.1, ...), custom_call_target="tpu_custom_call" | custom-call | tf_op jit(solution)/shard_map/attend/pallas_call | solution.py:277
  37.2 0.0 copy-done.8
  37.2 0.6 reshape.85.out_b
  37.8 0.0 copy-done.9
  37.8 0.6 reshape.86.gain1
  38.4 0.0 copy-done.10
  38.4 0.6 reshape.87.shift1
  39.0 0.0 copy-done.7
  39.0 0.6 reshape.88.up_b
  39.6 0.6 reshape.89.down_b
  40.1 0.6 reshape.90.gain2
  40.7 0.6 reshape.91.shift2
  41.3 30.6 %feed.1 = (bf16[384,768]{1,0:T(8,128)(2,1)}, f32[384,768]{1,0:T(8,128)}, bf16[384,768]{1,0:T(8,128)(2,1)}, bf16[6,8,864,128]{3,2,1,0:T(8,128)(2,1)}, f32[6,512]{1,0:T(8,128)}, /*index=5*/f32[8,768]{1,0:T(8,128)}) custom-call(bf16[384,768]{1,0:T(8,128)(2,1)} %bitcast.24, bf16[384,768]{1,0:T(8,128)(2,1)} %bitcast.18, bf16[384,768]{1,0:T(8,128)(2,1)} %bitcast.22, ...), custom_call_target="tpu_custom_call" | custom-call | tf_op jit(solution)/shard_map/feed/pallas_call | solution.py:436
  72.0 0.0 copy-start.5
  72.0 0.0 copy-start.6
  72.0 45.9 %attend_back.1 = (bf16[3,128,768]{2,1,0:T(8,128)(2,1)}, bf16[3,8,288,128]{3,2,1,0:T(8,128)(2,1)}, f32[8,384]{1,0:T(8,128)}, f32[64,128]{1,0:T(8,128)}) custom-call(bf16[3,128,768]{2,1,0:T(8,128)(2,1)} %bitcast.23, bf16[3,4,128,768]{3,2,1,0:T(8,128)(2,1)} %get-tuple-element.40.x_in, bf16[3,3,256,128]{3,2,1,0:T(8,128)(2,1)} %get-tuple-element.41.q_in, ...), custom_call_target="tpu_custom_call" | custom-call | tf_op jit(solution)/shard_map/attend_back/pallas_call | solution.py:651
  117.9 0.7 slice_bitcast_fusion
  118.7 0.1 reshape_reshape.12
  118.7 0.8 convert.33
  119.5 0.1 slice_reduce_fusion
  119.6 0.1 reshape_squeeze.24
  119.7 0.1 reshape_squeeze.25
  119.8 0.1 reshape_squeeze.26
  119.9 0.0 copy-done.6
  119.9 0.1 reshape_squeeze.27
  120.0 0.1 reshape_squeeze.28
  120.1 0.1 reshape_squeeze.29
  120.2 0.1 concatenate.16
  120.3 0.7 copy.38
  121.0 124.5 %reduce_grads.1 = (f32[96,3072]{1,0:T(8,128)}, f32[384,768]{1,0:T(8,128)}, f32[96,768]{1,0:T(8,128)}, f32[96,2304]{1,0:T(8,128)}, f32[2,3,16,128]{3,2,1,0:T(8,128)}) custom-call(bf16[6,8,864,128]{3,2,1,0:T(8,128)(2,1)} %get-tuple-element.48.packed, bf16[6,8,16,128]{3,2,1,0:T(8,128)(2,1)} %bitcast.21, bf16[3,8,288,128]{3,2,1,0:T(8,128)(2,1)} %get-tuple-element.53.packed_qkv), custom_call_target="tpu_custom_call" | custom-call | tf_op jit(solution)/shard_map/reduce_grads/pallas_call | solution.py:831
  245.5 1.3 slice.76
  246.9 1.4 slice.77
  248.2 1.4 fusion.3
  249.7 1.3 slice.81
  251.0 0.8 copy.45
  251.8 0.9 copy.46
  252.7 0.2 copy-done.4
  252.9 0.7 copy.47
  253.6 1.0 copy.48
  254.7 0.7 copy-done
  255.3 1.0 copy.49
  (25 shorter events, 0.2 us)
Async XLA Ops:
  4.7 32.5 %copy-start.8 = (f32[768]{0:T(1024)S(1)}, f32[768]{0:T(1024)}, u32[]{:S(2)}) copy-start(f32[768]{0:T(1024)} %param.25) | copy-start | bytes 9220
  4.7 33.1 %copy-start.9 = (f32[768]{0:T(1024)S(1)}, f32[768]{0:T(1024)}, u32[]{:S(2)}) copy-start(f32[768]{0:T(1024)} %param.26) | copy-start | bytes 9220
  4.7 33.7 %copy-start.10 = (f32[768]{0:T(1024)S(1)}, f32[768]{0:T(1024)}, u32[]{:S(2)}) copy-start(f32[768]{0:T(1024)} %param.27) | copy-start | bytes 9220
  4.7 34.3 %copy-start.7 = (f32[3072]{0:T(1024)S(1)}, f32[3072]{0:T(1024)}, u32[]{:S(2)}) copy-start(f32[3072]{0:T(1024)} %param.29) | copy-start | bytes 36868
  4.7 34.9 %copy-start.11 = (f32[768]{0:T(1024)S(1)}, f32[768]{0:T(1024)}, u32[]{:S(2)}) copy-start(f32[768]{0:T(1024)} %param.31) | copy-start | bytes 9220
  4.7 35.4 %copy-start.12 = (f32[768]{0:T(1024)S(1)}, f32[768]{0:T(1024)}, u32[]{:S(2)}) copy-start(f32[768]{0:T(1024)} %param.32) | copy-start | bytes 9220
  4.7 36.0 %copy-start.13 = (f32[768]{0:T(1024)S(1)}, f32[768]{0:T(1024)}, u32[]{:S(2)}) copy-start(f32[768]{0:T(1024)} %param.33) | copy-start | bytes 9220
  72.0 47.6 %copy-start.5 = (f32[8,768]{1,0:T(8,128)S(1)}, f32[8,768]{1,0:T(8,128)}, u32[]{:S(2)}) copy-start(f32[8,768]{1,0:T(8,128)} %get-tuple-element.51) | copy-start | bytes 73732
  72.0 47.9 %copy-start.6 = (f32[6,512]{1,0:T(8,128)S(1)}, f32[6,512]{1,0:T(8,128)}, u32[]{:S(2)}) copy-start(f32[6,512]{1,0:T(8,128)} %get-tuple-element.52) | copy-start | bytes 36868
  121.0 130.0 %copy-start.3 = (bf16[3,128,768]{2,1,0:T(8,128)(2,1)S(1)}, bf16[3,128,768]{2,1,0:T(8,128)(2,1)}, u32[]{:S(2)}) copy-start(bf16[3,128,768]{2,1,0:T(8,128)(2,1)} %get-tuple-element.87) | copy-start | bytes 1769476
  245.5 6.3 %copy-start.2 = (f32[96,2304]{1,0:T(8,128)S(1)}, f32[96,2304]{1,0:T(8,128)}, u32[]{:S(2)}) copy-start(f32[96,2304]{1,0:T(8,128)} %get-tuple-element.88) | copy-start | bytes 2654212
  251.8 1.1 copy-start.4
  251.8 1.8 copy-start.1
  253.6 1.7 copy-start
where the time goes:
time: 257 us; the launch traced here: 256 us
  Pallas kernels  233 us (91%)
  local copies, waits for them, and re-layouts  19.2 us (7%)
  other arithmetic  2.89 us (1%)
    pallas_call x1, Pallas kernels, reduce_by_kernel(): pl.pallas_call(reduce_kernel, out_shape=(struct((96, 3072), f32), struct(...  125 us
    pallas_call x1, Pallas kernels, attend_back(): pl.pallas_call(attend_back_kernel, out_shape=(struct((pages, block, width...  45.9 us
    pallas_call x1, Pallas kernels, attend(): pl.pallas_call(attend_kernel, out_shape=(struct((pages, 4, block, width),...  32.4 us
    pallas_call x1, Pallas kernels, feed(): pl.pallas_call(feed_kernel, out_shape=(struct((rows, width), low), struct...  30.6 us
    unnamed x35, local copies, waits for them, and re-layouts  5.46 us
    slice x4, local copies, waits for them, and re-layouts, reduce_by_kernel(): sums.append(flat[at:at + count])  5.43 us

commit v1 on v0

--- a/solution.py
+++ b/solution.py
@@ -9,22 +9,10 @@
 from jax.sharding import PartitionSpec as P
 
 norm_eps = 1e-12
-
 MESH = pl.DeviceIdType.MESH
 LANES = 128
-SMALL_ROWS = 16
 low = jnp.bfloat16
 f32 = jnp.float32
-ORDERS = ((0, 1, 2), (1, 2, 0), (2, 0, 1))
-
-
-def flip(page, way):
-    x, z = page % 2, page // 2
-    if way == 0:
-        return z * 2 + (1 - x)
-    if way == 1:
-        return (z + 1 - 2 * (z % 2)) * 2 + x
-    return (3 - z) * 2 + x
 
 
 def core_of(blk):
@@ -33,13 +21,6 @@
 
 def side_of(blk):
     return (blk + 2) % 4
-
-
-def shard_at(page, order, code):
-    for place, way in enumerate(ORDERS[order]):
-        if code >> (2 - place) & 1:
-            page = flip(page, way)
-    return page
 
 
 def greet(others):
@@ -328,7 +309,7 @@
 
 def feed_kernel(
     ctx, tokens, cotangent, out_w, up_w, down_w, out_b, gain1, shift1, up_b, down_b, gain2, shift2,
-    output, dresid1, dctx, packed, g_up_b, g_rows,
+    output, dresid1, dctx, packed, g_rows,
     w_out, w_up, w_down, act, slope, norm1, inverse1, hidden, hidden_t, grow, staged, w_sem, up_sem, down_sem, pack_sem,
 ):
     chunks, chunk = w_up.shape[0], w_up.shape[2]
@@ -351,6 +332,7 @@
     for j in range(chunks):
         up_load(j).start()
         down_load(j).start()
+    g_rows[...] = jnp.zeros_like(g_rows)
     out_load.wait()
     resid = tokens[...].astype(f32) + dot(ctx[...], w_out[...]) + out_b[...]
     normed, inverse = norm_of(resid)
@@ -387,7 +369,7 @@
     def _(j):
         dffn = staged[...]
         dupper = (dot_nt(dffn, w_down[j]) * slope[j]).astype(low)
-        g_up_b[pl.ds(j, 1)] = column_sum(dupper.astype(f32))
+        g_rows[pl.ds(8 + j, 1), :chunk] = column_sum(dupper.astype(f32))
         grow[...] += dot_nt(dupper, w_up[j])
         grad_up = dot(hidden_t[...], dupper).astype(low)
         for piece in range(up_pieces):
@@ -411,7 +393,6 @@
     dresid1[...] = back
     dattn = back.astype(low)
     g_rows[5:6] = column_sum(dattn.astype(f32))
-    g_rows[6:8] = jnp.zeros((2, width), f32)
     dctx[...] = dot_nt(dattn, w_out[...]).astype(low)
     grad_out = dot_tn(ctx[...], dattn).astype(low)
     first_row = packed.shape[2] - shard
@@ -440,11 +421,10 @@
             struct((rows, width), f32),
             struct((rows, width), low),
             struct((6, 8, packed_rows, LANES), low),
-            struct((chunks, chunk), f32),
-            struct((8, width), f32),
+            struct((16, width), f32),
         ),
         in_specs=[vmem_spec()] * 3 + [any_spec()] * 3 + [vmem_spec()] * 7,
-        out_specs=(vmem_spec(),) * 6,
+        out_specs=(vmem_spec(),) * 5,
         scratch_shapes=[
             vmem((width, width), low),
             vmem((chunks, width, chunk), low),
@@ -467,20 +447,273 @@
     )
 
 
+ORDERS = ("xaym", "ayxm", "yxam")
+GROUPS = ((12, 16), (8, 12), (6, 8), (4, 6), (2, 4), (1, 2))
+
+
+def flip(page, way):
+    x, z = page % 2, page // 2
+    if way == "x":
+        return z * 2 + (1 - x)
+    if way == "a":
+        return (z + 1 - 2 * (z % 2)) * 2 + x
+    return ((z + 2) % 4) * 2 + x
+
+
+class Ways:
+    def __init__(self):
+        self.page, self.blk = lax.axis_index("page"), lax.axis_index("blk")
+        self.core, self.half = self.blk % 2, self.blk // 2
+        self.mate, self.side = (self.page, core_of(self.blk)), (self.page, side_of(self.blk))
+
+    def partner(self, way):
+        return self.side if way == "y" else (flip(self.page, way), self.blk)
+
+    def piece(self, order, code):
+        page, half = self.page, self.half
+        for place, way in enumerate(ORDERS[order]):
+            if code >> (3 - place) & 1:
+                if way == "y":
+                    half = 1 - half
+                else:
+                    page = flip(page, way)
+        return page, half
+
+    def everyone(self):
+        return [self.partner(way) for way in "xamy"] + [self.mate]
+
+
+def step_of(code):
+    return 4 - code.bit_length()
+
+
+class EarlySum:
+    def __init__(self, ways, packed, held, mates, got, final, sems):
+        self.ways, self.packed, self.held, self.mates, self.got, self.final = ways, packed, held, mates, got, final
+        (self.own_sem, self.core_send, self.core_recv, self.send_sem, self.recv_sem, self.last_send,
+         self.last_recv, self.end_send, self.end_recv) = sems
+        self.rows = held.shape[2]
+
+    def slices(self):
+        return ((12, 16), (8, 12), (4, 8), (0, 4))
+
+    def start(self):
+        ways = self.ways
+        for at, (begin, end) in enumerate(self.slices()):
+            for code in range(begin, end):
+                for order in range(3):
+                    page, half = ways.piece(order, code)
+                    rows = pl.ds(pl.multiple_of(half * self.rows, 16), self.rows)
+                    remote(
+                        self.packed.at[3 - 3 * ways.core + order, page, rows],
+                        self.mates.at[order, code], self.core_send.at[order, at],
+                        self.core_recv.at[order, at], ways.mate,
+                    ).start()
+                    pltpu.make_async_copy(
+                        self.packed.at[3 * ways.core + order, page, rows], self.held.at[order, code],
+                        self.own_sem.at[order, at],
+                    ).start()
+
+    def core_group(self, order, at):
+        begin, end = self.slices()[at]
+        part = self.mates.at[order, begin:end]
+        return remote(part, part, self.core_send.at[order, at], self.core_recv.at[order, at], self.ways.mate)
+
+    def own_group(self, order, at):
+        begin, end = self.slices()[at]
+        part = self.held.at[order, begin:end]
+        return pltpu.make_async_copy(part, part, self.own_sem.at[order, at])
+
+    def add_core(self, at):
+        begin, end = self.slices()[at]
+        for order in range(3):
+            self.own_group(order, at).wait()
+            self.core_group(order, at).wait_recv()
+            self.held[order, begin:end] = self.held[order, begin:end] + self.mates[order, begin:end]
+
+    def copy(self, order, group):
+        begin, end = GROUPS[group]
+        way = ORDERS[order][step_of(begin)]
+        return remote(
+            self.held.at[order, begin:end], self.got.at[order, begin - 1 : end - 1],
+            self.send_sem.at[order, group], self.recv_sem.at[order, group], self.ways.partner(way),
+        )
+
+    def send(self, group):
+        for order in range(3):
+            self.copy(order, group).start()
+
+    def receive(self, group):
+        begin, end = GROUPS[group]
+        base = 1 << (begin.bit_length() - 1)
+        for order in range(3):
+            self.copy(order, group).wait_recv()
+            to = slice(begin - base, end - base)
+            self.held[order, to] = self.held[order, to] + self.got[order, begin - 1 : end - 1]
+
+    def last_copy(self, order):
+        part = self.final.at[self.ways.core, order, self.ways.half]
+        return remote(part, part, self.last_send.at[order], self.last_recv.at[order], self.ways.side)
+
+    def end_copy(self, order):
+        part = self.final.at[self.ways.core, order]
+        return remote(part, part, self.end_send.at[order], self.end_recv.at[order], self.ways.mate)
+
+    def share(self):
+        for order in range(3):
+            self.copy(order, 5).wait_recv()
+            self.final[self.ways.core, order, self.ways.half] = self.held[order, 0] + self.got[order, 0]
+            self.last_copy(order).start()
+
+    def hand_over(self):
+        for order in range(3):
+            self.last_copy(order).wait_recv()
+            self.end_copy(order).start()
+
+    def finish(self):
+        for order in range(3):
+            self.end_copy(order).wait()
+            self.last_copy(order).wait_send()
+            for at in range(4):
+                self.core_group(order, at).wait_send()
+            for group in range(len(GROUPS)):
+                self.copy(order, group).wait_send()
+
+
+class LateSum:
+    def __init__(self, ways, hp, packed, held, got, final, sems):
+        self.ways, self.hp = ways, hp
+        self.packed, self.held, self.got, self.final = packed, held, got, final
+        (self.first_send, self.first_recv, self.send_sem, self.recv_sem, self.last_send, self.last_recv,
+         self.end_send, self.end_recv) = sems
+        self.rows = held.shape[3]
+
+    def start(self):
+        ways, hp = self.ways, self.hp
+        for code in range(8, 16):
+            for order in range(3):
+                page, half = ways.piece(order, code)
+                rows = pl.ds(pl.multiple_of(half * self.rows, 16), self.rows)
+                remote(
+                    self.packed.at[hp, order, page, rows], self.got.at[hp, order, code - 1],
+                    self.first_send.at[hp, order], self.first_recv.at[hp, order],
+                    ways.partner(ORDERS[order][0]),
+                ).start()
+
+    def first(self, order):
+        part = self.got.at[self.hp, order, 7:15]
+        return remote(
+            part, part, self.first_send.at[self.hp, order], self.first_recv.at[self.hp, order],
+            self.ways.partner(ORDERS[order][0]),
+        )
+
+    def copy(self, order, step):
+        begin, end = 8 >> step, 16 >> step
+        return remote(
+            self.held.at[self.hp, order, begin:end], self.got.at[self.hp, order, begin - 1 : end - 1],
+            self.send_sem.at[self.hp, order, step - 1], self.recv_sem.at[self.hp, order, step - 1],
+            self.ways.partner(ORDERS[order][step]),
+        )
+
+    def advance(self, step):
+        ways, hp = self.ways, self.hp
+        for order in range(3):
+            if step == 0:
+                self.first(order).wait_recv()
+                for code in (4, 5, 6, 7, 0, 1, 2, 3):
+                    page, half = ways.piece(order, code)
+                    rows = pl.ds(pl.multiple_of(half * self.rows, 16), self.rows)
+                    self.held[hp, order, code] = self.packed[hp, order, page, rows] + self.got[hp, order, code + 7]
+                    if code == 7:
+                        self.copy(order, 1).start()
+            elif step < 3:
+                self.copy(order, step).wait_recv()
+                count = 8 >> step
+                self.held[hp, order, :count] = (
+                    self.held[hp, order, :count] + self.got[hp, order, count - 1 : 2 * count - 1]
+                )
+                self.copy(order, step + 1).start()
+            elif step == 3:
+                self.copy(order, 3).wait_recv()
+                self.final[ways.core, hp, order, ways.half] = self.held[hp, order, 0] + self.got[hp, order, 0]
+                self.last_copy(order).start()
+            else:
+                self.last_copy(order).wait_recv()
+                self.end_copy(order).start()
+
+    def last_copy(self, order):
+        part = self.final.at[self.ways.core, self.hp, order, self.ways.half]
+        return remote(
+            part, part, self.last_send.at[self.hp, order], self.last_recv.at[self.hp, order], self.ways.side
+        )
+
+    def end_copy(self, order):
+        part = self.final.at[self.ways.core, self.hp, order]
+        return remote(
+            part, part, self.end_send.at[self.hp, order], self.end_recv.at[self.hp, order], self.ways.mate
+        )
+
+    def finish(self):
+        for order in range(3):
+            self.end_copy(order).wait()
+            self.last_copy(order).wait_send()
+            self.first(order).wait_send()
+            for step in (1, 2, 3):
+                self.copy(order, step).wait_send()
+
+
+class SmallSum:
+    def __init__(self, ways, value, got, sems):
+        self.ways, self.value, self.got = ways, value, got
+        self.send_sem, self.recv_sem = sems
+        self.to = ways.everyone()
+
+    def copy(self, step):
+        return remote(
+            self.value.at[step], self.got.at[step], self.send_sem.at[step], self.recv_sem.at[step], self.to[step]
+        )
+
+    def start(self):
+        self.copy(0).start()
+
+    def advance(self, step):
+        self.copy(step).wait_recv()
+        self.value[step + 1] = self.value[step] + self.got[step]
+        if step < 4:
+            self.copy(step + 1).start()
+
+    def finish(self):
+        for step in range(5):
+            self.copy(step).wait_send()
+
+
 def attend_back_kernel(
-    dctx_own, x_in, q_in, k_in, v_in, sc_in, p_in, qkv_w, box_w, dresid1,
-    input_grad, packed, g_bias, g_box,
-    x, q, k, v, sc, probs, dctx, dq, dkv, x_t, w_c, dx, dx_mate, dx_side, box_t,
-    in_sem, p_sem, w_sem, own_sem, mate_send, mate_recv, core_send, core_recv, side_send, side_recv,
+    summed, dctx_own, x_in, q_in, k_in, v_in, sc_in, p_in, qkv_w, box_w, dresid1, *refs
 ):
-    page, blk = lax.axis_index("page"), lax.axis_index("blk")
-    core = blk % 2
-    mate, side = (page, core_of(blk)), (page, side_of(blk))
+    if summed:
+        (
+            early_in, small_in,
+            dx_out, early_out, late_out, small_out, tiny_out,
+            x, q, k, v, sc, probs, dctx, dq, dkv, x_t, w_c, dx, dx_mate, dx_side, box_t, g_box, g_bias, late_packed,
+            in_sem, p_sem, w_sem, own_sem, mate_send, mate_recv, core_send, core_recv, side_send, side_recv,
+            early_held, early_mates, early_got, late_held, late_got, small_value, small_got, tiny_value, tiny_got,
+            *sems,
+        ) = refs
+        early_sems, late_sems, small_sems, tiny_sems = sems[:9], sems[9:17], sems[17:19], sems[19:21]
+    else:
+        (
+            dx_out, late_packed, tiny_out,
+            x, q, k, v, sc, probs, dctx, dq, dkv, x_t, w_c, dx, dx_mate, dx_side, box_t, g_box, g_bias,
+            in_sem, p_sem, w_sem, own_sem, mate_send, mate_recv, core_send, core_recv, side_send, side_recv,
+        ) = refs
+    ways = Ways()
+    core, mate, side = ways.core, ways.mate, ways.side
     pages, pairs, chip, _ = q.shape
     keys = k.shape[2]
     block = chip // 2
     half = pairs * LANES
     width = x.shape[-1]
+    shard = width // 8
     head = LANES // 2
     scale = 0.125
 
@@ -513,91 +746,102 @@
             mate_recv.at[pg], mate,
         )
 
-    greet((mate, side))
+    greet(ways.everyone() if summed else [mate, side])
+    mate_copy(0).start()
+    own_copy(0).start()
+    for copy in loads(0):
+        copy.start()
+    p_load(0, 0).start()
+    if summed:
+        early = EarlySum(ways, early_in, early_held, early_mates, early_got, early_out, early_sems)
+        small = SmallSum(ways, small_value, small_got, small_sems)
+        tiny = SmallSum(ways, tiny_value, tiny_got, tiny_sems)
+
+        def late(hp):
+            return LateSum(ways, hp, late_packed, late_held, late_got, late_out, late_sems)
+
+        early.start()
+        small_value[0] = small_in[...]
+        small.start()
     for pg in range(pages):
-        mate_copy(pg).start()
-        own_copy(pg).start()
-        for copy in loads(pg):
-            copy.start()
-        p_load(0, pg).start()
+        if pg > 0:
+            mate_copy(pg).start()
+            own_copy(pg).start()
+            for copy in loads(pg):
+                copy.start()
+        for hp in range(pairs):
+            if pg + hp > 0:
+                p_load(hp, pg).start()
     for copy in w_loads:
         copy.start()
-    for hp in range(1, pairs):
-        for pg in range(pages):
-            p_load(hp, pg).start()
     for e in range(2):
         box_t[e] = jnp.zeros_like(box_t[e])
         box_t[e, :, e * head : (e + 1) * head] = box_w[...].astype(f32).T.astype(low)
     g_box[...] = jnp.zeros_like(g_box)
-    for pg in range(pages):
+
+    def take(pg):
         for copy in loads(pg):
             copy.wait()
-        x_t[:, pg * keys : (pg + 1) * keys] = x[pg].reshape(keys, width).T
+        at = pl.ds(pl.multiple_of(pg * keys, LANES), keys)
+        x_t[:, at] = x[pg].reshape(keys, width).T
         own_copy(pg).wait()
         mate_copy(pg).wait_recv()
 
-    @pl.loop(0, pairs)
-    def _(hp):
+    def one_pair(pg, hp):
         lanes = pl.ds(pl.multiple_of(hp * LANES, LANES), LANES)
-
-        @pl.loop(0, pages)
-        def _(pg):
-            p_load(hp, pg).wait()
-            both = sc[pg]
-            cosine2, sine2 = turned(both)
-            flat = both.T
-            sine_t, cosine_t = flat[:head, :chip], flat[head:, :chip]
-            basis = both.astype(low)
-            basis_t = flat.astype(low)
-            q_pair, k_pair, v_pair = q[pg, hp], k[pg, hp], v[pg, hp]
-            q_t, k_t = q_pair.T, k_pair.T
-            dc = dctx[pg, :, :, lanes].reshape(chip, LANES)
-            left = lane_halves((chip, LANES))
-            zero = jnp.zeros_like(dc)
-            dk, dv, dqs = 0.0, 0.0, []
-            for e in range(2):
-                mine = left if e == 0 else jnp.logical_not(left)
-                own_rows = slice(e * head, (e + 1) * head)
-                p = probs[pg, hp, e]
-                dc_own = jnp.where(mine, dc, zero)
-                q_own = jnp.where(mine, q_pair, zero)
-                dp = dot_nt(v_pair, dc_own)
-                p_wide = p.astype(f32)
-                delta = jnp.sum(p_wide * dp, axis=0, keepdims=True)
-                ds = (p_wide * (dp - delta)).astype(low)
-                dv = dv + dot(p, dc_own)
-                dk_feat = dot(ds, jnp.concatenate([q_own, basis[:chip]], 1)) * scale
-                dq_feat = dot(jnp.concatenate([k_t[own_rows], basis_t], 0), ds) * scale
-                dk_proj = rotate_key(dk_feat[:, LANES:], cosine2, sine2).astype(low)
-                a, b = dq_feat[head : 2 * head], dq_feat[2 * head :]
-                dq_proj = jnp.concatenate(
-                    [a * cosine_t - b * sine_t, a * sine_t + b * cosine_t], 0
-                ).astype(low)
-                dk = dk + dk_feat[:, :LANES] + dot(dk_proj, box_t[e])
-                dqs.append(dq_feat[:head] + dot(box_w[...], dq_proj))
-                g_box[...] += dot(k_t[own_rows], dk_proj) + dot_nt(q_t[own_rows], dq_proj)
-            at = pl.ds(pl.multiple_of(pg * keys, LANES), keys)
-            at_q = pl.ds(pl.multiple_of(pg * chip, LANES), chip)
-            dq[hp, at_q] = jnp.concatenate(dqs, 0).T.astype(low)
-            dkv[hp, at, :LANES] = dk.astype(low)
-            dkv[hp, at, LANES:] = dv.astype(low)
-
+        p_load(hp, pg).wait()
+        both = sc[pg]
+        cosine2, sine2 = turned(both)
+        flat = both.T
+        sine_t, cosine_t = flat[:head, :chip], flat[head:, :chip]
+        basis = both.astype(low)
+        basis_t = flat.astype(low)
+        q_pair, k_pair, v_pair = q[pg, hp], k[pg, hp], v[pg, hp]
+        q_t, k_t = q_pair.T, k_pair.T
+        dc = dctx[pg, :, :, lanes].reshape(chip, LANES)
+        left = lane_halves((chip, LANES))
+        zero = jnp.zeros_like(dc)
+        dk, dv, dqs = 0.0, 0.0, []
+        for e in range(2):
+            mine = left if e == 0 else jnp.logical_not(left)
+            own_rows = slice(e * head, (e + 1) * head)
+            p = probs[pg, hp, e]
+            dc_own = jnp.where(mine, dc, zero)
+            q_own = jnp.where(mine, q_pair, zero)
+            dp = dot_nt(v_pair, dc_own)
+            p_wide = p.astype(f32)
+            delta = jnp.sum(p_wide * dp, axis=0, keepdims=True)
+            ds = (p_wide * (dp - delta)).astype(low)
+            dv = dv + dot(p, dc_own)
+            dk_feat = dot(ds, jnp.concatenate([q_own, basis[:chip]], 1)) * scale
+            dq_feat = dot(jnp.concatenate([k_t[own_rows], basis_t], 0), ds) * scale
+            dk_proj = rotate_key(dk_feat[:, LANES:], cosine2, sine2).astype(low)
+            a, b = dq_feat[head : 2 * head], dq_feat[2 * head :]
+            dq_proj = jnp.concatenate(
+                [a * cosine_t - b * sine_t, a * sine_t + b * cosine_t], 0
+            ).astype(low)
+            dk = dk + dk_feat[:, :LANES] + dot(dk_proj, box_t[e])
+            dqs.append(dq_feat[:head] + dot(box_w[...], dq_proj))
+            g_box[...] += dot(k_t[own_rows], dk_proj) + dot_nt(q_t[own_rows], dq_proj)
+        at = pl.ds(pl.multiple_of(pg * keys, LANES), keys)
+        at_q = pl.ds(pl.multiple_of(pg * chip, LANES), chip)
+        dq[hp, at_q] = jnp.concatenate(dqs, 0).T.astype(low)
+        dkv[hp, at, :LANES] = dk.astype(low)
+        dkv[hp, at, LANES:] = dv.astype(low)
+
+    def pair_grads(hp):
         dkv_all = dkv[hp]
         dq_all = dq[hp]
         g_kv = column_sum(dkv_all.astype(f32))
-        g_bias[0:1, lanes] = column_sum(dq_all.astype(f32))
-        g_bias[1:2, lanes] = g_kv[:, :LANES]
-        g_bias[2:3, lanes] = g_kv[:, LANES:]
+        g_bias[pl.ds(hp, 1)] = column_sum(dq_all.astype(f32))
+        g_bias[pl.ds(hp + pairs, 1)] = g_kv[:, :LANES]
+        g_bias[pl.ds(hp + 2 * pairs, 1)] = g_kv[:, LANES:]
         grad = dot(x_t[...], dkv_all).astype(low)
         x_q = jnp.concatenate([x_t[:, pg * keys : pg * keys + chip] for pg in range(pages)], 1)
         grad_q = dot(x_q, dq_all).astype(low)
-        shard = width // 8
-        packed[hp, :, :shard] = grad_q.reshape(8, shard, LANES)
-        packed[hp, :, shard : 2 * shard] = grad[:, :LANES].reshape(8, shard, LANES)
-        packed[hp, :, 2 * shard :] = grad[:, LANES:].reshape(8, shard, LANES)
-
-    for copy in w_loads:
-        copy.wait()
+        late_packed[hp, 0] = grad_q.reshape(8, shard, LANES)
+        late_packed[hp, 1] = grad[:, :LANES].reshape(8, shard, LANES)
+        late_packed[hp, 2] = grad[:, LANES:].reshape(8, shard, LANES)
 
     def core_copy(pg, at):
         return remote(
@@ -608,8 +852,7 @@
     def side_copy(pg):
         return remote(dx.at[pg, 1, core], dx_side.at[pg], side_send.at[pg], side_recv.at[pg], side)
 
-    @pl.loop(0, pages)
-    def _(pg):
+    def input_part(pg):
         for at in (1, 0):
             rows = pl.ds(pl.multiple_of(pg * keys + at * chip, LANES), chip)
             dks = jnp.concatenate([dkv[hp, rows, :LANES] for hp in range(pairs)], 1)
@@ -622,251 +865,288 @@
             dx[pg, at] = total.astype(low).reshape(2, block, width)
             core_copy(pg, at).start()
 
-    @pl.loop(0, pages)
-    def _(pg):
+    def pass_input(pg):
         core_copy(pg, 1).wait_recv()
         dx[pg, 1, core] = dx[pg, 1, core] + dx_mate[pg, 1]
         side_copy(pg).start()
 
-    @pl.loop(0, pages)
+    def early_step(at):
+        if not summed:
+            return
+        if at == 0:
+            early.add_core(0)
+            early.send(0)
+        elif at == 1:
+            early.add_core(1)
+            early.send(1)
+            early.add_core(2)
+            early.add_core(3)
+            small.advance(0)
+        elif at == 2:
+            early.receive(0)
+            early.send(2)
+            early.send(3)
+            small.advance(1)
+        elif at == 3:
+            early.receive(1)
+            small.advance(2)
+        elif at == 4:
+            early.receive(2)
+            early.send(4)
+            small.advance(3)
+        elif at == 5:
+            early.receive(3)
+            small.advance(4)
+        elif at == 6:
+            early.receive(4)
+            early.send(5)
+        elif at == 7:
+            early.share()
+        elif at == 8:
+            early.hand_over()
+
+    def bias_rows():
+        for part in range(3):
+            for which in range(2):
+                own = jnp.where(core == which, 1.0, 0.0)
+                for hp in range(pairs):
+                    at = part * pairs + hp
+                    yield 64 + (2 * part + which) * pairs + hp, g_bias[at : at + 1] * own
+
+    for copy in w_loads:
+        copy.wait()
+
+    @pl.loop(0, pages - 1)
     def _(pg):
+        take(pg)
+
+        @pl.when(pg > 0)
+        def _():
+            pass_input(pg - 1)
+
+        @pl.loop(0, pairs)
+        def _(hp):
+            for at in range(pairs * (pages - 1)):
+
+                @pl.when(pg * pairs + hp == at)
+                def _(at=at):
+                    early_step(at)
+
+            one_pair(pg, hp)
+
+        input_part(pg)
+
+    last = pages - 1
+    take(last)
+    pass_input(last - 1)
+
+    @pl.loop(0, pairs)
+    def _(hp):
+        for at in range(pairs):
+
+            @pl.when(hp == at)
+            def _(at=at):
+                early_step(pairs * last + at)
+
+        one_pair(last, hp)
+        pair_grads(hp)
+        if summed:
+            late(hp).start()
+
+            @pl.when(hp > 0)
+            def _():
+                late(hp - 1).advance(0)
+
+            @pl.when(hp == 2)
+            def _():
+                late(0).advance(1)
+
+    if summed:
+        tiny_value[0, : 8 * 8] = g_box[...]
+        tiny_value[0, 64:] = jnp.zeros((24, LANES), f32)
+        for at, row in bias_rows():
+            tiny_value[0, at : at + 1] = row
+        tiny.start()
+    input_part(last)
+    if summed:
+        tiny.advance(0)
+        late(2).advance(0)
+        late(1).advance(1)
+        late(0).advance(2)
+        pass_input(last)
+        tiny.advance(1)
+        late(2).advance(1)
+        late(1).advance(2)
+        late(0).advance(3)
+        tiny.advance(2)
+        late(2).advance(2)
+        late(1).advance(3)
+        late(0).advance(4)
+        tiny.advance(3)
+        late(2).advance(3)
+        late(1).advance(4)
+        tiny.advance(4)
+        late(2).advance(4)
+    else:
+        pass_input(last)
+
+    for pg in range(pages):
         core_copy(pg, 0).wait_recv()
         side_copy(pg).wait_recv()
         total = dx[pg, 0, core].astype(f32) + dx_mate[pg, 0].astype(f32) + dx_side[pg].astype(f32)
-        input_grad[pg] = (total + dresid1[pg]).astype(low)
+        dx_out[pg] = (total + dresid1[pg]).astype(low)
         for at in range(2):
             core_copy(pg, at).wait_send()
         side_copy(pg).wait_send()
         mate_copy(pg).wait_send()
-
-
-def attend_back(dctx, x, q, k, v, sc, probs, qkv_w, box_w, dresid1):
+    if summed:
+        small_out[...] = small_value[5]
+        tiny_out[...] = tiny_value[5]
+        early.finish()
+        for hp in range(pairs):
+            late(hp).finish()
+        small.finish()
+        tiny.finish()
+    else:
+        tiny_out[:64] = g_box[...]
+        tiny_out[64:] = jnp.zeros((24, LANES), f32)
+        for at, row in bias_rows():
+            tiny_out[at : at + 1] = row
+
+
+def attend_back(dctx, x, q, k, v, sc, probs, qkv_w, box_w, dresid1, packed, small, summed):
     pages, pairs, chip, _ = q.shape
     keys = k.shape[2]
     width = x.shape[-1]
     block = chip // 2
     half = pairs * LANES
+    shard = width // 8
+    wide = packed.shape[2] // 2
     struct = jax.ShapeDtypeStruct
     vmem, dma = pltpu.VMEM, pltpu.SemaphoreType.DMA
+    late_packed = (pairs, 3, 8, shard, LANES)
+    tiny_rows = 88
+    scratch = [
+        vmem((pages, 4, block, width), low),
+        vmem((pages, pairs, chip, LANES), low),
+        vmem((pages, pairs, keys, LANES), low),
+        vmem((pages, pairs, keys, LANES), low),
+        vmem((pages, keys, LANES), f32),
+        vmem((pages, pairs, 2, keys, chip), low),
+        vmem((pages, 2, block, half), low),
+        vmem((pairs, pages * chip, LANES), low),
+        vmem((pairs, pages * keys, 2 * LANES), low),
+        vmem((width, pages * keys), low),
+        vmem((3, width, half), low),
+        vmem((pages, 2, 2, block, width), low),
+        vmem((pages, 2, block, width), low),
+        vmem((pages, block, width), low),
+        vmem((2, LANES, LANES), low),
+        vmem(box_w.shape, f32),
+        vmem((3 * pairs, LANES), f32),
+    ]
+    copies = [
+        dma((pages, 5)), dma((pages, pairs)), dma((3,)), dma((pages,)), dma((pages,)), dma((pages,)),
+        dma((pages, 2)), dma((pages, 2)), dma((pages,)), dma((pages,)),
+    ]
+    operands = [dctx, x, q, k, v, sc, probs, qkv_w, box_w, dresid1]
+    in_specs = [any_spec()] * 8 + [vmem_spec()] * 2
+    if summed:
+        operands += [packed, small]
+        in_specs += [any_spec(), vmem_spec()]
+        outs = (
+            struct((pages, block, width), low),
+            struct((2, 3, 2, wide, LANES), low),
+            struct((2, pairs, 3, 2, shard // 2, LANES), low),
+            struct(small.shape, f32),
+            struct((tiny_rows, LANES), f32),
+        )
+        scratch += [vmem(late_packed, low)] + copies
+        scratch += [
+            vmem((3, 16, wide, LANES), low),
+            vmem((3, 16, wide, LANES), low),
+            vmem((3, 15, wide, LANES), low),
+            vmem((pairs, 3, 8, shard // 2, LANES), low),
+            vmem((pairs, 3, 15, shard // 2, LANES), low),
+            vmem((6,) + small.shape, f32),
+            vmem((5,) + small.shape, f32),
+            vmem((6, tiny_rows, LANES), f32),
+            vmem((5, tiny_rows, LANES), f32),
+        ]
+        groups = len(GROUPS)
+        scratch += [dma((3, 4))] * 3 + [dma((3, groups))] * 2 + [dma((3,))] * 4
+        scratch += [dma((pairs, 3))] * 2 + [dma((pairs, 3, 3))] * 2 + [dma((pairs, 3))] * 4
+        scratch += [dma((5,))] * 4
+    else:
+        outs = (
+            struct((pages, block, width), low),
+            struct(late_packed, low),
+            struct((tiny_rows, LANES), f32),
+        )
+        scratch += copies
     return pl.pallas_call(
-        attend_back_kernel,
-        out_shape=(
-            struct((pages, block, width), low),
-            struct((pairs, 8, 3 * width // 8, LANES), low),
-            struct((8, half), f32),
-            struct(box_w.shape, f32),
-        ),
-        in_specs=[any_spec()] * 8 + [vmem_spec()] * 2,
-        out_specs=(vmem_spec(),) * 4,
-        scratch_shapes=[
-            vmem((pages, 4, block, width), low),
-            vmem((pages, pairs, chip, LANES), low),
-            vmem((pages, pairs, keys, LANES), low),
-            vmem((pages, pairs, keys, LANES), low),
-            vmem((pages, keys, LANES), f32),
-            vmem((pages, pairs, 2, keys, chip), low),
-            vmem((pages, 2, block, half), low),
-            vmem((pairs, pages * chip, LANES), low),
-            vmem((pairs, pages * keys, 2 * LANES), low),
-            vmem((width, pages * keys), low),
-            vmem((3, width, half), low),
-            vmem((pages, 2, 2, block, width), low),
-            vmem((pages, 2, block, width), low),
-            vmem((pages, block, width), low),
-            vmem((2, LANES, LANES), low),
-            dma((pages, 5)), dma((pages, pairs)), dma((3,)), dma((pages,)), dma((pages,)), dma((pages,)),
-            dma((pages, 2)), dma((pages, 2)), dma((pages,)), dma((pages,)),
-        ],
+        functools.partial(attend_back_kernel, summed),
+        out_shape=outs,
+        in_specs=in_specs,
+        out_specs=(vmem_spec(),) * len(outs),
+        scratch_shapes=scratch,
         compiler_params=pltpu.CompilerParams(
-            collective_id=2, has_side_effects=True, vmem_limit_bytes=60 * 2**20
+            collective_id=2, has_side_effects=True, vmem_limit_bytes=63 * 2**20
         ),
         name="attend_back",
-    )(dctx, x, q, k, v, sc, probs, qkv_w, box_w, dresid1)
-
-
-def reduce_kernel(
-    packed, small, packed_qkv, up_ref, down_ref, out_ref, qkv_ref, small_ref,
-    held, from_core, got1, got2, got3, got_side, total, got_core,
-    local_sem, small_sem, qkv_sem, core_send, core_recv, send1, recv1, send2, recv2, send3, recv3,
-    side_send, side_recv, last_send, last_recv,
+    )(*operands)
+
+
+def finish_kernel(
+    early, late, small, tiny, dx, up, down, out, qkv, qkv_b, box, out_b, gain1, shift1, up_b, down_b, gain2, shift2, input_grad
 ):
-    page, blk = lax.axis_index("page"), lax.axis_index("blk")
-    core = blk % 2
-    mate = (page, core_of(blk))
-    side = (page, side_of(blk))
-    greet([(flip(page, way), blk) for way in range(3)] + [mate, side])
-    wide = packed.shape[2]
-    both = wide + SMALL_ROWS
-    half = 3 * core
-
-    def send(src, dst, sems, recv, to):
-        copy = pltpu.make_async_remote_copy(
-            src_ref=src, dst_ref=dst, send_sem=sems, recv_sem=recv, device_id=to,
-            device_id_type=MESH,
-        )
-        copy.start()
-        return copy
-
-    codes = (6, 7, 4, 5, 2, 3, 0, 1)
-    first, locals_ = {}, {}
-    for code in codes:
+    page = lax.axis_index("page")
+    shard = out.shape[0]
+    pieces = up.shape[1] // (6 * LANES)
+    for which in range(2):
         for order in range(3):
-            shard = shard_at(page, order, code)
-            other = 3 - half + order
-            first[order, code] = (
-                send(
-                    packed.at[other, shard], from_core.at[order, code, :wide],
-                    core_send.at[order, code, 0], core_recv.at[order, code, 0], mate,
-                ),
-                send(
-                    small.at[other, shard], from_core.at[order, code, wide:],
-                    core_send.at[order, code, 1], core_recv.at[order, code, 1], mate,
-                ),
-            )
-            locals_[order, code] = (
-                pltpu.make_async_copy(
-                    packed.at[half + order, shard], held.at[order, code, :wide],
-                    local_sem.at[order, code],
-                ),
-                pltpu.make_async_copy(
-                    small.at[half + order, shard], held.at[order, code, wide:both],
-                    small_sem.at[order, code],
-                ),
-                pltpu.make_async_copy(
-                    packed_qkv.at[order, shard], held.at[order, code, both:],
-                    qkv_sem.at[order, code],
-                ),
-            )
-            for copy in locals_[order, code]:
-                copy.start()
-    sent = {}
-
-    def partner(order, place):
-        return (flip(page, ORDERS[order][place]), blk)
-
-    for code in codes:
-        for order in range(3):
-            for copy in locals_[order, code]:
-                copy.wait()
-            for copy in first[order, code]:
-                copy.wait_recv()
-            held[order, code, :both] = held[order, code, :both] + from_core[order, code]
-            if code >= 4:
-                slot = code - 4
-                sent[1, order, slot] = send(
-                    held.at[order, code], got1.at[order, slot], send1.at[order, slot],
-                    recv1.at[order, slot], partner(order, 0),
-                )
-    for slot in (2, 3, 0, 1):
-        for order in range(3):
-            sent[1, order, slot].wait_recv()
-            held[order, slot] = held[order, slot] + got1[order, slot]
-            if slot >= 2:
-                sent[2, order, slot - 2] = send(
-                    held.at[order, slot], got2.at[order, slot - 2], send2.at[order, slot - 2],
-                    recv2.at[order, slot - 2], partner(order, 1),
-                )
-    for slot in (1, 0):
-        for order in range(3):
-            sent[2, order, slot].wait_recv()
-            held[order, slot] = held[order, slot] + got2[order, slot]
-            if slot == 1:
-                sent[3, order] = send(
-                    held.at[order, 1], got3.at[order], send3.at[order], recv3.at[order],
-                    partner(order, 2),
-                )
-    for order in range(3):
-        sent[3, order].wait_recv()
-        held[order, 0] = held[order, 0] + got3[order]
-        sent[4, order] = send(
-            held.at[order, 0], got_side.at[order], side_send.at[order], side_recv.at[order], side
-        )
-
-    def write(part, order, which):
-        rows = part[order].astype(jnp.float32)
-        at = 0
-        for piece in range(4):
-            lanes = pl.ds(pl.multiple_of(which * 1536 + order * 512 + piece * LANES, LANES), LANES)
-            up_ref[:, lanes] = rows[at : at + 96]
-            at += 96
-        lanes = pl.ds(pl.multiple_of(which * 384 + order * LANES, LANES), LANES)
-        down_ref[:, lanes] = rows[at : at + 384]
-        at += 384
-        out_ref[:, lanes] = rows[at : at + 96]
-        at += 96
-        small_ref[pl.ds(which, 1), order] = rows[None, at : at + SMALL_ROWS]
-        at += SMALL_ROWS
-        for piece in range(3):
-            lanes = pl.ds(pl.multiple_of(piece * 768 + which * 384 + order * LANES, LANES), LANES)
-            qkv_ref[:, lanes] = rows[at : at + 96]
-            at += 96
-
-    for order in range(3):
-        sent[4, order].wait_recv()
-        total[order] = held[order, 0] + got_side[order]
-        sent[5, order] = send(
-            total.at[order], got_core.at[order], last_send.at[order], last_recv.at[order], mate
-        )
-        write(total, order, core)
-    for order in range(3):
-        sent[5, order].wait_recv()
-        write(got_core, order, 1 - core)
-    for copies in first.values():
-        for copy in copies:
-            copy.wait_send()
-    for copy in sent.values():
-        copy.wait_send()
-
-
-def reduce_by_kernel(packed, packed_qkv, vectors):
-    shards = lax.axis_size("page")
-    small = jnp.concatenate([v.reshape(shards, -1) for v in vectors], axis=1).astype(low)
-    width = small.shape[1]
-    small = jnp.pad(small, ((0, 0), (0, 6 * SMALL_ROWS * LANES - width)))
-    small = small.reshape(8, 6, SMALL_ROWS, LANES).transpose(1, 0, 2, 3)
-    wide = packed.shape[2] + SMALL_ROWS
-    rows = wide + packed_qkv.shape[2]
+            column = which * 3 + order
+            rows = early[which, order].astype(f32).reshape(-1, LANES)
+            for piece in range(pieces):
+                at = (column * pieces + piece) * LANES
+                up[:, at : at + LANES] = rows[piece * shard : (piece + 1) * shard]
+            at = column * LANES
+            first = pieces * shard
+            down[:, at : at + LANES] = rows[first : first + down.shape[0]]
+            out[:, at : at + LANES] = rows[first + down.shape[0] :]
+            for part in range(3):
+                at = (part * 6 + column) * LANES
+                qkv[:, at : at + LANES] = late[which, order, part].astype(f32).reshape(shard, LANES)
+    rows = pltpu.roll(small[:8], lax.rem(8 * shard - page * shard, 8 * shard), 1)
+    for at, ref in enumerate((gain2, shift2, down_b, gain1, shift1, out_b)):
+        ref[...] = rows[at, :shard]
+    flat = jnp.concatenate([small[8 + at : 9 + at, : pieces * LANES] for at in range(6)], 1)
+    every = flat.shape[1]
+    flat = pltpu.roll(flat, lax.rem(every - page * up_b.shape[0], every), 1)
+    up_b[...] = flat[0, : up_b.shape[0]]
+    box[...] = tiny[pl.ds(pl.multiple_of(page * 8, 8), 8)]
+    count = qkv_b.shape[0]
+    first = page * count
+    parts = [tiny[pl.ds(64 + first // LANES + piece, 1)] for piece in range(4)]
+    rest = lax.rem(first, LANES)
+    row = pltpu.roll(jnp.concatenate(parts, 1), lax.rem(4 * LANES - rest, 4 * LANES), 1)
+    qkv_b[...] = row[0, :count]
+    input_grad[...] = dx[...]
+
+
+def finish(early, late, small, tiny, dx):
     struct = jax.ShapeDtypeStruct
-    vmem, dma = pltpu.VMEM, pltpu.SemaphoreType.DMA
-    up_s, down_s, out_s, qkv_s, small_s = pl.pallas_call(
-        reduce_kernel,
-        out_shape=(
-            struct((96, 3072), f32),
-            struct((384, 768), f32),
-            struct((96, 768), f32),
-            struct((96, 2304), f32),
-            struct((2, 3, SMALL_ROWS, LANES), f32),
-        ),
-        in_specs=[any_spec()] * 3,
-        out_specs=(vmem_spec(),) * 5,
-        scratch_shapes=[
-            vmem((3, 8, rows, LANES), low),
-            vmem((3, 8, wide, LANES), low),
-            vmem((3, 4, rows, LANES), low),
-            vmem((3, 2, rows, LANES), low),
-            vmem((3, rows, LANES), low),
-            vmem((3, rows, LANES), low),
-            vmem((3, rows, LANES), low),
-            vmem((3, rows, LANES), low),
-            dma((3, 8)), dma((3, 8)), dma((3, 8)), dma((3, 8, 2)), dma((3, 8, 2)),
-            dma((3, 4)), dma((3, 4)),
-            dma((3, 2)), dma((3, 2)),
-            dma((3,)), dma((3,)),
-            dma((3,)), dma((3,)),
-            dma((3,)), dma((3,)),
-        ],
-        compiler_params=pltpu.CompilerParams(
-            collective_id=3, has_side_effects=True, vmem_limit_bytes=56 * 2**20
-        ),
-        name="reduce_grads",
-    )(packed, small, packed_qkv)
-    flat = small_s.reshape(-1)
-    sums, at = [], 0
-    for vector in vectors:
-        count = vector.shape[0] // shards
-        sums.append(flat[at : at + count])
-        at += count
-    return (qkv_s, out_s, up_s, down_s), sums
+    shapes = (
+        (96, 3072), (384, 768), (96, 768), (96, 2304), (288,), (8, LANES), (96,), (96,), (96,), (384,), (96,), (96,), (96,),
+    )
+    return pl.pallas_call(
+        finish_kernel,
+        out_shape=tuple(struct(shape, f32) for shape in shapes) + (struct(dx.shape, low),),
+        in_specs=[vmem_spec()] * 5,
+        out_specs=(vmem_spec(),) * 14,
+        compiler_params=pltpu.CompilerParams(vmem_limit_bytes=40 * 2**20),
+        name="finish",
+    )(early, late, small, tiny, dx)
 
 
 def reduce_by_collectives(packed, packed_qkv, vectors):
@@ -874,17 +1154,16 @@
     up = packed[:, :, :384].reshape(6, 8, 4, 96, LANES).transpose(1, 3, 0, 2, 4).reshape(768, 3072)
     down = packed[:, :, 384:768].transpose(1, 2, 0, 3).reshape(3072, 768)
     out = packed[:, :, 768:].transpose(1, 2, 0, 3).reshape(768, 768)
-    own = packed_qkv.reshape(3, 8, 3, 96, LANES).transpose(1, 3, 2, 0, 4).reshape(768, 3, 384)
+    own = packed_qkv.transpose(2, 3, 1, 0, 4).reshape(768, 3, 384)
     qkv = jnp.zeros((768, 3, 2, 384), low)
     qkv = lax.dynamic_update_slice(qkv, own[:, :, None], (0, 0, core, 0)).reshape(768, 2304)
     grads = jax.tree.map(lambda g: g.astype(f32), (qkv, out, up, down, *vectors))
     page_sums = tuple(
         lax.psum_scatter(grad, "page", scatter_dimension=0, tiled=True) for grad in grads
     )
-    sums = jax.tree.map(
+    return jax.tree.map(
         lambda part: part.astype(f32), lax.psum(jax.tree.map(lambda g: g.astype(low), page_sums), "blk")
     )
-    return sums[:4], sums[4:]
 
 
 def local(
@@ -894,31 +1173,34 @@
     pages, block, width = tokens.shape
     rows = pages * block
     x, q, k, v, sc, probs, ctx = attend(tokens, boxes, lengths, qkv_weight, qkv_bias, box_weight)
-    output, dresid1, dctx, packed, g_up_b, g_rows = feed(
+    output, dresid1, dctx, packed, small = feed(
         ctx.reshape(rows, width), tokens.reshape(rows, width), cotangent.reshape(rows, width),
         out_weight, up_weight, down_weight, out_bias, norm1_gain, norm1_bias, up_bias, down_bias,
         norm2_gain, norm2_bias,
     )
-    input_grad, packed_qkv, g_bias, g_box = attend_back(
+    summed = lax.axis_size("page") == 8
+    parts = attend_back(
         dctx.reshape(pages, block, width), x, q, k, v, sc, probs, qkv_weight, box_weight,
-        dresid1.reshape(pages, block, width),
+        dresid1.reshape(pages, block, width), packed, small, summed,
     )
-    core = lax.axis_index("blk") % 2
-    own_bias = g_bias[:3].reshape(3, 1, width // 2)
-    bias = lax.dynamic_update_slice(jnp.zeros((3, 2, width // 2), f32), own_bias, (0, core, 0))
-    vectors = (
-        bias.reshape(-1), g_box.reshape(-1), g_rows[5], g_rows[3], g_rows[4], g_up_b.reshape(-1),
-        g_rows[2], g_rows[0], g_rows[1],
-    )
-    if lax.axis_size("page") == 8:
-        weights, sums = reduce_by_kernel(packed, packed_qkv, vectors)
+    output = output.reshape(pages, block, width)
+    if summed:
+        dx, early, late, small, tiny = parts
+        (
+            up_w, down_w, out_w, qkv_w, qkv_b, box, out_b, gain1, shift1, up_b, down_b, gain2, shift2, input_grad,
+        ) = finish(early, late, small, tiny, dx)
+        box = box.reshape(-1)
     else:
-        weights, sums = reduce_by_collectives(packed, packed_qkv, vectors)
-    qkv_w, out_w, up_w, down_w = weights
-    qkv_b, box, out_b, gain1, shift1, up_b, down_b, gain2, shift2 = sums
+        input_grad, packed_qkv, tiny = parts
+        vectors = (
+            tiny[64:82].reshape(-1), tiny[:64].reshape(-1), small[5], small[3], small[4],
+            small[8:14, :512].reshape(-1), small[2], small[0], small[1],
+        )
+        (
+            qkv_w, out_w, up_w, down_w, qkv_b, box, out_b, gain1, shift1, up_b, down_b, gain2, shift2,
+        ) = reduce_by_collectives(packed, packed_qkv, vectors)
     return (
-        output.reshape(pages, block, width), input_grad, qkv_w, qkv_b, box, out_w, out_b, gain1,
-        shift1, up_w, up_b, down_w, down_b, gain2, shift2,
+        output, input_grad, qkv_w, qkv_b, box, out_w, out_b, gain1, shift1, up_w, up_b, down_w, down_b, gain2, shift2,
     )
 
 

time: 257 us -> 187 us (0.73)
  Pallas kernels: 233 us -> 167 us
  local copies, waits for them, and re-layouts: 19.2 us -> 15.8 us
    pallas_call x2, Pallas kernels: 170 us -> 104 us  [the longest x1 102 us: attend_back(): pl.pallas_call(functools.partial(attend_back_kernel, summed), out_shape=o...]
    slice x5 -> x0, local copies, waits for them, and re-layouts: 5.5 us -> none  [the longest x4 5.43 us: reduce_by_kernel(): sums.append(flat[at:at + count])]
    reshape x6, local copies, waits for them, and re-layouts: 3.48 us -> 7.63 us  [row(): return vector.reshape(1, -1)]
    unnamed x35 -> x10, local copies, waits for them, and re-layouts: 5.46 us -> 4.98 us
where the time goes in v1:
time: 187 us; the launch traced here: 186 us
  Pallas kernels  167 us (89%)
  local copies, waits for them, and re-layouts  15.8 us (8%)
  other arithmetic  2.12 us (1%)
    pallas_call x1, Pallas kernels, attend_back(): pl.pallas_call(functools.partial(attend_back_kernel, summed), out_shape=o...  102 us
    pallas_call x1, Pallas kernels, attend(): pl.pallas_call(attend_kernel, out_shape=(struct((pages, 4, block, width),...  32.4 us
    pallas_call x1, Pallas kernels, feed(): pl.pallas_call(feed_kernel, out_shape=(struct((rows, width), low), struct...  30.7 us
    reshape x6, local copies, waits for them, and re-layouts, row(): return vector.reshape(1, -1)  7.63 us
    unnamed x10, local copies, waits for them, and re-layouts  4.98 us

profile of v1, /device:TPU:9, one launch (start us, length us, event | category | flops | bytes accessed | tf_op | source)
XLA Modules:
  0.0 185.8 jit_solution(783664979991370892)
XLA Ops:
  0.6 1.3 reshape.79.out_b
  1.9 1.3 reshape.80.gain1
  3.2 1.3 reshape.81.shift1
  4.5 1.3 reshape.83.down_b
  5.7 1.3 reshape.84.gain2
  7.0 1.3 reshape.85.shift2
  8.3 0.7 convert_bitcast_fusion
  9.0 0.6 pad.6.boxes
  9.6 1.3 reshape.75.qkv_b
  10.9 1.3 reshape.82.up_b
  12.2 1.4 fusion.2.box2
  13.6 32.4 %attend.1 = (bf16[3,4,128,768]{3,2,1,0:T(8,128)(2,1)}, bf16[3,3,256,128]{3,2,1,0:T(8,128)(2,1)}, bf16[3,3,512,128]{3,2,1,0:T(8,128)(2,1)}, bf16[3,3,512,128]{3,2...) custom-call(bf16[3,128,768]{2,1,0:T(8,128)(2,1)} %tokens.1, ...), custom_call_target="tpu_custom_call" | custom-call | tf_op jit(solution)/shard_map/attend/pallas_call | solution.py:258
  46.0 30.7 %feed.1 = (bf16[384,768]{1,0:T(8,128)(2,1)}, f32[384,768]{1,0:T(8,128)}, bf16[384,768]{1,0:T(8,128)(2,1)}, bf16[6,8,864,128]{3,2,1,0:T(8,128)(2,1)}, f32[16,768]{1,0:T(8,128)}) custom-call(bf16[384,768]{1,0:T(8,128)(2,1)} %bitcast.13, bf16[384,768]{1,0:T(8,128)(2,1)} %bitcast.9, bf16[384,768]{1,0:T(8,128)(2,1)} %bitcast.11, bf16[768,768]{1,0:T(8,128)(2,1)} %out_w.1, ...), custom_call_target="tpu_custom_call" | custom-call | tf_op jit(solution)/shard_map/feed/pallas_call | solution.py:417
  76.7 101.8 %attend_back.1 = (bf16[3,128,768]{2,1,0:T(8,128)(2,1)}, bf16[2,3,2,432,128]{4,3,2,1,0:T(8,128)(2,1)}, bf16[2,3,3,2,48,128]{5,4,3,2,1,0:T(8,128)(2,1)}, f32[16,768]{1,0:T(8,128)}, f32[88,128]{1,0:T(8,128)}) custom-call(bf16[3,128,768]{2,1,0:T(8,128)(2,1)} %bitcast.12, bf16[3,4,128,768]{3,2,1,0:T(8,128)(2,1)} %get-tuple-element.49.x_in, ...), custom_call_target="tpu_custom_call" | custom-call | tf_op jit(solution)/shard_map/attend_back/pallas_call | solution.py:1087
  178.6 0.0 copy-start
  178.6 1.3 copy-done
  179.9 0.0 copy-start.1
  179.9 1.1 copy-done.1
  181.0 0.0 copy-start.2
  181.0 1.0 copy-done.2
  182.0 0.0 copy-start.3
  182.0 0.8 copy-done.3
  182.8 0.0 copy-start.4
  182.8 0.8 copy-done.4
  183.6 2.1 %finish.1 = (f32[96,3072]{1,0:T(8,128)}, f32[384,768]{1,0:T(8,128)}, f32[96,768]{1,0:T(8,128)}, f32[96,2304]{1,0:T(8,128)}, f32[288]{0:T(512)}, /*index=5*/f32[8...) custom-call(bf16[2,3,2,432,128]{4,3,2,1,0:T(8,128)(2,1)S(1)} %copy-d, ...), custom_call_target="tpu_custom_call" | custom-call | tf_op jit(solution)/shard_map/finish/pallas_call | solution.py:1142
Async XLA Ops:
  178.6 1.3 copy-start
  179.9 1.1 copy-start.1
  181.0 1.0 copy-start.2
  182.0 0.8 copy-start.3
  182.8 0.8 copy-start.4

commit v2 on v1

--- a/solution.py
+++ b/solution.py
@@ -83,9 +83,9 @@
 
 
 def attend_kernel(
-    tokens, boxes, lengths, freq, qkv_w, qkv_b, box2,
+    tokens, boxes, lengths, freq, qkv_w, qkv_b, box_w,
     x_out, q_out, k_out, v_out, sc_out, p_out, ctx_out,
-    x, box, w_q, w_kv, q, k, v, sc, probs, ctx,
+    x, box, w_q, w_kv, q, k, v, sc, probs, ctx, box2,
     own_sem, w_sem, out_sem, p_sem, ctx_sem,
     mate_send, mate_recv, side_send, side_recv, pass_send, pass_recv, ctx_send, ctx_recv,
 ):
@@ -127,6 +127,18 @@
                 remote(src.at[pg], dst.at[pg, core], mate_send.at[pg, which], mate_recv.at[pg, which], mate)
             )
             to_mate[-1].start()
+    zero = jnp.zeros_like(box_w)
+    box2[...] = jnp.concatenate(
+        [jnp.concatenate([box_w[...], zero], 1), jnp.concatenate([zero, box_w[...]], 1)], 0
+    )
+
+    def bias_of(part):
+        both = [
+            qkv_b[(2 * part + which) * half : (2 * part + which + 1) * half].reshape(1, half)
+            for which in range(2)
+        ]
+        return jnp.where(core == 0, both[0], both[1])
+
     for copy in loads:
         copy.wait()
 
@@ -159,8 +171,8 @@
             sc[pg, at * LANES : (at + 1) * LANES] = jnp.concatenate([sine, cosine], 0).T
         pltpu.make_async_copy(sc.at[pg], sc_out.at[pg], out_sem.at[pg, 1]).start()
         x_all = x[pg].reshape(keys, x.shape[-1])
-        q_all = (dot(x_all[:chip], w_q[...]) + qkv_b[:, of_half(0)]).astype(low)
-        bias = jnp.concatenate([qkv_b[:, of_half(1)], qkv_b[:, of_half(2)]], 1)
+        q_all = (dot(x_all[:chip], w_q[...]) + bias_of(0)).astype(low)
+        bias = jnp.concatenate([bias_of(1), bias_of(2)], 1)
         kv_all = (dot(x_all, w_kv[...]) + bias).astype(low)
         for hp in range(pairs):
             q[pg, hp] = q_all[:, hp * LANES : (hp + 1) * LANES]
@@ -248,11 +260,7 @@
     count = pos // 8
     freqs = 10000.0 ** (-np.arange(count) / count)
     freq = jnp.asarray(np.tile(np.tile(freqs, 4)[:, None], (1, LANES)), f32)
-    boxes_t = jnp.pad(boxes.astype(f32).transpose(0, 2, 1), ((0, 0), (0, 4), (0, 0)))
-    zero = jnp.zeros_like(box_weight)
-    box2 = jnp.concatenate(
-        [jnp.concatenate([box_weight, zero], 1), jnp.concatenate([zero, box_weight], 1)], 0
-    )
+    boxes_t = boxes.astype(f32).transpose(0, 2, 1)
     struct = jax.ShapeDtypeStruct
     vmem, dma = pltpu.VMEM, pltpu.SemaphoreType.DMA
     return pl.pallas_call(
@@ -270,7 +278,7 @@
         out_specs=(any_spec(),) * 7,
         scratch_shapes=[
             vmem((pages, 4, block, width), low),
-            vmem((pages, 4, 8, LANES), f32),
+            vmem((pages, 4, 4, LANES), f32),
             vmem((width, half), low),
             vmem((width, 2 * half), low),
             vmem((pages, pairs, chip, LANES), low),
@@ -279,6 +287,7 @@
             vmem((pages, keys, LANES), f32),
             vmem((pages, pairs, 2, keys, chip), low),
             vmem((pages, 2, block, half), low),
+            vmem((2 * head_dim, 2 * pos), low),
             dma((pages, 2)), dma((3,)), dma((pages, 5)), dma((pages, pairs)), dma((pages,)),
             dma((pages, 2)), dma((pages, 2)), dma((pages, 2)), dma((pages, 2)),
             dma((pages, 2)), dma((pages, 2)), dma((pages,)), dma((pages,)),
@@ -287,164 +296,7 @@
             collective_id=1, has_side_effects=True, vmem_limit_bytes=56 * 2**20
         ),
         name="attend",
-    )(tokens, boxes_t, lengths, freq, qkv_w, qkv_b.reshape(1, -1), box2)
-
-
-def norm_of(resid):
-    center = resid - jnp.mean(resid, axis=-1, keepdims=True)
-    spread = jnp.mean(center * center, axis=-1, keepdims=True)
-    inverse = lax.rsqrt(spread + norm_eps)
-    return center * inverse, inverse
-
-
-def norm_back(grad, normed, inverse):
-    mean = jnp.mean(grad, axis=-1, keepdims=True)
-    along = jnp.mean(grad * normed, axis=-1, keepdims=True)
-    return inverse * (grad - mean - normed * along)
-
-
-def column_sum(values):
-    return jnp.sum(values, axis=0, keepdims=True)
-
-
-def feed_kernel(
-    ctx, tokens, cotangent, out_w, up_w, down_w, out_b, gain1, shift1, up_b, down_b, gain2, shift2,
-    output, dresid1, dctx, packed, g_rows,
-    w_out, w_up, w_down, act, slope, norm1, inverse1, hidden, hidden_t, grow, staged, w_sem, up_sem, down_sem, pack_sem,
-):
-    chunks, chunk = w_up.shape[0], w_up.shape[2]
-    width = ctx.shape[1]
-    up_pieces = chunk // LANES
-    shard = width // 8
-    out_load = pltpu.make_async_copy(out_w, w_out, w_sem)
-    out_load.start()
-
-    def up_load(j):
-        return pltpu.make_async_copy(
-            up_w.at[:, pl.ds(pl.multiple_of(j * chunk, LANES), chunk)], w_up.at[j], up_sem.at[j]
-        )
-
-    def down_load(j):
-        return pltpu.make_async_copy(
-            down_w.at[pl.ds(pl.multiple_of(j * chunk, LANES), chunk)], w_down.at[j], down_sem.at[j]
-        )
-
-    for j in range(chunks):
-        up_load(j).start()
-        down_load(j).start()
-    g_rows[...] = jnp.zeros_like(g_rows)
-    out_load.wait()
-    resid = tokens[...].astype(f32) + dot(ctx[...], w_out[...]) + out_b[...]
-    normed, inverse = norm_of(resid)
-    norm1[...] = normed
-    inverse1[...] = jnp.broadcast_to(inverse, inverse1.shape)
-    first = normed * gain1[...] + shift1[...]
-    hidden[...] = first.astype(low)
-    hidden_t[...] = first.astype(low).T
-    grow[...] = first + down_b[...]
-
-    @pl.loop(0, chunks)
-    def _(j):
-        up_load(j).wait()
-        upper = dot(hidden[...], w_up[j]) + up_b[pl.ds(j, 1)]
-        cdf = 0.5 + 0.5 * lax.erf(upper * 0.7071067811865476)
-        act_low = (upper * cdf).astype(low)
-        act[j] = act_low
-        slope[j] = cdf + upper * (jnp.exp(upper * upper * -0.5) * 0.3989422804014327)
-        down_load(j).wait()
-        grow[...] += dot(act_low, w_down[j])
-
-    normed2, inverse2 = norm_of(grow[...])
-    output[...] = (normed2 * gain2[...] + shift2[...]).astype(low)
-    cot = cotangent[...].astype(f32)
-    g_rows[0:1] = column_sum(cot * normed2)
-    g_rows[1:2] = column_sum(cot)
-    dresid2 = norm_back(cot * gain2[...], normed2, inverse2)
-    dffn = dresid2.astype(low)
-    g_rows[2:3] = column_sum(dffn.astype(f32))
-    grow[...] = dresid2
-    staged[...] = dffn
-
-    @pl.loop(0, chunks)
-    def _(j):
-        dffn = staged[...]
-        dupper = (dot_nt(dffn, w_down[j]) * slope[j]).astype(low)
-        g_rows[pl.ds(8 + j, 1), :chunk] = column_sum(dupper.astype(f32))
-        grow[...] += dot_nt(dupper, w_up[j])
-        grad_up = dot(hidden_t[...], dupper).astype(low)
-        for piece in range(up_pieces):
-            part = grad_up[:, piece * LANES : (piece + 1) * LANES].reshape(8, shard, LANES)
-            packed[j, :, piece * shard : (piece + 1) * shard] = part
-        grad_down = dot_tn(act[j], dffn).astype(low)
-        for piece in range(up_pieces):
-            row = j * up_pieces + piece
-            per = up_pieces * chunks // 8
-            at = pl.ds(pl.multiple_of(up_pieces * shard + (row % per) * LANES, LANES), LANES)
-            for column in range(6):
-                packed[column, row // per, at] = grad_down[
-                    piece * LANES : (piece + 1) * LANES, column * LANES : (column + 1) * LANES
-                ]
-
-    dhidden = grow[...]
-    normed = norm1[...]
-    g_rows[3:4] = column_sum(dhidden * normed)
-    g_rows[4:5] = column_sum(dhidden)
-    back = norm_back(dhidden * gain1[...], normed, inverse1[:, :1])
-    dresid1[...] = back
-    dattn = back.astype(low)
-    g_rows[5:6] = column_sum(dattn.astype(f32))
-    dctx[...] = dot_nt(dattn, w_out[...]).astype(low)
-    grad_out = dot_tn(ctx[...], dattn).astype(low)
-    first_row = packed.shape[2] - shard
-    for column in range(6):
-        part = grad_out[:, column * LANES : (column + 1) * LANES].reshape(8, shard, LANES)
-        packed[column, :, first_row:] = part
-
-
-def feed(ctx, tokens, cotangent, out_w, up_w, down_w, out_b, gain1, shift1, up_b, down_b, gain2, shift2):
-    rows, width = ctx.shape
-    hidden_width = up_w.shape[1]
-    chunks = 6
-    chunk = hidden_width // chunks
-    shard = width // 8
-    packed_rows = (chunk // LANES) * shard + hidden_width // 8 + shard
-    struct = jax.ShapeDtypeStruct
-    vmem, dma = pltpu.VMEM, pltpu.SemaphoreType.DMA
-
-    def row(vector):
-        return vector.reshape(1, -1)
-
-    return pl.pallas_call(
-        feed_kernel,
-        out_shape=(
-            struct((rows, width), low),
-            struct((rows, width), f32),
-            struct((rows, width), low),
-            struct((6, 8, packed_rows, LANES), low),
-            struct((16, width), f32),
-        ),
-        in_specs=[vmem_spec()] * 3 + [any_spec()] * 3 + [vmem_spec()] * 7,
-        out_specs=(vmem_spec(),) * 5,
-        scratch_shapes=[
-            vmem((width, width), low),
-            vmem((chunks, width, chunk), low),
-            vmem((chunks, chunk, width), low),
-            vmem((chunks, rows, chunk), low),
-            vmem((chunks, rows, chunk), f32),
-            vmem((rows, width), f32),
-            vmem((rows, LANES), f32),
-            vmem((rows, width), low),
-            vmem((width, rows), low),
-            vmem((rows, width), f32),
-            vmem((rows, width), low),
-            dma, dma((chunks,)), dma((chunks,)), dma,
-        ],
-        compiler_params=pltpu.CompilerParams(vmem_limit_bytes=60 * 2**20),
-        name="feed",
-    )(
-        ctx, tokens, cotangent, out_w, up_w, down_w, row(out_b), row(gain1), row(shift1),
-        up_b.reshape(chunks, chunk), row(down_b), row(gain2), row(shift2),
-    )
+    )(tokens, boxes_t, lengths, freq, qkv_w, qkv_b, box_weight)
 
 
 ORDERS = ("xaym", "ayxm", "yxam")
@@ -488,48 +340,48 @@
 
 
 class EarlySum:
-    def __init__(self, ways, packed, held, mates, got, final, sems):
-        self.ways, self.packed, self.held, self.mates, self.got, self.final = ways, packed, held, mates, got, final
-        (self.own_sem, self.core_send, self.core_recv, self.send_sem, self.recv_sem, self.last_send,
-         self.last_recv, self.end_send, self.end_recv) = sems
+    def __init__(self, ways, held, got, sems):
+        self.ways, self.held, self.got = ways, held, got
+        self.send_sem, self.recv_sem = sems
         self.rows = held.shape[2]
 
-    def slices(self):
-        return ((12, 16), (8, 12), (4, 8), (0, 4))
-
-    def start(self):
+    slices = ((12, 16), (8, 12), (4, 8), (0, 4))
+
+    def halve_cores(self, packed, mates, sems):
         ways = self.ways
-        for at, (begin, end) in enumerate(self.slices()):
+        self.mates = mates
+        self.own_sem, self.core_send, self.core_recv = sems
+        for at, (begin, end) in enumerate(self.slices):
             for code in range(begin, end):
                 for order in range(3):
                     page, half = ways.piece(order, code)
                     rows = pl.ds(pl.multiple_of(half * self.rows, 16), self.rows)
                     remote(
-                        self.packed.at[3 - 3 * ways.core + order, page, rows],
-                        self.mates.at[order, code], self.core_send.at[order, at],
-                        self.core_recv.at[order, at], ways.mate,
+                        packed.at[3 - 3 * ways.core + order, page, rows], mates.at[order, code],
+                        self.core_send.at[order, at], self.core_recv.at[order, at], ways.mate,
                     ).start()
                     pltpu.make_async_copy(
-                        self.packed.at[3 * ways.core + order, page, rows], self.held.at[order, code],
+                        packed.at[3 * ways.core + order, page, rows], self.held.at[order, code],
                         self.own_sem.at[order, at],
                     ).start()
 
     def core_group(self, order, at):
-        begin, end = self.slices()[at]
+        begin, end = self.slices[at]
         part = self.mates.at[order, begin:end]
         return remote(part, part, self.core_send.at[order, at], self.core_recv.at[order, at], self.ways.mate)
 
-    def own_group(self, order, at):
-        begin, end = self.slices()[at]
-        part = self.held.at[order, begin:end]
-        return pltpu.make_async_copy(part, part, self.own_sem.at[order, at])
-
     def add_core(self, at):
-        begin, end = self.slices()[at]
+        begin, end = self.slices[at]
         for order in range(3):
-            self.own_group(order, at).wait()
+            own = self.held.at[order, begin:end]
+            pltpu.make_async_copy(own, own, self.own_sem.at[order, at]).wait()
             self.core_group(order, at).wait_recv()
             self.held[order, begin:end] = self.held[order, begin:end] + self.mates[order, begin:end]
+
+    def end_cores(self):
+        for order in range(3):
+            for at in range(4):
+                self.core_group(order, at).wait_send()
 
     def copy(self, order, group):
         begin, end = GROUPS[group]
@@ -551,6 +403,19 @@
             to = slice(begin - base, end - base)
             self.held[order, to] = self.held[order, to] + self.got[order, begin - 1 : end - 1]
 
+    def end_steps(self, groups):
+        for order in range(3):
+            for group in groups:
+                self.copy(order, group).wait_send()
+
+    def share(self, final, sems):
+        self.final = final
+        self.last_send, self.last_recv, self.end_send, self.end_recv = sems
+        for order in range(3):
+            self.copy(order, 5).wait_recv()
+            final[self.ways.core, order, self.ways.half] = self.held[order, 0] + self.got[order, 0]
+            self.last_copy(order).start()
+
     def last_copy(self, order):
         part = self.final.at[self.ways.core, order, self.ways.half]
         return remote(part, part, self.last_send.at[order], self.last_recv.at[order], self.ways.side)
@@ -558,26 +423,16 @@
     def end_copy(self, order):
         part = self.final.at[self.ways.core, order]
         return remote(part, part, self.end_send.at[order], self.end_recv.at[order], self.ways.mate)
-
-    def share(self):
-        for order in range(3):
-            self.copy(order, 5).wait_recv()
-            self.final[self.ways.core, order, self.ways.half] = self.held[order, 0] + self.got[order, 0]
-            self.last_copy(order).start()
 
     def hand_over(self):
         for order in range(3):
             self.last_copy(order).wait_recv()
             self.end_copy(order).start()
 
-    def finish(self):
+    def end(self):
         for order in range(3):
             self.end_copy(order).wait()
             self.last_copy(order).wait_send()
-            for at in range(4):
-                self.core_group(order, at).wait_send()
-            for group in range(len(GROUPS)):
-                self.copy(order, group).wait_send()
 
 
 class LateSum:
@@ -687,19 +542,227 @@
             self.copy(step).wait_send()
 
 
+def norm_of(resid):
+    center = resid - jnp.mean(resid, axis=-1, keepdims=True)
+    spread = jnp.mean(center * center, axis=-1, keepdims=True)
+    inverse = lax.rsqrt(spread + norm_eps)
+    return center * inverse, inverse
+
+
+def norm_back(grad, normed, inverse):
+    mean = jnp.mean(grad, axis=-1, keepdims=True)
+    along = jnp.mean(grad * normed, axis=-1, keepdims=True)
+    return inverse * (grad - mean - normed * along)
+
+
+def column_sum(values):
+    return jnp.sum(values, axis=0, keepdims=True)
+
+
+def feed_kernel(
+    summed, ctx, tokens, cotangent, out_w, up_w, down_w, out_b, gain1, shift1, up_b, down_b, gain2, shift2,
+    output, dresid1, dctx, packed, g_rows, part_out,
+    w_out, w_up, w_down, act, slope, norm1, inverse1, hidden, hidden_t, grow, staged, up_rows, w_sem, up_sem, down_sem, *refs,
+):
+    def row(ref):
+        return ref[...].reshape(1, -1)
+
+    if summed:
+        packed_down, held, mates, got, *sems = refs
+        ways = Ways()
+        greet(ways.everyone())
+        early = EarlySum(ways, held, got, sems[3:])
+    else:
+        packed_down = part_out
+
+    def early_step(at):
+        if not summed:
+            return
+        if at == 0:
+            early.add_core(0)
+            early.send(0)
+        elif at == 1:
+            early.add_core(1)
+            early.send(1)
+            early.add_core(2)
+            early.add_core(3)
+
+    chunks, chunk = w_up.shape[0], w_up.shape[2]
+    width = ctx.shape[1]
+    up_pieces = chunk // LANES
+    shard = width // 8
+    out_load = pltpu.make_async_copy(out_w, w_out, w_sem)
+    out_load.start()
+
+    def up_load(j):
+        return pltpu.make_async_copy(
+            up_w.at[:, pl.ds(pl.multiple_of(j * chunk, LANES), chunk)], w_up.at[j], up_sem.at[j]
+        )
+
+    def down_load(j):
+        return pltpu.make_async_copy(
+            down_w.at[pl.ds(pl.multiple_of(j * chunk, LANES), chunk)], w_down.at[j], down_sem.at[j]
+        )
+
+    for j in range(chunks):
+        up_load(j).start()
+        down_load(j).start()
+    g_rows[...] = jnp.zeros_like(g_rows)
+    for j in range(chunks):
+        up_rows[j : j + 1] = up_b[j * chunk : (j + 1) * chunk].reshape(1, chunk)
+    out_load.wait()
+    resid = tokens[...].astype(f32) + dot(ctx[...], w_out[...]) + row(out_b)
+    normed, inverse = norm_of(resid)
+    norm1[...] = normed
+    inverse1[...] = jnp.broadcast_to(inverse, inverse1.shape)
+    first = normed * row(gain1) + row(shift1)
+    hidden[...] = first.astype(low)
+    hidden_t[...] = first.astype(low).T
+    grow[...] = first + row(down_b)
+
+    @pl.loop(0, chunks)
+    def _(j):
+        up_load(j).wait()
+        upper = dot(hidden[...], w_up[j]) + up_rows[pl.ds(j, 1)]
+        cdf = 0.5 + 0.5 * lax.erf(upper * 0.7071067811865476)
+        act_low = (upper * cdf).astype(low)
+        act[j] = act_low
+        slope[j] = cdf + upper * (jnp.exp(upper * upper * -0.5) * 0.3989422804014327)
+        down_load(j).wait()
+        grow[...] += dot(act_low, w_down[j])
+
+    normed2, inverse2 = norm_of(grow[...])
+    output[...] = (normed2 * row(gain2) + row(shift2)).astype(low)
+    cot = cotangent[...].astype(f32)
+    g_rows[0:1] = column_sum(cot * normed2)
+    g_rows[1:2] = column_sum(cot)
+    dresid2 = norm_back(cot * row(gain2), normed2, inverse2)
+    dffn = dresid2.astype(low)
+    g_rows[2:3] = column_sum(dffn.astype(f32))
+    grow[...] = dresid2
+    staged[...] = dffn
+
+    @pl.loop(0, chunks)
+    def _(j):
+        grad_down = dot_tn(act[j], staged[...]).astype(low)
+        for piece in range(up_pieces):
+            at = j * up_pieces + piece
+            per = up_pieces * chunks // 8
+            rows = pl.ds(pl.multiple_of((at % per) * LANES, LANES), LANES)
+            for column in range(6):
+                packed_down[column, at // per, rows] = grad_down[
+                    piece * LANES : (piece + 1) * LANES, column * LANES : (column + 1) * LANES
+                ]
+
+    if summed:
+        early.halve_cores(packed_down, mates, sems[:3])
+
+    @pl.loop(0, chunks)
+    def _(j):
+        for at in range(chunks):
+
+            @pl.when(j == at)
+            def _(at=at):
+                early_step(at)
+
+        dffn = staged[...]
+        dupper = (dot_nt(dffn, w_down[j]) * slope[j]).astype(low)
+        g_rows[pl.ds(8 + j, 1), :chunk] = column_sum(dupper.astype(f32))
+        grow[...] += dot_nt(dupper, w_up[j])
+        grad_up = dot(hidden_t[...], dupper).astype(low)
+        for piece in range(up_pieces):
+            part = grad_up[:, piece * LANES : (piece + 1) * LANES].reshape(8, shard, LANES)
+            packed[j, :, piece * shard : (piece + 1) * shard] = part
+
+    dhidden = grow[...]
+    normed = norm1[...]
+    g_rows[3:4] = column_sum(dhidden * normed)
+    g_rows[4:5] = column_sum(dhidden)
+    back = norm_back(dhidden * row(gain1), normed, inverse1[:, :1])
+    dresid1[...] = back
+    dattn = back.astype(low)
+    g_rows[5:6] = column_sum(dattn.astype(f32))
+    dctx[...] = dot_nt(dattn, w_out[...]).astype(low)
+    grad_out = dot_tn(ctx[...], dattn).astype(low)
+    first_row = packed.shape[2] - shard
+    for column in range(6):
+        part = grad_out[:, column * LANES : (column + 1) * LANES].reshape(8, shard, LANES)
+        packed[column, :, first_row:] = part
+    if summed:
+        early.receive(0)
+        early.receive(1)
+        part_out[...] = held[:, :8]
+        early.end_cores()
+        early.end_steps(range(2))
+
+
+def feed(ctx, tokens, cotangent, out_w, up_w, down_w, vectors, summed):
+    rows, width = ctx.shape
+    hidden_width = up_w.shape[1]
+    chunks = 6
+    chunk = hidden_width // chunks
+    shard = width // 8
+    packed_rows = (chunk // LANES) * shard + shard
+    down_rows = hidden_width // 8
+    struct = jax.ShapeDtypeStruct
+    vmem, dma = pltpu.VMEM, pltpu.SemaphoreType.DMA
+    packed_down = (6, 8, down_rows, LANES)
+    extra, params = [], {}
+    if summed:
+        half = down_rows // 2
+        extra = [
+            vmem(packed_down, low), vmem((3, 16, half, LANES), low), vmem((3, 16, half, LANES), low),
+            vmem((3, 15, half, LANES), low), dma((3, 4)), dma((3, 4)), dma((3, 4)),
+            dma((3, len(GROUPS))), dma((3, len(GROUPS))),
+        ]
+        params = dict(collective_id=3, has_side_effects=True)
+
+    return pl.pallas_call(
+        functools.partial(feed_kernel, summed),
+        out_shape=(
+            struct((rows, width), low),
+            struct((rows, width), f32),
+            struct((rows, width), low),
+            struct((6, 8, packed_rows, LANES), low),
+            struct((16, width), f32),
+            struct((3, 8, half, LANES) if summed else packed_down, low),
+        ),
+        in_specs=[vmem_spec()] * 3 + [any_spec()] * 3 + [vmem_spec()] * 7,
+        out_specs=(vmem_spec(),) * 6,
+        scratch_shapes=[
+            vmem((width, width), low),
+            vmem((chunks, width, chunk), low),
+            vmem((chunks, chunk, width), low),
+            vmem((chunks, rows, chunk), low),
+            vmem((chunks, rows, chunk), f32),
+            vmem((rows, width), f32),
+            vmem((rows, LANES), f32),
+            vmem((rows, width), low),
+            vmem((width, rows), low),
+            vmem((rows, width), f32),
+            vmem((rows, width), low),
+            vmem((chunks, chunk), f32),
+            dma, dma((chunks,)), dma((chunks,)), *extra,
+        ],
+        compiler_params=pltpu.CompilerParams(vmem_limit_bytes=60 * 2**20, **params),
+        name="feed",
+    )(ctx, tokens, cotangent, out_w, up_w, down_w, *vectors)
+
+
 def attend_back_kernel(
     summed, dctx_own, x_in, q_in, k_in, v_in, sc_in, p_in, qkv_w, box_w, dresid1, *refs
 ):
     if summed:
         (
-            early_in, small_in,
-            dx_out, early_out, late_out, small_out, tiny_out,
+            early_in, down_in, small_in,
+            dx_out, early_out, down_out, late_out, small_out, tiny_out,
             x, q, k, v, sc, probs, dctx, dq, dkv, x_t, w_c, dx, dx_mate, dx_side, box_t, g_box, g_bias, late_packed,
             in_sem, p_sem, w_sem, own_sem, mate_send, mate_recv, core_send, core_recv, side_send, side_recv,
-            early_held, early_mates, early_got, late_held, late_got, small_value, small_got, tiny_value, tiny_got,
+            early_held, early_mates, early_got, down_held, down_got, late_held, late_got, small_value, small_got, tiny_value, tiny_got,
             *sems,
         ) = refs
-        early_sems, late_sems, small_sems, tiny_sems = sems[:9], sems[9:17], sems[17:19], sems[19:21]
+        core_sems, early_sems, early_ends, down_sems, down_ends = sems[:3], sems[3:5], sems[5:9], sems[9:11], sems[11:15]
+        down_load, late_sems, small_sems, tiny_sems = sems[15], sems[16:24], sems[24:26], sems[26:28]
     else:
         (
             dx_out, late_packed, tiny_out,
@@ -753,14 +816,20 @@
         copy.start()
     p_load(0, 0).start()
     if summed:
-        early = EarlySum(ways, early_in, early_held, early_mates, early_got, early_out, early_sems)
+        down_copy = pltpu.make_async_copy(down_in, down_held, down_load)
+        down_copy.start()
+        early = EarlySum(ways, early_held, early_got, early_sems)
+        down = EarlySum(ways, down_held, down_got, down_sems)
         small = SmallSum(ways, small_value, small_got, small_sems)
         tiny = SmallSum(ways, tiny_value, tiny_got, tiny_sems)
 
         def late(hp):
             return LateSum(ways, hp, late_packed, late_held, late_got, late_out, late_sems)
 
-        early.start()
+        early.halve_cores(early_in, early_mates, core_sems)
+        down_copy.wait()
+        down.send(2)
+        down.send(3)
         small_value[0] = small_in[...]
         small.start()
     for pg in range(pages):
@@ -873,37 +942,40 @@
     def early_step(at):
         if not summed:
             return
-        if at == 0:
+        if at == 1:
+            down.receive(2)
+            down.receive(3)
+            down.send(4)
             early.add_core(0)
             early.send(0)
-        elif at == 1:
             early.add_core(1)
             early.send(1)
             early.add_core(2)
             early.add_core(3)
+        elif at == 2:
+            down.receive(4)
+            down.send(5)
+        elif at == 3:
             small.advance(0)
-        elif at == 2:
+        elif at == 4:
             early.receive(0)
             early.send(2)
             early.send(3)
+        elif at == 5:
+            early.receive(1)
+            down.share(down_out, down_ends)
             small.advance(1)
-        elif at == 3:
-            early.receive(1)
-            small.advance(2)
-        elif at == 4:
+        elif at == 6:
             early.receive(2)
             early.send(4)
-            small.advance(3)
-        elif at == 5:
             early.receive(3)
-            small.advance(4)
-        elif at == 6:
+            down.hand_over()
+        elif at == 7:
             early.receive(4)
             early.send(5)
-        elif at == 7:
-            early.share()
+            small.advance(2)
         elif at == 8:
-            early.hand_over()
+            small.advance(3)
 
     def bias_rows():
         for part in range(3):
@@ -969,11 +1041,14 @@
         tiny.start()
     input_part(last)
     if summed:
+        early.share(early_out, early_ends)
         tiny.advance(0)
         late(2).advance(0)
         late(1).advance(1)
         late(0).advance(2)
         pass_input(last)
+        small.advance(4)
+        early.hand_over()
         tiny.advance(1)
         late(2).advance(1)
         late(1).advance(2)
@@ -1002,7 +1077,11 @@
     if summed:
         small_out[...] = small_value[5]
         tiny_out[...] = tiny_value[5]
-        early.finish()
+        early.end_cores()
+        early.end_steps(range(6))
+        early.end()
+        down.end_steps((2, 3, 4, 5))
+        down.end()
         for hp in range(pairs):
             late(hp).finish()
         small.finish()
@@ -1014,7 +1093,7 @@
             tiny_out[at : at + 1] = row
 
 
-def attend_back(dctx, x, q, k, v, sc, probs, qkv_w, box_w, dresid1, packed, small, summed):
+def attend_back(dctx, x, q, k, v, sc, probs, qkv_w, box_w, dresid1, packed, down, small, summed):
     pages, pairs, chip, _ = q.shape
     keys = k.shape[2]
     width = x.shape[-1]
@@ -1052,11 +1131,13 @@
     operands = [dctx, x, q, k, v, sc, probs, qkv_w, box_w, dresid1]
     in_specs = [any_spec()] * 8 + [vmem_spec()] * 2
     if summed:
-        operands += [packed, small]
-        in_specs += [any_spec(), vmem_spec()]
+        rest = down.shape[2]
+        operands += [packed, down, small]
+        in_specs += [any_spec(), any_spec(), vmem_spec()]
         outs = (
             struct((pages, block, width), low),
             struct((2, 3, 2, wide, LANES), low),
+            struct((2, 3, 2, rest, LANES), low),
             struct((2, pairs, 3, 2, shard // 2, LANES), low),
             struct(small.shape, f32),
             struct((tiny_rows, LANES), f32),
@@ -1066,6 +1147,8 @@
             vmem((3, 16, wide, LANES), low),
             vmem((3, 16, wide, LANES), low),
             vmem((3, 15, wide, LANES), low),
+            vmem((3, 8, rest, LANES), low),
+            vmem((3, 7, rest, LANES), low),
             vmem((pairs, 3, 8, shard // 2, LANES), low),
             vmem((pairs, 3, 15, shard // 2, LANES), low),
             vmem((6,) + small.shape, f32),
@@ -1074,7 +1157,7 @@
             vmem((5, tiny_rows, LANES), f32),
         ]
         groups = len(GROUPS)
-        scratch += [dma((3, 4))] * 3 + [dma((3, groups))] * 2 + [dma((3,))] * 4
+        scratch += [dma((3, 4))] * 3 + ([dma((3, groups))] * 2 + [dma((3,))] * 4) * 2 + [dma]
         scratch += [dma((pairs, 3))] * 2 + [dma((pairs, 3, 3))] * 2 + [dma((pairs, 3))] * 4
         scratch += [dma((5,))] * 4
     else:
@@ -1098,11 +1181,19 @@
 
 
 def finish_kernel(
-    early, late, small, tiny, dx, up, down, out, qkv, qkv_b, box, out_b, gain1, shift1, up_b, down_b, gain2, shift2, input_grad
+    early_in, rest_in, late_in, small_in, tiny_in, dx_in,
+    up, down, out, qkv, qkv_b, box, out_b, gain1, shift1, up_b, down_b, gain2, shift2, input_grad,
+    early, rest, late, small, tiny, sems,
 ):
     page = lax.axis_index("page")
     shard = out.shape[0]
     pieces = up.shape[1] // (6 * LANES)
+    pairs = ((early_in, early), (rest_in, rest), (late_in, late), (small_in, small), (tiny_in, tiny), (dx_in, input_grad))
+    copies = [pltpu.make_async_copy(src, dst, sems.at[at]) for at, (src, dst) in enumerate(pairs)]
+    for copy in copies:
+        copy.start()
+    for copy in copies:
+        copy.wait()
     for which in range(2):
         for order in range(3):
             column = which * 3 + order
@@ -1111,9 +1202,8 @@
                 at = (column * pieces + piece) * LANES
                 up[:, at : at + LANES] = rows[piece * shard : (piece + 1) * shard]
             at = column * LANES
-            first = pieces * shard
-            down[:, at : at + LANES] = rows[first : first + down.shape[0]]
-            out[:, at : at + LANES] = rows[first + down.shape[0] :]
+            out[:, at : at + LANES] = rows[pieces * shard :]
+            down[:, at : at + LANES] = rest[which, order].astype(f32).reshape(-1, LANES)
             for part in range(3):
                 at = (part * 6 + column) * LANES
                 qkv[:, at : at + LANES] = late[which, order, part].astype(f32).reshape(shard, LANES)
@@ -1131,29 +1221,31 @@
     rest = lax.rem(first, LANES)
     row = pltpu.roll(jnp.concatenate(parts, 1), lax.rem(4 * LANES - rest, 4 * LANES), 1)
     qkv_b[...] = row[0, :count]
-    input_grad[...] = dx[...]
-
-
-def finish(early, late, small, tiny, dx):
+
+
+def finish(early, rest, late, small, tiny, dx):
     struct = jax.ShapeDtypeStruct
     shapes = (
         (96, 3072), (384, 768), (96, 768), (96, 2304), (288,), (8, LANES), (96,), (96,), (96,), (384,), (96,), (96,), (96,),
     )
+    operands = (early, rest, late, small, tiny, dx)
     return pl.pallas_call(
         finish_kernel,
         out_shape=tuple(struct(shape, f32) for shape in shapes) + (struct(dx.shape, low),),
-        in_specs=[vmem_spec()] * 5,
+        in_specs=[any_spec()] * 6,
         out_specs=(vmem_spec(),) * 14,
-        compiler_params=pltpu.CompilerParams(vmem_limit_bytes=40 * 2**20),
+        scratch_shapes=[pltpu.VMEM(operand.shape, operand.dtype) for operand in operands[:5]]
+        + [pltpu.SemaphoreType.DMA((6,))],
+        compiler_params=pltpu.CompilerParams(vmem_limit_bytes=63 * 2**20),
         name="finish",
-    )(early, late, small, tiny, dx)
-
-
-def reduce_by_collectives(packed, packed_qkv, vectors):
+    )(*operands)
+
+
+def reduce_by_collectives(packed, packed_down, packed_qkv, vectors):
     core = lax.axis_index("blk") % 2
     up = packed[:, :, :384].reshape(6, 8, 4, 96, LANES).transpose(1, 3, 0, 2, 4).reshape(768, 3072)
-    down = packed[:, :, 384:768].transpose(1, 2, 0, 3).reshape(3072, 768)
-    out = packed[:, :, 768:].transpose(1, 2, 0, 3).reshape(768, 768)
+    down = packed_down.transpose(1, 2, 0, 3).reshape(3072, 768)
+    out = packed[:, :, 384:].transpose(1, 2, 0, 3).reshape(768, 768)
     own = packed_qkv.transpose(2, 3, 1, 0, 4).reshape(768, 3, 384)
     qkv = jnp.zeros((768, 3, 2, 384), low)
     qkv = lax.dynamic_update_slice(qkv, own[:, :, None], (0, 0, core, 0)).reshape(768, 2304)
@@ -1173,22 +1265,22 @@
     pages, block, width = tokens.shape
     rows = pages * block
     x, q, k, v, sc, probs, ctx = attend(tokens, boxes, lengths, qkv_weight, qkv_bias, box_weight)
-    output, dresid1, dctx, packed, small = feed(
+    summed = lax.axis_size("page") == 8
+    output, dresid1, dctx, packed, small, down = feed(
         ctx.reshape(rows, width), tokens.reshape(rows, width), cotangent.reshape(rows, width),
-        out_weight, up_weight, down_weight, out_bias, norm1_gain, norm1_bias, up_bias, down_bias,
-        norm2_gain, norm2_bias,
+        out_weight, up_weight, down_weight,
+        (out_bias, norm1_gain, norm1_bias, up_bias, down_bias, norm2_gain, norm2_bias), summed,
     )
-    summed = lax.axis_size("page") == 8
     parts = attend_back(
         dctx.reshape(pages, block, width), x, q, k, v, sc, probs, qkv_weight, box_weight,
-        dresid1.reshape(pages, block, width), packed, small, summed,
+        dresid1.reshape(pages, block, width), packed, down, small, summed,
     )
     output = output.reshape(pages, block, width)
     if summed:
-        dx, early, late, small, tiny = parts
+        dx, early, rest, late, small, tiny = parts
         (
             up_w, down_w, out_w, qkv_w, qkv_b, box, out_b, gain1, shift1, up_b, down_b, gain2, shift2, input_grad,
-        ) = finish(early, late, small, tiny, dx)
+        ) = finish(early, rest, late, small, tiny, dx)
         box = box.reshape(-1)
     else:
         input_grad, packed_qkv, tiny = parts
@@ -1198,7 +1290,7 @@
         )
         (
             qkv_w, out_w, up_w, down_w, qkv_b, box, out_b, gain1, shift1, up_b, down_b, gain2, shift2,
-        ) = reduce_by_collectives(packed, packed_qkv, vectors)
+        ) = reduce_by_collectives(packed, down, packed_qkv, vectors)
     return (
         output, input_grad, qkv_w, qkv_b, box, out_w, out_b, gain1, shift1, up_w, up_b, down_w, down_b, gain2, shift2,
     )

time: 187 us -> 161 us (0.86)
  local copies, waits for them, and re-layouts: 15.8 us -> 0.82 us
  Pallas kernels: 167 us -> 157 us
    pallas_call x1, Pallas kernels: 102 us -> 81 us  [attend_back(): pl.pallas_call(functools.partial(attend_back_kernel, summed), out_shape=o...]
    reshape x8 -> x0, local copies, waits for them, and re-layouts: 10.3 us -> none  [the longest x6 7.63 us: row(): return vector.reshape(1, -1)]
    pallas_call x1, Pallas kernels: 30.7 us -> 39.5 us  [feed(): pl.pallas_call(functools.partial(feed_kernel, summed), out_shape=(struct(...]
    unnamed x10 -> x3, local copies, waits for them, and re-layouts: 4.98 us -> 0.82 us
where the time goes in v2:
time: 161 us; the launch traced here: 160 us
  Pallas kernels  157 us (98%)
    pallas_call x1, Pallas kernels, attend_back(): pl.pallas_call(functools.partial(attend_back_kernel, summed), out_shape=o...  81 us
    pallas_call x1, Pallas kernels, feed(): pl.pallas_call(functools.partial(feed_kernel, summed), out_shape=(struct(...  39.5 us
    pallas_call x1, Pallas kernels, attend(): pl.pallas_call(attend_kernel, out_shape=(struct((pages, 4, block, width),...  32.4 us
    pallas_call x1, Pallas kernels, finish(): pl.pallas_call(finish_kernel, out_shape=tuple((struct(shape, f32) for sha...  3.86 us

profile of v2, /device:TPU:9, one launch (start us, length us, event | category | flops | bytes accessed | tf_op | source)
XLA Modules:
  0.0 159.6 jit_solution(2095199410197438362)
XLA Ops:
  0.6 1.3 convert_bitcast_fusion.boxes
  1.9 32.4 %attend.1 = (bf16[3,4,128,768]{3,2,1,0:T(8,128)(2,1)}, bf16[3,3,256,128]{3,2,1,0:T(8,128)(2,1)}, bf16[3,3,512,128]{3,2,1,0:T(8,128)(2,1)}, bf16[3,3,512,128]{3,2...) custom-call(bf16[3,128,768]{2,1,0:T(8,128)(2,1)} %tokens.1, ...), custom_call_target="tpu_custom_call" | custom-call | tf_op jit(solution)/shard_map/attend/pallas_call | solution.py:266
  34.4 39.5 %feed.1 = (bf16[384,768]{1,0:T(8,128)(2,1)}, f32[384,768]{1,0:T(8,128)}, bf16[384,768]{1,0:T(8,128)(2,1)}, bf16[6,8,480,128]{3,2,1,0:T(8,128)(2,1)}, f32[16,768]...) custom-call(bf16[384,768]{1,0:T(8,128)(2,1)} %bitcast.13, bf16[384,768]{1,0:T(8,128)(2,1)} %bitcast.9, ...), custom_call_target="tpu_custom_call" | custom-call | tf_op jit(solution)/shard_map/feed/pallas_call | solution.py:720
  73.9 81.0 %attend_back.1 = (bf16[3,128,768]{2,1,0:T(8,128)(2,1)}, bf16[2,3,2,240,128]{4,3,2,1,0:T(8,128)(2,1)}, bf16[2,3,2,192,128]{4,3,2,1,0:T(8,128)(2,1)}, bf16[2,3,3,2...) custom-call(bf16[3,128,768]{2,1,0:T(8,128)(2,1)} %bitcast.12, ...), custom_call_target="tpu_custom_call" | custom-call | tf_op jit(solution)/shard_map/attend_back/pallas_call | solution.py:1170
  154.9 0.0 copy-start
  154.9 3.9 %finish.1 = (f32[96,3072]{1,0:T(8,128)}, f32[384,768]{1,0:T(8,128)}, f32[96,768]{1,0:T(8,128)}, f32[96,2304]{1,0:T(8,128)}, f32[288]{0:T(512)}, /*index=5*/f32[8...) custom-call(bf16[2,3,2,240,128]{4,3,2,1,0:T(8,128)(2,1)} %get-tuple-, ...), custom_call_target="tpu_custom_call" | custom-call | tf_op jit(solution)/shard_map/finish/pallas_call | solution.py:1232
  158.8 0.0 copy-done
  158.8 0.8 copy.34
Async XLA Ops:
  154.9 3.9 %copy-start = (bf16[384,768]{1,0:T(8,128)(2,1)S(1)}, bf16[384,768]{1,0:T(8,128)(2,1)}, u32[]{:S(2)}) copy-start(bf16[384,768]{1,0:T(8,128)(2,1)} %get-tuple-element.49) | copy-start | bytes 1769476

commit v3 on v2

v3 whole, which is shorter than its diff:
```python
import functools

import jax
import jax.numpy as jnp
import numpy as np
from jax import lax
from jax.experimental import pallas as pl
from jax.experimental.pallas import tpu as pltpu
from jax.sharding import PartitionSpec as P

norm_eps = 1e-12
MESH = pl.DeviceIdType.MESH
LANES = 128
low = jnp.bfloat16
f32 = jnp.float32


def core_of(blk):
    return blk + 1 - 2 * (blk % 2)


def side_of(blk):
    return (blk + 2) % 4


def greet(others):
    barrier = pltpu.get_barrier_semaphore()
    for other in others:
        pl.semaphore_signal(barrier, inc=1, device_id=other, device_id_type=MESH)
    pl.semaphore_wait(barrier, len(others))


def remote(src, dst, send_sem, recv_sem, to):
    return pltpu.make_async_remote_copy(
        src_ref=src, dst_ref=dst, send_sem=send_sem, recv_sem=recv_sem, device_id=to,
        device_id_type=MESH,
    )


def dot(a, b):
    return jnp.dot(a, b, preferred_element_type=f32)


def dot_nt(a, b):
    return lax.dot_general(a, b, (((1,), (1,)), ((), ())), preferred_element_type=f32)


def dot_tn(a, b):
    return lax.dot_general(a, b, (((0,), (0,)), ((), ())), preferred_element_type=f32)


def sin_cos(theta):
    turns = jnp.floor(theta * 0.6366197723675814 + 0.5)
    rest = theta - turns * 1.5703125
    rest = rest - turns * 4.837512969970703125e-4
    rest = rest - turns * 7.54978995489188216e-8
    square = rest * rest
    sine = ((-1.9515295891e-4 * square + 8.3321608736e-3) * square - 1.6666654611e-1) * square
    sine = sine * rest + rest
    cosine = (2.443315711809948e-5 * square - 1.388731625493765e-3) * square + 4.166664568298827e-2
    cosine = cosine * square * square - 0.5 * square + 1.0
    quarter = turns.astype(jnp.int32)
    odd = (quarter & 1) == 1
    sine_at = jnp.where(odd, cosine, sine)
    cosine_at = jnp.where(odd, sine, cosine)
    sine_at = jnp.where((quarter & 2) == 2, -sine_at, sine_at)
    cosine_at = jnp.where(((quarter + 1) & 2) == 2, -cosine_at, cosine_at)
    return sine_at, cosine_at


def lane_halves(shape):
    return lax.broadcasted_iota(jnp.int32, shape, 1) < LANES // 2


def turned(both):
    swapped = pltpu.roll(both, LANES // 2, 1)
    left = lane_halves(both.shape)
    return jnp.where(left, -swapped, both), jnp.where(left, both, swapped)


def rotate_key(proj, cosine2, sine2):
    return proj * cosine2 + pltpu.roll(proj, LANES // 2, 1) * sine2


def attend_kernel(
    tokens, boxes, lengths, freq, qkv_w, qkv_b, box_w,
    x_t_out, q_out, k_out, v_out, sc_out, p_out, ctx_out,
    x, x_t, box, w_q, w_kv, q, k, v, sc, probs, ctx, box2,
    own_sem, w_sem, out_sem, p_sem, ctx_sem,
    mate_send, mate_recv, side_send, side_recv, pass_send, pass_recv, ctx_send, ctx_recv,
):
    page, blk = lax.axis_index("page"), lax.axis_index("blk")
    core, side_at = blk % 2, blk // 2
    mate, side = (page, core_of(blk)), (page, side_of(blk))
    pages = tokens.shape[0]
    half = w_q.shape[1]
    pairs = half // LANES
    chip = 2 * tokens.shape[1]
    keys = 2 * chip
    scale = 0.125

    def of_half(part):
        return pl.ds(pl.multiple_of(part * 2 * half + core * half, LANES), half)

    loads = [
        pltpu.make_async_copy(qkv_w.at[:, of_half(0)], w_q, w_sem.at[0]),
        pltpu.make_async_copy(qkv_w.at[:, of_half(1)], w_kv.at[:, :half], w_sem.at[1]),
        pltpu.make_async_copy(qkv_w.at[:, of_half(2)], w_kv.at[:, half:], w_sem.at[2]),
    ]
    own = []
    for pg in range(pages):
        own.append(pltpu.make_async_copy(tokens.at[pg], x.at[pg, core], own_sem.at[pg, 0]))
        own.append(pltpu.make_async_copy(boxes.at[pg], box.at[pg, core], own_sem.at[pg, 1]))
    for copy in own:
        copy.start()
    for copy in loads:
        copy.start()
    greet((mate, side))
    to_mate, to_side = [], []
    for pg in range(pages):
        for which, (src, dst) in enumerate(((tokens, x), (boxes, box))):
            to_side.append(
                remote(src.at[pg], dst.at[pg, 2 + core], side_send.at[pg, which], side_recv.at[pg, which], side)
            )
            to_side[-1].start()
            to_mate.append(
                remote(src.at[pg], dst.at[pg, core], mate_send.at[pg, which], mate_recv.at[pg, which], mate)
            )
            to_mate[-1].start()
    zero = jnp.zeros_like(box_w)
    box2[...] = jnp.concatenate(
        [jnp.concatenate([box_w[...], zero], 1), jnp.concatenate([zero, box_w[...]], 1)], 0
    )

    def bias_of(part):
        both = [
            qkv_b[(2 * part + which) * half : (2 * part + which + 1) * half].reshape(1, half)
            for which in range(2)
        ]
        return jnp.where(core == 0, both[0], both[1])

    for copy in loads:
        copy.wait()

    @pl.loop(0, pages)
    def _(pg):
        passed = []
        for which, (src, dst) in enumerate(((tokens, x), (boxes, box))):
            remote(
                src.at[pg], dst.at[pg, 2 + core], side_send.at[pg, which], side_recv.at[pg, which], side
            ).wait_recv()
            copy = remote(
                dst.at[pg, 2 + core], dst.at[pg, 2 + core], pass_send.at[pg, which],
                pass_recv.at[pg, which], mate,
            )
            copy.start()
            passed.append(copy)
            pltpu.make_async_copy(src.at[pg], dst.at[pg, core], own_sem.at[pg, which]).wait()
            remote(
                src.at[pg], dst.at[pg, core], mate_send.at[pg, which], mate_recv.at[pg, which], mate
            ).wait_recv()
        for copy in passed:
            copy.wait_recv()
        for at in range(4):
            rows = box[pg, at]
            spread = [
                jnp.broadcast_to(rows[c : c + 1], (freq.shape[0] // 4, LANES)) for c in range(4)
            ]
            sine, cosine = sin_cos(jnp.concatenate(spread, 0) * freq[...])
            sc[pg, at * LANES : (at + 1) * LANES] = jnp.concatenate([sine, cosine], 0).T
        pltpu.make_async_copy(sc.at[pg], sc_out.at[pg], out_sem.at[pg, 1]).start()
        x_all = x[pg].reshape(keys, x.shape[-1])
        x_t[pg] = x_all.T
        pltpu.make_async_copy(x_t.at[pg], x_t_out.at[pg], out_sem.at[pg, 0]).start()
        q_all = (dot(x_all[:chip], w_q[...]) + bias_of(0)).astype(low)
        bias = jnp.concatenate([bias_of(1), bias_of(2)], 1)
        kv_all = (dot(x_all, w_kv[...]) + bias).astype(low)
        for hp in range(pairs):
            q[pg, hp] = q_all[:, hp * LANES : (hp + 1) * LANES]
            k[pg, hp] = kv_all[:, hp * LANES : (hp + 1) * LANES]
            v[pg, hp] = kv_all[:, half + hp * LANES : half + (hp + 1) * LANES]
        for which, (src, dst) in enumerate(((q, q_out), (k, k_out), (v, v_out))):
            pltpu.make_async_copy(src.at[pg], dst.at[pg], out_sem.at[pg, 2 + which]).start()
        place = lax.broadcasted_iota(jnp.int32, (keys, chip), 0) + side_at * chip
        place = jnp.where(place >= keys, place - keys, place)
        valid = place < lengths[pg]

        @pl.loop(0, pairs)
        def _(hp):
            both = sc[pg]
            cosine2, sine2 = turned(both)
            basis = both.astype(low)
            basis_q = (both[:chip] * scale).astype(low)
            left = lane_halves((chip, LANES))
            cosine_q = jnp.where(left, -cosine2[:chip], cosine2[:chip]) * scale
            sine_q = jnp.where(left, sine2[:chip], -sine2[:chip]) * scale
            q_pair, k_pair = q[pg, hp], k[pg, hp]
            q_proj = dot(q_pair, box2[...])
            k_proj = dot(k_pair, box2[...])
            v_t = v[pg, hp].T
            outs = []
            for e in range(2):
                at = slice(e * LANES, (e + 1) * LANES)
                q_pos = rotate_key(q_proj[:, at], cosine_q, sine_q).astype(low)
                k_pos = rotate_key(k_proj[:, at], cosine2, sine2).astype(low)
                mine = left if e == 0 else jnp.logical_not(left)
                q_own = jnp.where(mine, q_pair.astype(f32) * scale, 0.0).astype(low)
                scores = dot_nt(
                    jnp.concatenate([basis, k_pos], 1), jnp.concatenate([q_pos, basis_q], 1)
                )
                scores = scores + dot_nt(k_pair, q_own)
                scores = jnp.where(valid, scores, -1e30)
                top = jnp.max(scores, axis=0, keepdims=True)
                grown = jnp.exp(scores - top)
                total = jnp.sum(grown, axis=0, keepdims=True)
                p = (grown * (1.0 / total)).astype(low)
                probs[pg, hp, e] = p
                outs.append(dot(v_t[e * LANES // 2 : (e + 1) * LANES // 2], p))
            pltpu.make_async_copy(probs.at[pg, hp], p_out.at[pg, hp], p_sem.at[pg, hp]).start()
            context = jnp.concatenate(outs, 0).T.astype(low)
            lanes = pl.ds(pl.multiple_of(hp * LANES, LANES), LANES)
            ctx[pg, 0, :, lanes] = context[: chip // 2]
            ctx[pg, 1, :, lanes] = context[chip // 2 :]

        mine = pl.ds(pl.multiple_of(core * half, LANES), half)
        pltpu.make_async_copy(ctx.at[pg, core], ctx_out.at[pg, :, mine], ctx_sem.at[pg]).start()
        remote(
            ctx.at[pg, 1 - core], ctx_out.at[pg, :, mine], ctx_send.at[pg], ctx_recv.at[pg], mate
        ).start()
        for copy in passed:
            copy.wait_send()

    mine = pl.ds(pl.multiple_of(core * half, LANES), half)
    for pg in range(pages):
        for which, (src, dst) in enumerate(((x_t, x_t_out), (sc, sc_out), (q, q_out), (k, k_out), (v, v_out))):
            pltpu.make_async_copy(src.at[pg], dst.at[pg], out_sem.at[pg, which]).wait()
        for hp in range(pairs):
            pltpu.make_async_copy(probs.at[pg, hp], p_out.at[pg, hp], p_sem.at[pg, hp]).wait()
        pltpu.make_async_copy(ctx.at[pg, core], ctx_out.at[pg, :, mine], ctx_sem.at[pg]).wait()
        remote(
            ctx.at[pg, 1 - core], ctx_out.at[pg, :, mine], ctx_send.at[pg], ctx_recv.at[pg], mate
        ).wait()
    for copy in to_side + to_mate:
        copy.wait_send()


def any_spec():
    return pl.BlockSpec(memory_space=pl.ANY)


def vmem_spec():
    return pl.BlockSpec(memory_space=pltpu.VMEM)


def attend(tokens, boxes, lengths, qkv_w, qkv_b, box_weight):
    pages, block, width = tokens.shape
    head_dim, pos = box_weight.shape
    half = width // 2
    pairs = half // LANES
    chip, keys = 2 * block, 4 * block
    count = pos // 8
    freqs = 10000.0 ** (-np.arange(count) / count)
    freq = jnp.asarray(np.tile(np.tile(freqs, 4)[:, None], (1, LANES)), f32)
    boxes_t = boxes.astype(f32).transpose(0, 2, 1)
    struct = jax.ShapeDtypeStruct
    vmem, dma = pltpu.VMEM, pltpu.SemaphoreType.DMA
    return pl.pallas_call(
        attend_kernel,
        out_shape=(
            struct((pages, width, keys), low),
            struct((pages, pairs, chip, LANES), low),
            struct((pages, pairs, keys, LANES), low),
            struct((pages, pairs, keys, LANES), low),
            struct((pages, keys, LANES), f32),
            struct((pages, pairs, 2, keys, chip), low),
            struct((pages, block, width), low),
        ),
        in_specs=[any_spec(), any_spec(), pl.BlockSpec(memory_space=pltpu.SMEM), vmem_spec(), any_spec(), vmem_spec(), vmem_spec()],
        out_specs=(any_spec(),) * 7,
        scratch_shapes=[
            vmem((pages, 4, block, width), low),
            vmem((pages, width, keys), low),
            vmem((pages, 4, 4, LANES), f32),
            vmem((width, half), low),
            vmem((width, 2 * half), low),
            vmem((pages, pairs, chip, LANES), low),
            vmem((pages, pairs, keys, LANES), low),
            vmem((pages, pairs, keys, LANES), low),
            vmem((pages, keys, LANES), f32),
            vmem((pages, pairs, 2, keys, chip), low),
            vmem((pages, 2, block, half), low),
            vmem((2 * head_dim, 2 * pos), low),
            dma((pages, 2)), dma((3,)), dma((pages, 5)), dma((pages, pairs)), dma((pages,)),
            dma((pages, 2)), dma((pages, 2)), dma((pages, 2)), dma((pages, 2)),
            dma((pages, 2)), dma((pages, 2)), dma((pages,)), dma((pages,)),
        ],
        compiler_params=pltpu.CompilerParams(
            collective_id=1, has_side_effects=True, vmem_limit_bytes=56 * 2**20
        ),
        name="attend",
    )(tokens, boxes_t, lengths, freq, qkv_w, qkv_b, box_weight)


ORDERS = ("xaym", "ayxm", "yxam")
GROUPS = ((12, 16), (8, 12), (6, 8), (4, 6), (2, 4), (1, 2))


def flip(page, way):
    x, z = page % 2, page // 2
    if way == "x":
        return z * 2 + (1 - x)
    if way == "a":
        return (z + 1 - 2 * (z % 2)) * 2 + x
    return ((z + 2) % 4) * 2 + x


class Ways:
    def __init__(self):
        self.page, self.blk = lax.axis_index("page"), lax.axis_index("blk")
        self.core, self.half = self.blk % 2, self.blk // 2
        self.mate, self.side = (self.page, core_of(self.blk)), (self.page, side_of(self.blk))

    def partner(self, way):
        return self.side if way == "y" else (flip(self.page, way), self.blk)

    def piece(self, order, code):
        page, half = self.page, self.half
        for place, way in enumerate(ORDERS[order]):
            if code >> (3 - place) & 1:
                if way == "y":
                    half = 1 - half
                else:
                    page = flip(page, way)
        return page, half

    def everyone(self):
        return [self.partner(way) for way in "xamy"] + [self.mate]


def step_of(code):
    return 4 - code.bit_length()


class EarlySum:
    def __init__(self, ways, packed, mates, got, final, sems):
        self.ways, self.packed, self.mates, self.got, self.final = ways, packed, mates, got, final
        (self.core_send, self.core_recv, self.send_sem, self.recv_sem, self.last_send, self.last_recv,
         self.end_send, self.end_recv) = sems
        self.rows = packed.shape[2] // 2

    slices = ((12, 16), (8, 12), (4, 8), (0, 4))

    def place(self, order, code, core, begin=0, end=None):
        page, half = self.ways.piece(order, code)
        count = (self.rows if end is None else end) - begin
        return 3 * core + order, page, pl.ds(pl.multiple_of(half * self.rows + begin, 16), count)

    def swap(self, orders, begin=0, end=None):
        ways = self.ways
        for at, (first, last) in enumerate(self.slices):
            for code in range(first, last):
                for order in orders:
                    remote(
                        self.packed.at[self.place(order, code, 1 - ways.core, begin, end)],
                        self.mates.at[order, code, begin:end], self.core_send.at[order, at],
                        self.core_recv.at[order, at], ways.mate,
                    ).start()

    def core_group(self, order, at):
        begin, end = self.slices[at]
        part = self.mates.at[order, begin:end]
        return remote(part, part, self.core_send.at[order, at], self.core_recv.at[order, at], self.ways.mate)

    def add_core(self, at):
        for order in range(3):
            self.core_group(order, at).wait_recv()
            for code in range(*self.slices[at]):
                place = self.place(order, code, self.ways.core)
                self.packed[place] = self.packed[place] + self.mates[order, code]

    def group(self, order, group):
        begin, end = GROUPS[group]
        part = self.got.at[order, begin - 1 : end - 1]
        way = ORDERS[order][step_of(begin)]
        return remote(
            part, part, self.send_sem.at[order, group], self.recv_sem.at[order, group], self.ways.partner(way)
        )

    def send(self, group):
        begin, end = GROUPS[group]
        for code in range(begin, end):
            for order in range(3):
                remote(
                    self.packed.at[self.place(order, code, self.ways.core)], self.got.at[order, code - 1],
                    self.send_sem.at[order, group], self.recv_sem.at[order, group],
                    self.ways.partner(ORDERS[order][step_of(begin)]),
                ).start()

    def receive(self, group):
        begin, end = GROUPS[group]
        base = 1 << (begin.bit_length() - 1)
        for order in range(3):
            self.group(order, group).wait_recv()
            for code in range(begin, end):
                place = self.place(order, code - base, self.ways.core)
                self.packed[place] = self.packed[place] + self.got[order, code - 1]

    def share(self):
        for order in range(3):
            self.group(order, 5).wait_recv()
            place = self.place(order, 0, self.ways.core)
            self.final[self.ways.core, order, self.ways.half] = self.packed[place] + self.got[order, 0]
            self.last_copy(order).start()

    def last_copy(self, order):
        part = self.final.at[self.ways.core, order, self.ways.half]
        return remote(part, part, self.last_send.at[order], self.last_recv.at[order], self.ways.side)

    def end_copy(self, order):
        part = self.final.at[self.ways.core, order]
        return remote(part, part, self.end_send.at[order], self.end_recv.at[order], self.ways.mate)

    def hand_over(self):
        for order in range(3):
            self.last_copy(order).wait_recv()
            self.end_copy(order).start()

    def end(self):
        for order in range(3):
            self.end_copy(order).wait()
            self.last_copy(order).wait_send()
            for at in range(4):
                self.core_group(order, at).wait_send()
            for group in range(len(GROUPS)):
                self.group(order, group).wait_send()


class LateSum:
    def __init__(self, ways, hp, packed, held, got, final, sems):
        self.ways, self.hp = ways, hp
        self.packed, self.held, self.got, self.final = packed, held, got, final
        (self.first_send, self.first_recv, self.send_sem, self.recv_sem, self.last_send, self.last_recv,
         self.end_send, self.end_recv) = sems
        self.rows = held.shape[3]

    def start(self):
        ways, hp = self.ways, self.hp
        for code in range(8, 16):
            for order in range(3):
                page, half = ways.piece(order, code)
                rows = pl.ds(pl.multiple_of(half * self.rows, 16), self.rows)
                remote(
                    self.packed.at[hp, order, page, rows], self.got.at[hp, order, code - 1],
                    self.first_send.at[hp, order], self.first_recv.at[hp, order],
                    ways.partner(ORDERS[order][0]),
                ).start()

    def first(self, order):
        part = self.got.at[self.hp, order, 7:15]
        return remote(
            part, part, self.first_send.at[self.hp, order], self.first_recv.at[self.hp, order],
            self.ways.partner(ORDERS[order][0]),
        )

    def copy(self, order, step):
        begin, end = 8 >> step, 16 >> step
        return remote(
            self.held.at[self.hp, order, begin:end], self.got.at[self.hp, order, begin - 1 : end - 1],
            self.send_sem.at[self.hp, order, step - 1], self.recv_sem.at[self.hp, order, step - 1],
            self.ways.partner(ORDERS[order][step]),
        )

    def advance(self, step):
        ways, hp = self.ways, self.hp
        for order in range(3):
            if step == 0:
                self.first(order).wait_recv()
                for code in (4, 5, 6, 7, 0, 1, 2, 3):
                    page, half = ways.piece(order, code)
                    rows = pl.ds(pl.multiple_of(half * self.rows, 16), self.rows)
                    self.held[hp, order, code] = self.packed[hp, order, page, rows] + self.got[hp, order, code + 7]
                    if code == 7:
                        self.copy(order, 1).start()
            elif step < 3:
                self.copy(order, step).wait_recv()
                count = 8 >> step
                self.held[hp, order, :count] = (
                    self.held[hp, order, :count] + self.got[hp, order, count - 1 : 2 * count - 1]
                )
                self.copy(order, step + 1).start()
            elif step == 3:
                self.copy(order, 3).wait_recv()
                self.final[ways.core, hp, order, ways.half] = self.held[hp, order, 0] + self.got[hp, order, 0]
                self.last_copy(order).start()
            else:
                self.last_copy(order).wait_recv()
                self.end_copy(order).start()

    def last_copy(self, order):
        part = self.final.at[self.ways.core, self.hp, order, self.ways.half]
        return remote(
            part, part, self.last_send.at[self.hp, order], self.last_recv.at[self.hp, order], self.ways.side
        )

    def end_copy(self, order):
        part = self.final.at[self.ways.core, self.hp, order]
        return remote(
            part, part, self.end_send.at[self.hp, order], self.end_recv.at[self.hp, order], self.ways.mate
        )

    def finish(self):
        for order in range(3):
            self.end_copy(order).wait()
            self.last_copy(order).wait_send()
            self.first(order).wait_send()
            for step in (1, 2, 3):
                self.copy(order, step).wait_send()


class SmallSum:
    def __init__(self, ways, value, got, sems):
        self.ways, self.value, self.got = ways, value, got
        self.send_sem, self.recv_sem = sems
        self.to = ways.everyone()

    def copy(self, step):
        return remote(
            self.value.at[step], self.got.at[step], self.send_sem.at[step], self.recv_sem.at[step], self.to[step]
        )

    def start(self):
        self.copy(0).start()

    def advance(self, step):
        self.copy(step).wait_recv()
        self.value[step + 1] = self.value[step] + self.got[step]
        if step < 4:
            self.copy(step + 1).start()

    def finish(self):
        for step in range(5):
            self.copy(step).wait_send()


def norm_of(resid):
    center = resid - jnp.mean(resid, axis=-1, keepdims=True)
    spread = jnp.mean(center * center, axis=-1, keepdims=True)
    inverse = lax.rsqrt(spread + norm_eps)
    return center * inverse, inverse


def norm_back(grad, normed, inverse):
    mean = jnp.mean(grad, axis=-1, keepdims=True)
    along = jnp.mean(grad * normed, axis=-1, keepdims=True)
    return inverse * (grad - mean - normed * along)


def column_sum(values):
    return jnp.sum(values, axis=0, keepdims=True)


def middle_kernel(
    summed, ctx_in, tokens_in, cotangent_in, out_w, up_w, down_w, out_b, gain1, shift1, up_b, down_b, gain2, shift2,
    x_t_in, q_in, k_in, v_in, sc_in, p_in, qkv_w, box_w, *refs
):
    if summed:
        (
            layer_out, dx_out, early_out, down_out, late_out, small_out, tiny_out,
            dresid1, dctx_own, dctx, dx_mate, dx_side,
            own_sem, mate_send, mate_recv, core_send, core_recv, side_send, side_recv,
            packed_down, packed, down_mates, early_mates, down_got, early_got, late_got,
            small_value, small_got, tiny_value, tiny_got, *sems,
        ) = refs
        down_sems, early_sems, late_sems, small_sems, tiny_sems = sems[:8], sems[8:16], sems[16:24], sems[24:26], sems[26:]
        g_rows = small_value.at[0]
    else:
        (
            layer_out, dx_out, packed_down, packed, late_out, g_rows, tiny_out,
            dresid1, dctx_own, dctx, dx_mate, dx_side,
            own_sem, mate_send, mate_recv, core_send, core_recv, side_send, side_recv,
        ) = refs
    ways = Ways()
    core, mate, side = ways.core, ways.mate, ways.side
    greet(ways.everyone() if summed else [mate, side])
    pages, block, width = dctx_own.shape
    half = width // 2
    pairs = half // LANES
    chip, keys = 2 * block, 4 * block
    shard = width // 8
    head = LANES // 2
    scale = 0.125
    chunks = 6
    chunk = up_w.shape[1] // chunks
    up_pieces = chunk // LANES
    if summed:
        down = EarlySum(ways, packed_down, down_mates, down_got, down_out, down_sems)
        early = EarlySum(ways, packed, early_mates, early_got, early_out, early_sems)
        small = SmallSum(ways, small_value, small_got, small_sems)
        tiny = SmallSum(ways, tiny_value, tiny_got, tiny_sems)
        first_chunk = chunks // 2 * (1 - core)
    else:
        first_chunk = 0

    def row(ref):
        return ref[...].reshape(1, -1)

    def of_half(part, which):
        return pl.ds(pl.multiple_of(part * 2 * half + which * half, LANES), half)

    def own_copy(pg):
        return pltpu.make_async_copy(
            dctx_own.at[pg, :, of_half(0, core)], dctx.at[pg, core], own_sem.at[pg]
        )

    def mate_copy(pg):
        return remote(
            dctx_own.at[pg, :, of_half(0, 1 - core)], dctx.at[pg, core], mate_send.at[pg],
            mate_recv.at[pg], mate,
        )

    def send_dctx():
        for pg in range(pages):
            mate_copy(pg).start()
            own_copy(pg).start()

    def feed_step(at):
        if not summed:
            return
        if at == 1:
            down.add_core(0)
            down.send(0)
        elif at == 3:
            down.add_core(1)
            down.send(1)
            down.add_core(2)
            down.add_core(3)

    def back_step(at):
        if not summed:
            return
        if at == 0:
            down.receive(0)
            down.send(2)
            down.send(3)
            early.add_core(0)
            early.send(0)
            early.add_core(1)
            early.send(1)
            early.add_core(2)
            early.add_core(3)
        elif at == 1:
            down.receive(1)
        elif at == 2:
            small.advance(0)
        elif at == 3:
            down.receive(2)
            down.receive(3)
            down.send(4)
        elif at == 4:
            small.advance(1)
        elif at == 5:
            early.receive(0)
            early.send(2)
            early.send(3)
        elif at == 6:
            down.receive(4)
            down.send(5)
            early.receive(1)
        elif at == 7:
            small.advance(2)
            early.receive(2)
            early.receive(3)
            early.send(4)
        elif at == 8:
            small.advance(3)
            down.share()
            early.receive(4)
            early.send(5)

    def feed_phase(
        ctx, tokens, cotangent, output, w_out, w_up, w_down, act, slope, norm1, inverse1, hidden, hidden_t, grow,
        staged, up_rows, in_sem, w_sem, up_sem, down_sem,
    ):
        out_load = pltpu.make_async_copy(out_w, w_out, w_sem)
        out_load.start()
        rows_in = [
            pltpu.make_async_copy(src, dst, in_sem.at[at])
            for at, (src, dst) in enumerate(((ctx_in, ctx), (tokens_in, tokens), (cotangent_in, cotangent)))
        ]
        for copy in rows_in:
            copy.start()

        def up_load(j):
            return pltpu.make_async_copy(
                up_w.at[:, pl.ds(pl.multiple_of(j * chunk, LANES), chunk)], w_up.at[j], up_sem.at[j]
            )

        def down_load(j):
            return pltpu.make_async_copy(
                down_w.at[pl.ds(pl.multiple_of(j * chunk, LANES), chunk)], w_down.at[j], down_sem.at[j]
            )

        for j in range(chunks):
            up_load(j).start()
            down_load(j).start()
        g_rows[...] = jnp.zeros_like(g_rows)
        for j in range(chunks):
            up_rows[j : j + 1] = up_b[j * chunk : (j + 1) * chunk].reshape(1, chunk)
        out_load.wait()
        for copy in rows_in:
            copy.wait()
        resid = tokens[...].astype(f32) + dot(ctx[...], w_out[...]) + row(out_b)
        normed, inverse = norm_of(resid)
        norm1[...] = normed
        inverse1[...] = jnp.broadcast_to(inverse, inverse1.shape)
        first = normed * row(gain1) + row(shift1)
        hidden[...] = first.astype(low)
        hidden_t[...] = first.astype(low).T
        grow[...] = first + row(down_b)

        @pl.loop(0, chunks)
        def _(j):
            up_load(j).wait()
            upper = dot(hidden[...], w_up[j]) + up_rows[pl.ds(j, 1)]
            cdf = 0.5 + 0.5 * lax.erf(upper * 0.7071067811865476)
            act_low = (upper * cdf).astype(low)
            act[j] = act_low
            slope[j] = (cdf + upper * (jnp.exp(upper * upper * -0.5) * 0.3989422804014327)).astype(low)
            down_load(j).wait()
            grow[...] += dot(act_low, w_down[j])

        normed2, inverse2 = norm_of(grow[...])
        output[...] = (normed2 * row(gain2) + row(shift2)).astype(low)
        output_copy = pltpu.make_async_copy(output, layer_out, w_sem)
        output_copy.start()
        cot = cotangent[...].astype(f32)
        g_rows[0:1] = column_sum(cot * normed2)
        g_rows[1:2] = column_sum(cot)
        dresid2 = norm_back(cot * row(gain2), normed2, inverse2)
        dffn = dresid2.astype(low)
        g_rows[2:3] = column_sum(dffn.astype(f32))
        grow[...] = dresid2
        staged[...] = dffn

        @pl.loop(0, chunks)
        def _(j):
            grad_down = dot_tn(act[j], staged[...]).astype(low)
            for piece in range(up_pieces):
                at = j * up_pieces + piece
                per = up_pieces * chunks // 8
                rows = pl.ds(pl.multiple_of((at % per) * LANES, LANES), LANES)
                for column in range(6):
                    packed_down[column, at // per, rows] = grad_down[
                        piece * LANES : (piece + 1) * LANES, column * LANES : (column + 1) * LANES
                    ]

        if summed:
            down.swap(range(3))
        up_end = up_pieces * shard // 2
        per_half = up_end + shard // 2

        @pl.loop(0, chunks)
        def _(step):
            for at in range(chunks):

                @pl.when(step == at)
                def _(at=at):
                    feed_step(at)

            j = lax.rem(step + first_chunk, chunks)
            dffn = staged[...]
            dupper = (dot_nt(dffn, w_down[j]) * slope[j].astype(f32)).astype(low)
            g_rows[pl.ds(8 + j, 1), :chunk] = column_sum(dupper.astype(f32))
            grow[...] += dot_nt(dupper, w_up[j])
            grad_up = dot(hidden_t[...], dupper).astype(low)
            for piece in range(up_pieces):
                part = grad_up[:, piece * LANES : (piece + 1) * LANES].reshape(8, shard, LANES)
                at = piece // (up_pieces // 2) * per_half + piece % (up_pieces // 2) * shard
                packed[j, :, at : at + shard] = part
            if summed:

                for order in range(3):

                    @pl.when(step == order)
                    def _(order=order):
                        early.swap([order], 0, up_end)

        dhidden = grow[...]
        normed = norm1[...]
        g_rows[3:4] = column_sum(dhidden * normed)
        g_rows[4:5] = column_sum(dhidden)
        back = norm_back(dhidden * row(gain1), normed, inverse1[:, :1])
        dresid1[...] = back.reshape(dresid1.shape)
        dattn = back.astype(low)
        g_rows[5:6] = column_sum(dattn.astype(f32))
        dctx_own[...] = dot_nt(dattn, w_out[...]).astype(low).reshape(dctx_own.shape)
        send_dctx()
        grad_out = dot_tn(ctx[...], dattn).astype(low)
        for column in range(6):
            part = grad_out[:, column * LANES : (column + 1) * LANES].reshape(8, shard, LANES)
            for half in range(2):
                at = half * per_half + up_end
                packed[column, :, at : at + shard // 2] = part[:, half * shard // 2 : (half + 1) * shard // 2]
        if summed:
            small.start()
            early.swap(range(3), up_end, per_half)
        output_copy.wait()

    def back_phase(
        x_t, q, k, v, sc, probs, dq, dkv, w_c, dx, box_t, g_box, g_bias, late_packed, late_held, in_sem, p_sem, w_sem
    ):
        def loads(pg):
            names = ((q_in, q), (k_in, k), (v_in, v), (sc_in, sc))
            copies = [
                pltpu.make_async_copy(src.at[pg], dst.at[pg], in_sem.at[pg, at])
                for at, (src, dst) in enumerate(names)
            ]
            at = pl.ds(pl.multiple_of(pg * keys, LANES), keys)
            copies.append(pltpu.make_async_copy(x_t_in.at[pg], x_t.at[:, at], in_sem.at[pg, 4]))
            return copies

        def p_load(hp, pg):
            return pltpu.make_async_copy(p_in.at[pg, hp], probs.at[pg, hp], p_sem.at[pg, hp])

        w_loads = [
            pltpu.make_async_copy(qkv_w.at[:, of_half(part, core)], w_c.at[part], w_sem.at[part])
            for part in range(3)
        ]
        for pg in range(pages):
            for copy in loads(pg):
                copy.start()
            for hp in range(pairs):
                p_load(hp, pg).start()
        for copy in w_loads:
            copy.start()

        def late(hp):
            return LateSum(ways, hp, late_packed, late_held, late_got, late_out, late_sems)

        for e in range(2):
            box_t[e] = jnp.zeros_like(box_t[e])
            box_t[e, :, e * head : (e + 1) * head] = box_w[...].astype(f32).T.astype(low)
        g_box[...] = jnp.zeros_like(g_box)

        def take(pg):
            for copy in loads(pg):
                copy.wait()
            own_copy(pg).wait()
            mate_copy(pg).wait_recv()

        def one_pair(pg, hp):
            lanes = pl.ds(pl.multiple_of(hp * LANES, LANES), LANES)
            p_load(hp, pg).wait()
            both = sc[pg]
            cosine2, sine2 = turned(both)
            flat = both.T
            sine_t, cosine_t = flat[:head, :chip], flat[head:, :chip]
            basis = both.astype(low)
            basis_t = flat.astype(low)
            q_pair, k_pair, v_pair = q[pg, hp], k[pg, hp], v[pg, hp]
            q_t, k_t = q_pair.T, k_pair.T
            dc = dctx[pg, :, :, lanes].reshape(chip, LANES)
            left = lane_halves((chip, LANES))
            zero = jnp.zeros_like(dc)
            dk, dv, dqs = 0.0, 0.0, []
            for e in range(2):
                mine = left if e == 0 else jnp.logical_not(left)
                own_rows = slice(e * head, (e + 1) * head)
                p = probs[pg, hp, e]
                dc_own = jnp.where(mine, dc, zero)
                q_own = jnp.where(mine, q_pair, zero)
                dp = dot_nt(v_pair, dc_own)
                p_wide = p.astype(f32)
                delta = jnp.sum(p_wide * dp, axis=0, keepdims=True)
                ds = (p_wide * (dp - delta)).astype(low)
                dv = dv + dot(p, dc_own)
                dk_feat = dot(ds, jnp.concatenate([q_own, basis[:chip]], 1)) * scale
                dq_feat = dot(jnp.concatenate([k_t[own_rows], basis_t], 0), ds) * scale
                dk_proj = rotate_key(dk_feat[:, LANES:], cosine2, sine2).astype(low)
                a, b = dq_feat[head : 2 * head], dq_feat[2 * head :]
                dq_proj = jnp.concatenate(
                    [a * cosine_t - b * sine_t, a * sine_t + b * cosine_t], 0
                ).astype(low)
                dk = dk + dk_feat[:, :LANES] + dot(dk_proj, box_t[e])
                dqs.append(dq_feat[:head] + dot(box_w[...], dq_proj))
                g_box[...] += dot(k_t[own_rows], dk_proj) + dot_nt(q_t[own_rows], dq_proj)
            at = pl.ds(pl.multiple_of(pg * keys, LANES), keys)
            at_q = pl.ds(pl.multiple_of(pg * chip, LANES), chip)
            dq[hp, at_q] = jnp.concatenate(dqs, 0).T.astype(low)
            dkv[hp, at, :LANES] = dk.astype(low)
            dkv[hp, at, LANES:] = dv.astype(low)

        def pair_grads(hp):
            dkv_all = dkv[hp]
            dq_all = dq[hp]
            g_kv = column_sum(dkv_all.astype(f32))
            g_bias[pl.ds(hp, 1)] = column_sum(dq_all.astype(f32))
            g_bias[pl.ds(hp + pairs, 1)] = g_kv[:, :LANES]
            g_bias[pl.ds(hp + 2 * pairs, 1)] = g_kv[:, LANES:]
            grad = dot(x_t[...], dkv_all).astype(low)
            x_q = jnp.concatenate([x_t[:, pg * keys : pg * keys + chip] for pg in range(pages)], 1)
            grad_q = dot(x_q, dq_all).astype(low)
            late_packed[hp, 0] = grad_q.reshape(8, shard, LANES)
            late_packed[hp, 1] = grad[:, :LANES].reshape(8, shard, LANES)
            late_packed[hp, 2] = grad[:, LANES:].reshape(8, shard, LANES)

        def core_copy(pg, at):
            return remote(
                dx.at[pg, at, 1 - core], dx_mate.at[pg, at], core_send.at[pg, at], core_recv.at[pg, at],
                mate,
            )

        def side_copy(pg):
            return remote(dx.at[pg, 1, core], dx_side.at[pg], side_send.at[pg], side_recv.at[pg], side)

        def input_part(pg):
            for at in (1, 0):
                rows = pl.ds(pl.multiple_of(pg * keys + at * chip, LANES), chip)
                dks = jnp.concatenate([dkv[hp, rows, :LANES] for hp in range(pairs)], 1)
                dvs = jnp.concatenate([dkv[hp, rows, LANES:] for hp in range(pairs)], 1)
                total = dot_nt(dks, w_c[1]) + dot_nt(dvs, w_c[2])
                if at == 0:
                    rows_q = pl.ds(pl.multiple_of(pg * chip, LANES), chip)
                    dqs = jnp.concatenate([dq[hp, rows_q] for hp in range(pairs)], 1)
                    total = total + dot_nt(dqs, w_c[0])
                dx[pg, at] = total.astype(low).reshape(2, block, width)
                core_copy(pg, at).start()

        def pass_input(pg):
            core_copy(pg, 1).wait_recv()
            dx[pg, 1, core] = dx[pg, 1, core] + dx_mate[pg, 1]
            side_copy(pg).start()

        def bias_rows():
            for part in range(3):
                for which in range(2):
                    own = jnp.where(core == which, 1.0, 0.0)
                    for hp in range(pairs):
                        at = part * pairs + hp
                        yield 64 + (2 * part + which) * pairs + hp, g_bias[at : at + 1] * own

        @pl.loop(0, pages - 1)
        def _(pg):
            take(pg)

            @pl.when(pg > 0)
            def _():
                pass_input(pg - 1)

            @pl.loop(0, pairs)
            def _(hp):
                for at in range(pairs * (pages - 1)):

                    @pl.when(pg * pairs + hp == at)
                    def _(at=at):
                        back_step(at)

                one_pair(pg, hp)

            @pl.when(pg == 0)
            def _():
                for copy in w_loads:
                    copy.wait()

            input_part(pg)

        last = pages - 1
        take(last)
        pass_input(last - 1)

        @pl.loop(0, pairs)
        def _(hp):
            for at in range(pairs):

                @pl.when(hp == at)
                def _(at=at):
                    back_step(pairs * last + at)

            one_pair(last, hp)
            pair_grads(hp)
            if summed:
                late(hp).start()

                @pl.when(hp > 0)
                def _():
                    late(hp - 1).advance(0)

                @pl.when(hp == 2)
                def _():
                    late(0).advance(1)

        if summed:
            tiny_value[0, : 8 * 8] = g_box[...]
            tiny_value[0, 64:] = jnp.zeros((24, LANES), f32)
            for at, row in bias_rows():
                tiny_value[0, at : at + 1] = row
            tiny.start()
        input_part(last)
        if summed:
            pass_input(last)
            tiny.advance(0)
            late(2).advance(0)
            late(1).advance(1)
            down.hand_over()
            early.share()
            late(0).advance(2)
            small.advance(4)
            tiny.advance(1)
            late(2).advance(1)
            late(1).advance(2)
            late(0).advance(3)
            tiny.advance(2)
            late(2).advance(2)
            late(1).advance(3)
            late(0).advance(4)
            early.hand_over()
            tiny.advance(3)
            late(2).advance(3)
            late(1).advance(4)
            tiny.advance(4)
            late(2).advance(4)
        else:
            pass_input(last)

        for pg in range(pages):
            core_copy(pg, 0).wait_recv()
            side_copy(pg).wait_recv()
            total = dx[pg, 0, core].astype(f32) + dx_mate[pg, 0].astype(f32) + dx_side[pg].astype(f32)
            dx_out[pg] = (total + dresid1[pg]).astype(low)
            for at in range(2):
                core_copy(pg, at).wait_send()
            side_copy(pg).wait_send()
            mate_copy(pg).wait_send()
        if summed:
            small_out[...] = small_value[5]
            tiny_out[...] = tiny_value[5]
            early.end()
            down.end()
            for hp in range(pairs):
                late(hp).finish()
            small.finish()
            tiny.finish()
        else:
            late_out[...] = late_packed[...]
            tiny_out[:64] = g_box[...]
            tiny_out[64:] = jnp.zeros((24, LANES), f32)
            for at, row in bias_rows():
                tiny_out[at : at + 1] = row

    vmem, dma = pltpu.VMEM, pltpu.SemaphoreType.DMA
    rows = pages * block
    pl.run_scoped(
        feed_phase,
        vmem((rows, width), low),
        vmem((rows, width), low),
        vmem((rows, width), low),
        vmem((rows, width), low),
        vmem((width, width), low),
        vmem((chunks, width, chunk), low),
        vmem((chunks, chunk, width), low),
        vmem((chunks, rows, chunk), low),
        vmem((chunks, rows, chunk), low),
        vmem((rows, width), f32),
        vmem((rows, LANES), f32),
        vmem((rows, width), low),
        vmem((width, rows), low),
        vmem((rows, width), f32),
        vmem((rows, width), low),
        vmem((chunks, chunk), f32),
        dma((3,)), dma, dma((chunks,)), dma((chunks,)),
    )
    late_shape = (pairs, 3, 8, shard, LANES)
    pl.run_scoped(
        back_phase,
        vmem((width, pages * keys), low),
        vmem((pages, pairs, chip, LANES), low),
        vmem((pages, pairs, keys, LANES), low),
        vmem((pages, pairs, keys, LANES), low),
        vmem((pages, keys, LANES), f32),
        vmem((pages, pairs, 2, keys, chip), low),
        vmem((pairs, pages * chip, LANES), low),
        vmem((pairs, pages * keys, 2 * LANES), low),
        vmem((3, width, half), low),
        vmem((pages, 2, 2, block, width), low),
        vmem((2, LANES, LANES), low),
        vmem(box_w.shape, f32),
        vmem((3 * pairs, LANES), f32),
        vmem(late_shape, low),
        vmem((pairs, 3, 8, shard // 2, LANES), low),
        dma((pages, 5)), dma((pages, pairs)), dma((3,)),
    )


def middle(rows_in, weights, vectors, saved, qkv_w, box_w, summed):
    pages, block, width = rows_in[0].shape[0] // 128, 128, rows_in[0].shape[1]
    rows = pages * block
    half = width // 2
    pairs = half // LANES
    shard = width // 8
    hidden_width = weights[1].shape[1]
    down_rows = hidden_width // 8
    packed_rows = down_rows + shard
    tiny_rows = 88
    small = (16, width)
    struct = jax.ShapeDtypeStruct
    vmem, dma = pltpu.VMEM, pltpu.SemaphoreType.DMA
    outs = [struct((rows, width), low), struct((pages, block, width), low)]
    scratch = [
        vmem((pages, block, width), f32),
        vmem((pages, block, width), low),
        vmem((pages, 2, block, half), low),
        vmem((pages, 2, block, width), low),
        vmem((pages, block, width), low),
        dma((pages,)), dma((pages,)), dma((pages,)), dma((pages, 2)), dma((pages, 2)), dma((pages,)), dma((pages,)),
    ]
    if summed:
        outs += [
            struct((2, 3, 2, packed_rows // 2, LANES), low),
            struct((2, 3, 2, down_rows // 2, LANES), low),
            struct((2, pairs, 3, 2, shard // 2, LANES), low),
            struct(small, f32),
            struct((tiny_rows, LANES), f32),
        ]
        scratch += [
            vmem((6, 8, down_rows, LANES), low),
            vmem((6, 8, packed_rows, LANES), low),
            vmem((3, 16, down_rows // 2, LANES), low),
            vmem((3, 16, packed_rows // 2, LANES), low),
            vmem((3, 15, down_rows // 2, LANES), low),
            vmem((3, 15, packed_rows // 2, LANES), low),
            vmem((pairs, 3, 15, shard // 2, LANES), low),
            vmem((6,) + small, f32),
            vmem((5,) + small, f32),
            vmem((6, tiny_rows, LANES), f32),
            vmem((5, tiny_rows, LANES), f32),
        ]
        groups = len(GROUPS)
        scratch += ([dma((3, 4))] * 2 + [dma((3, groups))] * 2 + [dma((3,))] * 4) * 2
        scratch += [dma((pairs, 3))] * 2 + [dma((pairs, 3, 3))] * 2 + [dma((pairs, 3))] * 4
        scratch += [dma((5,))] * 4
    else:
        outs += [
            struct((6, 8, down_rows, LANES), low),
            struct((6, 8, packed_rows, LANES), low),
            struct((pairs, 3, 8, shard, LANES), low),
            struct(small, f32),
            struct((tiny_rows, LANES), f32),
        ]
    return pl.pallas_call(
        functools.partial(middle_kernel, summed),
        out_shape=tuple(outs),
        in_specs=[any_spec()] * 6 + [vmem_spec()] * 7 + [any_spec()] * 7 + [vmem_spec()],
        out_specs=(any_spec(),) + (vmem_spec(),) * 6,
        scratch_shapes=scratch,
        compiler_params=pltpu.CompilerParams(
            collective_id=2, has_side_effects=True, vmem_limit_bytes=63 * 2**20
        ),
        name="middle",
    )(*rows_in, *weights, *vectors, *saved, qkv_w, box_w)


def finish_kernel(
    early_in, rest_in, late_in, small_in, tiny_in, dx_in, layer_in,
    up, down, out, qkv, qkv_b, box, out_b, gain1, shift1, up_b, down_b, gain2, shift2, input_grad, layer_out,
    early, rest, late, small, tiny, sems,
):
    page = lax.axis_index("page")
    shard = out.shape[0]
    pieces = up.shape[1] // (6 * LANES)
    pairs = (
        (early_in, early), (rest_in, rest), (late_in, late), (small_in, small), (tiny_in, tiny), (dx_in, input_grad),
        (layer_in, layer_out),
    )
    copies = [pltpu.make_async_copy(src, dst, sems.at[at]) for at, (src, dst) in enumerate(pairs)]
    for copy in copies:
        copy.start()
    for copy in copies:
        copy.wait()
    for which in range(2):
        for order in range(3):
            column = which * 3 + order
            rows = early[which, order].astype(f32)
            at = column * LANES
            per = pieces // 2
            for half in range(2):
                for piece in range(per):
                    up_at = (column * pieces + half * per + piece) * LANES
                    up[:, up_at : up_at + LANES] = rows[half, piece * shard : (piece + 1) * shard]
                out[half * shard // 2 : (half + 1) * shard // 2, at : at + LANES] = rows[half, per * shard :]
            down[:, at : at + LANES] = rest[which, order].astype(f32).reshape(-1, LANES)
            for part in range(3):
                at = (part * 6 + column) * LANES
                qkv[:, at : at + LANES] = late[which, order, part].astype(f32).reshape(shard, LANES)
    rows = pltpu.roll(small[:8], lax.rem(8 * shard - page * shard, 8 * shard), 1)
    for at, ref in enumerate((gain2, shift2, down_b, gain1, shift1, out_b)):
        ref[...] = rows[at, :shard]
    flat = jnp.concatenate([small[8 + at : 9 + at, : pieces * LANES] for at in range(6)], 1)
    every = flat.shape[1]
    flat = pltpu.roll(flat, lax.rem(every - page * up_b.shape[0], every), 1)
    up_b[...] = flat[0, : up_b.shape[0]]
    box[...] = tiny[pl.ds(pl.multiple_of(page * 8, 8), 8)]
    count = qkv_b.shape[0]
    first = page * count
    parts = [tiny[pl.ds(64 + first // LANES + piece, 1)] for piece in range(4)]
    rest = lax.rem(first, LANES)
    row = pltpu.roll(jnp.concatenate(parts, 1), lax.rem(4 * LANES - rest, 4 * LANES), 1)
    qkv_b[...] = row[0, :count]


def finish(early, rest, late, small, tiny, dx, layer):
    struct = jax.ShapeDtypeStruct
    shapes = (
        (96, 3072), (384, 768), (96, 768), (96, 2304), (288,), (8, LANES), (96,), (96,), (96,), (384,), (96,), (96,), (96,),
    )
    operands = (early, rest, late, small, tiny, dx, layer)
    return pl.pallas_call(
        finish_kernel,
        out_shape=tuple(struct(shape, f32) for shape in shapes) + (struct(dx.shape, low), struct(layer.shape, low)),
        in_specs=[any_spec()] * 7,
        out_specs=(vmem_spec(),) * 15,
        scratch_shapes=[pltpu.VMEM(operand.shape, operand.dtype) for operand in operands[:5]]
        + [pltpu.SemaphoreType.DMA((7,))],
        compiler_params=pltpu.CompilerParams(vmem_limit_bytes=63 * 2**20),
        name="finish",
    )(*operands)


def reduce_by_collectives(packed, packed_down, packed_qkv, vectors):
    core = lax.axis_index("blk") % 2
    packed = packed.reshape(6, 8, 2, 240, LANES)
    up = packed[:, :, :, :192].reshape(6, 8, 4, 96, LANES).transpose(1, 3, 0, 2, 4).reshape(768, 3072)
    down = packed_down.transpose(1, 2, 0, 3).reshape(3072, 768)
    out = packed[:, :, :, 192:].transpose(1, 2, 3, 0, 4).reshape(768, 768)
    own = packed_qkv.transpose(2, 3, 1, 0, 4).reshape(768, 3, 384)
    qkv = jnp.zeros((768, 3, 2, 384), low)
    qkv = lax.dynamic_update_slice(qkv, own[:, :, None], (0, 0, core, 0)).reshape(768, 2304)
    grads = jax.tree.map(lambda g: g.astype(f32), (qkv, out, up, down, *vectors))
    page_sums = tuple(
        lax.psum_scatter(grad, "page", scatter_dimension=0, tiled=True) for grad in grads
    )
    return jax.tree.map(
        lambda part: part.astype(f32), lax.psum(jax.tree.map(lambda g: g.astype(low), page_sums), "blk")
    )


def local(
    tokens, lengths, boxes, qkv_weight, qkv_bias, box_weight, out_weight, out_bias, norm1_gain,
    norm1_bias, up_weight, up_bias, down_weight, down_bias, norm2_gain, norm2_bias, cotangent,
):
    pages, block, width = tokens.shape
    rows = pages * block
    *saved, ctx = attend(tokens, boxes, lengths, qkv_weight, qkv_bias, box_weight)
    summed = lax.axis_size("page") == 8
    output, input_grad, *parts = middle(
        [part.reshape(rows, width) for part in (ctx, tokens, cotangent)], (out_weight, up_weight, down_weight),
        (out_bias, norm1_gain, norm1_bias, up_bias, down_bias, norm2_gain, norm2_bias), saved,
        qkv_weight, box_weight, summed,
    )
    if summed:
        early, rest, late, small, tiny = parts
        (
            up_w, down_w, out_w, qkv_w, qkv_b, box, out_b, gain1, shift1, up_b, down_b, gain2, shift2, input_grad,
            output,
        ) = finish(early, rest, late, small, tiny, input_grad, output)
        box = box.reshape(-1)
    else:
        down, packed, packed_qkv, small, tiny = parts
        vectors = (
            tiny[64:82].reshape(-1), tiny[:64].reshape(-1), small[5], small[3], small[4],
            small[8:14, :512].reshape(-1), small[2], small[0], small[1],
        )
        (
            qkv_w, out_w, up_w, down_w, qkv_b, box, out_b, gain1, shift1, up_b, down_b, gain2, shift2,
        ) = reduce_by_collectives(packed, down, packed_qkv, vectors)
    return (
        output.reshape(pages, block, width), input_grad, qkv_w, qkv_b, box, out_w, out_b, gain1, shift1, up_w, up_b, down_w, down_b, gain2, shift2,
    )


def solution(mesh):
    return jax.shard_map(
        local,
        mesh=mesh,
        in_specs=(
            P("page", "blk", None),
            P("page"),
            P("page", "blk", None),
            P(),
            P(),
            P(),
            P(),
            P(),
            P(),
            P(),
            P(),
            P(),
            P(),
            P(),
            P(),
            P(),
            P("page", "blk", None),
        ),
        out_specs=(
            P("page", "blk", None),
            P("page", "blk", None),
            P("page", None),
            P("page"),
            P("page"),
            P("page", None),
            P("page"),
            P("page"),
            P("page"),
            P("page", None),
            P("page"),
            P("page", None),
            P("page"),
            P("page"),
            P("page"),
        ),
        check_vma=False,
    )
```

time: 161 us -> 143 us (0.89)
  Pallas kernels: 157 us -> 139 us
    pallas_call x3 -> x2, Pallas kernels: 153 us -> 135 us  [the longest x1 103 us: middle(): pl.pallas_call(functools.partial(middle_kernel, summed), out_shape=tuple(...]
where the time goes in v3:
time: 143 us; the launch traced here: 141 us
  Pallas kernels  139 us (97%)
    pallas_call x1, Pallas kernels, middle(): pl.pallas_call(functools.partial(middle_kernel, summed), out_shape=tuple(...  103 us
    pallas_call x1, Pallas kernels, attend(): pl.pallas_call(attend_kernel, out_shape=(struct((pages, width, keys), low...  32.3 us
    pallas_call x1, Pallas kernels, finish(): pl.pallas_call(finish_kernel, out_shape=tuple((struct(shape, f32) for sha...  4.1 us

profile of v3, /device:TPU:9, one launch (start us, length us, event | category | flops | bytes accessed | tf_op | source)
XLA Modules:
  0.0 141.5 jit_solution(17301700423107678874)
XLA Ops:
  0.6 1.3 convert_bitcast_fusion.boxes
  1.9 32.3 %attend.1 = (bf16[3,768,512]{2,1,0:T(8,128)(2,1)}, bf16[3,3,256,128]{3,2,1,0:T(8,128)(2,1)}, bf16[3,3,512,128]{3,2,1,0:T(8,128)(2,1)}, bf16[3,3,512,128]{3,2,1,0...) custom-call(bf16[3,128,768]{2,1,0:T(8,128)(2,1)} %tokens.1, ...), custom_call_target="tpu_custom_call" | custom-call | tf_op jit(solution)/shard_map/attend/pallas_call | solution.py:267
  34.3 102.9 %middle.1 = (bf16[384,768]{1,0:T(8,128)(2,1)}, bf16[3,128,768]{2,1,0:T(8,128)(2,1)}, bf16[2,3,2,240,128]{4,3,2,1,0:T(8,128)(2,1)}, bf16[2,3,2,192,128]{4,3,2,1,0...) custom-call(bf16[384,768]{1,0:T(8,128)(2,1)} %bitcast.9, ...), custom_call_target="tpu_custom_call" | custom-call | tf_op jit(solution)/shard_map/middle/pallas_call | solution.py:1149
  137.2 4.1 %finish.1 = (f32[96,3072]{1,0:T(8,128)}, f32[384,768]{1,0:T(8,128)}, f32[96,768]{1,0:T(8,128)}, f32[96,2304]{1,0:T(8,128)}, f32[288]{0:T(512)}, /*index=5*/f32[8...) custom-call(bf16[2,3,2,240,128]{4,3,2,1,0:T(8,128)(2,1)} %get-tuple-, ...), custom_call_target="tpu_custom_call" | custom-call | tf_op jit(solution)/shard_map/finish/pallas_call | solution.py:1216

commit v4 on v3

v4 whole, which is shorter than its diff:
```python
import functools

import jax
import jax.numpy as jnp
import numpy as np
from jax import lax
from jax.experimental import pallas as pl
from jax.experimental.pallas import tpu as pltpu
from jax.sharding import PartitionSpec as P

norm_eps = 1e-12
MESH = pl.DeviceIdType.MESH
LANES = 128
low = jnp.bfloat16
f32 = jnp.float32


def core_of(blk):
    return blk + 1 - 2 * (blk % 2)


def side_of(blk):
    return (blk + 2) % 4


def greet(others):
    barrier = pltpu.get_barrier_semaphore()
    for other in others:
        pl.semaphore_signal(barrier, inc=1, device_id=other, device_id_type=MESH)
    pl.semaphore_wait(barrier, len(others))


def remote(src, dst, send_sem, recv_sem, to):
    return pltpu.make_async_remote_copy(
        src_ref=src, dst_ref=dst, send_sem=send_sem, recv_sem=recv_sem, device_id=to,
        device_id_type=MESH,
    )


def dot(a, b):
    return jnp.dot(a, b, preferred_element_type=f32)


def dot_nt(a, b):
    return lax.dot_general(a, b, (((1,), (1,)), ((), ())), preferred_element_type=f32)


def dot_tn(a, b):
    return lax.dot_general(a, b, (((0,), (0,)), ((), ())), preferred_element_type=f32)


def sin_cos(theta):
    turns = jnp.floor(theta * 0.6366197723675814 + 0.5)
    rest = theta - turns * 1.5703125
    rest = rest - turns * 4.837512969970703125e-4
    rest = rest - turns * 7.54978995489188216e-8
    square = rest * rest
    sine = ((-1.9515295891e-4 * square + 8.3321608736e-3) * square - 1.6666654611e-1) * square
    sine = sine * rest + rest
    cosine = (2.443315711809948e-5 * square - 1.388731625493765e-3) * square + 4.166664568298827e-2
    cosine = cosine * square * square - 0.5 * square + 1.0
    quarter = turns.astype(jnp.int32)
    odd = (quarter & 1) == 1
    sine_at = jnp.where(odd, cosine, sine)
    cosine_at = jnp.where(odd, sine, cosine)
    sine_at = jnp.where((quarter & 2) == 2, -sine_at, sine_at)
    cosine_at = jnp.where(((quarter + 1) & 2) == 2, -cosine_at, cosine_at)
    return sine_at, cosine_at


def lane_halves(shape):
    return lax.broadcasted_iota(jnp.int32, shape, 1) < LANES // 2


def turned(both):
    swapped = pltpu.roll(both, LANES // 2, 1)
    left = lane_halves(both.shape)
    return jnp.where(left, -swapped, both), jnp.where(left, both, swapped)


def rotate_key(proj, cosine2, sine2):
    return proj * cosine2 + pltpu.roll(proj, LANES // 2, 1) * sine2


def any_spec():
    return pl.BlockSpec(memory_space=pl.ANY)


def vmem_spec():
    return pl.BlockSpec(memory_space=pltpu.VMEM)


GROUPS = ((12, 16), (8, 12), (6, 8), (4, 6), (2, 4), (1, 2))


def flip(page, way):
    x, z = page % 2, page // 2
    if way == "x":
        return z * 2 + (1 - x)
    if way == "a":
        return (z + 1 - 2 * (z % 2)) * 2 + x
    return ((z + 2) % 4) * 2 + x


DOWN_ORDERS = ("xyam", "axym", "yaxm")
EARLY_ORDERS = ("xaym", "axym", "yxam")
LATE_ORDERS = ("xyam", "xyam", "axym")
PLAN = {
    "f2": ("Dc0", "Ds0", "Dc1", "Ds1"),
    "f3": ("Dc2", "Dc3"),
    "fe": ("Dr0", "Ds3", "Ds2"),
    "fw": ("Ss",),
    "b0": ("Ec2", "Ec3", "Ec0", "Es0", "Ec1", "Es1", "Dr3", "Dr1"),
    "b1": ("Dr2",),
    "b2": ("Sa0",),
    "b4": ("Er0", "Es2", "Ds4", "Es3", "X0p"),
    "q1": ("Sa1", "Er1"),
    "g0": ("L0s", "X1p"),
    "g1": ("Er2", "X0fin", "Es4"),
    "p2": ("Dr4", "Ds5", "Sa2", "X1fin", "Ts"),
    "tail": ("Er3", "L1s", "X2p", "Er4", "L2s", "Es5", "Sa3", "L0a0", "Sa4", "Ta0", "Dsh", "X2fin", "L1a0", "Dho", "L2a0", "L0a1", "Dfin", "L1a1", "Ta1", "L2a1", "Esh", "L0a2", "L1a2", "L2a2", "Ta2", "L0a3", "Eho", "L1a3", "Ta3", "Efin", "L2a3", "Ta4", "L0fin", "L1fin", "L2fin"),
}


class Ways:
    def __init__(self):
        self.page, self.blk = lax.axis_index("page"), lax.axis_index("blk")
        self.core, self.half = self.blk % 2, self.blk // 2
        self.mate, self.side = (self.page, core_of(self.blk)), (self.page, side_of(self.blk))

    def partner(self, ways):
        page, blk = self.page, self.blk
        for way in ways:
            if way == "y":
                blk = side_of(blk)
            elif way == "c":
                blk = core_of(blk)
            else:
                page = flip(page, way)
        return page, blk

    def piece(self, order, code):
        page, half = self.page, self.half
        for place, way in enumerate(order):
            if code >> (3 - place) & 1:
                if way == "y":
                    half = 1 - half
                else:
                    page = flip(page, way)
        return page, half

    def everyone(self):
        return [self.partner(ways) for ways in ("x", "a", "m", "y", "c", "yc")]


def step_of(code):
    return 4 - code.bit_length()


class EarlySum:
    def __init__(self, ways, orders, packed, mates, got, final, sems):
        self.ways, self.orders = ways, orders
        self.packed, self.mates, self.got, self.final = packed, mates, got, final
        (self.core_send, self.core_recv, self.send_sem, self.recv_sem, self.last_send, self.last_recv,
         self.end_send, self.end_recv) = sems
        self.rows = packed.shape[2] // 2

    slices = ((12, 16), (8, 12), (4, 8), (0, 4))

    def place(self, order, code, core, begin=0, end=None):
        page, half = self.ways.piece(self.orders[order], code)
        count = (self.rows if end is None else end) - begin
        return 3 * core + order, page, pl.ds(pl.multiple_of(half * self.rows + begin, 16), count)

    def swap(self, orders, begin=0, end=None):
        ways = self.ways
        for at, (first, last) in enumerate(self.slices):
            for code in range(first, last):
                for order in orders:
                    remote(
                        self.packed.at[self.place(order, code, 1 - ways.core, begin, end)],
                        self.mates.at[order, code, begin:end], self.core_send.at[order, at],
                        self.core_recv.at[order, at], ways.mate,
                    ).start()

    def core_group(self, order, at):
        begin, end = self.slices[at]
        part = self.mates.at[order, begin:end]
        return remote(part, part, self.core_send.at[order, at], self.core_recv.at[order, at], self.ways.mate)

    def add_core(self, at):
        for order in range(3):
            self.core_group(order, at).wait_recv()
            for code in range(*self.slices[at]):
                place = self.place(order, code, self.ways.core)
                self.packed[place] = self.packed[place] + self.mates[order, code]

    def group(self, order, group):
        begin, end = GROUPS[group]
        part = self.got.at[order, begin - 1 : end - 1]
        way = self.orders[order][step_of(begin)]
        return remote(
            part, part, self.send_sem.at[order, group], self.recv_sem.at[order, group], self.ways.partner(way)
        )

    def send(self, group):
        begin, end = GROUPS[group]
        for code in range(begin, end):
            for order in range(3):
                remote(
                    self.packed.at[self.place(order, code, self.ways.core)], self.got.at[order, code - 1],
                    self.send_sem.at[order, group], self.recv_sem.at[order, group],
                    self.ways.partner(self.orders[order][step_of(begin)]),
                ).start()

    def receive(self, group):
        begin, end = GROUPS[group]
        base = 1 << (begin.bit_length() - 1)
        for order in range(3):
            self.group(order, group).wait_recv()
            for code in range(begin, end):
                place = self.place(order, code - base, self.ways.core)
                self.packed[place] = self.packed[place] + self.got[order, code - 1]

    def share(self):
        for order in range(3):
            self.group(order, 5).wait_recv()
            place = self.place(order, 0, self.ways.core)
            self.final[self.ways.core, order, self.ways.half] = self.packed[place] + self.got[order, 0]
            self.last_copy(order).start()

    def last_copy(self, order):
        part = self.final.at[self.ways.core, order, self.ways.half]
        return remote(part, part, self.last_send.at[order], self.last_recv.at[order], self.ways.side)

    def end_copy(self, order):
        part = self.final.at[self.ways.core, order]
        return remote(part, part, self.end_send.at[order], self.end_recv.at[order], self.ways.mate)

    def hand_over(self):
        for order in range(3):
            self.last_copy(order).wait_recv()
            self.end_copy(order).start()

    def end(self):
        for order in range(3):
            self.end_copy(order).wait()
            self.last_copy(order).wait_send()
            for at in range(4):
                self.core_group(order, at).wait_send()
            for group in range(len(GROUPS)):
                self.group(order, group).wait_send()


class LateSum:
    def __init__(self, ways, orders, hp, packed, held, got, final, sems):
        self.ways, self.orders, self.hp = ways, orders, hp
        self.packed, self.held, self.got, self.final = packed, held, got, final
        self.first_send, self.first_recv, self.send_sem, self.recv_sem, self.last_send, self.last_recv = sems
        self.rows = held.shape[3]

    def part(self, order, code):
        page, half = self.ways.piece(self.orders[order], code)
        return self.hp, order, page, pl.ds(pl.multiple_of(half * self.rows, 16), self.rows)

    def start(self):
        hp = self.hp
        for code in (12, 13, 14, 15, 8, 9, 10, 11):
            for order in range(3):
                remote(
                    self.packed.at[self.part(order, code)], self.got.at[hp, order, code - 1],
                    self.first_send.at[hp, order], self.first_recv.at[hp, order],
                    self.ways.partner(self.orders[order][0]),
                ).start()

    def first(self, order):
        part = self.got.at[self.hp, order, 7:15]
        return remote(
            part, part, self.first_send.at[self.hp, order], self.first_recv.at[self.hp, order],
            self.ways.partner(self.orders[order][0]),
        )

    def copy(self, order, step):
        begin, end = 8 >> step, 16 >> step
        return remote(
            self.held.at[self.hp, order, begin:end], self.got.at[self.hp, order, begin - 1 : end - 1],
            self.send_sem.at[self.hp, order, step - 1], self.recv_sem.at[self.hp, order, step - 1],
            self.ways.partner(self.orders[order][step]),
        )

    def shares(self):
        ways, hp = self.ways, self.hp
        part = self.final.at[ways.core, hp, ways.half]
        for which, to in enumerate((ways.side, ways.mate, ways.partner("yc"))):
            yield remote(part, part, self.last_send.at[hp, which], self.last_recv.at[hp, which], to)

    def advance(self, step):
        ways, hp = self.ways, self.hp
        for order in range(3):
            if step == 0:
                self.first(order).wait_recv()
                for code in (4, 5, 6, 7, 0, 1, 2, 3):
                    self.held[hp, order, code] = self.packed[self.part(order, code)] + self.got[hp, order, code + 7]
                    if code == 7:
                        self.copy(order, 1).start()
            elif step < 3:
                self.copy(order, step).wait_recv()
                count = 8 >> step
                self.held[hp, order, :count] = (
                    self.held[hp, order, :count] + self.got[hp, order, count - 1 : 2 * count - 1]
                )
                self.copy(order, step + 1).start()
            else:
                self.copy(order, 3).wait_recv()
                self.final[ways.core, hp, ways.half, order] = self.held[hp, order, 0] + self.got[hp, order, 0]
        if step == 3:
            for copy in self.shares():
                copy.start()

    def finish(self):
        for copy in self.shares():
            copy.wait()
        for order in range(3):
            self.first(order).wait_send()
            for step in (1, 2, 3):
                self.copy(order, step).wait_send()


class SmallSum:
    rounds = "xamyc"

    def __init__(self, ways, value, got, sems):
        self.ways, self.value, self.got = ways, value, got
        self.send_sem, self.recv_sem = sems

    def copy(self, step):
        return remote(
            self.value.at[step], self.got.at[step], self.send_sem.at[step], self.recv_sem.at[step],
            self.ways.partner(self.rounds[step]),
        )

    def start(self):
        self.copy(0).start()

    def advance(self, step):
        self.copy(step).wait_recv()
        self.value[step + 1] = self.value[step] + self.got[step]
        if step < 4:
            self.copy(step + 1).start()

    def finish(self):
        for step in range(5):
            self.copy(step).wait_send()


def norm_of(resid):
    center = resid - jnp.mean(resid, axis=-1, keepdims=True)
    spread = jnp.mean(center * center, axis=-1, keepdims=True)
    inverse = lax.rsqrt(spread + norm_eps)
    return center * inverse, inverse


def norm_back(grad, normed, inverse):
    mean = jnp.mean(grad, axis=-1, keepdims=True)
    along = jnp.mean(grad * normed, axis=-1, keepdims=True)
    return inverse * (grad - mean - normed * along)


def column_sum(values):
    return jnp.sum(values, axis=0, keepdims=True)


def layer_kernel(
    summed, tokens_in, boxes, cotangent_in, out_w, up_w, down_w, qkv_w, lengths, freq, out_b, gain1, shift1, up_b,
    down_b, gain2, shift2, qkv_b, box_w,
    x_t_hbm, q_hbm, k_hbm, v_hbm, sc_hbm, p_hbm, layer_out, dx_out, *refs
):
    if summed:
        (
            early_out, down_out, late_out, small_out, tiny_out,
            x, box, ctx_own, dresid1, dctx_own, dctx, dx_mate, dx_side,
            x_mate_send, x_mate_recv, x_side_send, x_side_recv, x_pass_send, x_pass_recv, ctx_send, ctx_recv,
            own_sem, mate_send, mate_recv, core_send, core_recv, side_send, side_recv,
            packed_down, packed, down_mates, early_mates, down_got, early_got, late_got,
            small_value, small_got, tiny_value, tiny_got, *sems,
        ) = refs
        down_sems, early_sems, late_sems, small_sems, tiny_sems = sems[:8], sems[8:16], sems[16:22], sems[22:24], sems[24:]
        g_rows = small_value.at[0]
    else:
        (
            packed_down, packed, late_out, g_rows, tiny_out,
            x, box, ctx_own, dresid1, dctx_own, dctx, dx_mate, dx_side,
            x_mate_send, x_mate_recv, x_side_send, x_side_recv, x_pass_send, x_pass_recv, ctx_send, ctx_recv,
            own_sem, mate_send, mate_recv, core_send, core_recv, side_send, side_recv,
        ) = refs
    ways = Ways()
    core, mate, side = ways.core, ways.mate, ways.side
    greet(ways.everyone() if summed else [mate, side])
    pages, block, width = dctx_own.shape
    half = width // 2
    pairs = half // LANES
    chip, keys = 2 * block, 4 * block
    shard = width // 8
    head = LANES // 2
    scale = 0.125
    chunks = 6
    chunk = up_w.shape[1] // chunks
    up_pieces = chunk // LANES
    if summed:
        down = EarlySum(ways, DOWN_ORDERS, packed_down, down_mates, down_got, down_out, down_sems)
        early = EarlySum(ways, EARLY_ORDERS, packed, early_mates, early_got, early_out, early_sems)
        small = SmallSum(ways, small_value, small_got, small_sems)
        tiny = SmallSum(ways, tiny_value, tiny_got, tiny_sems)
        first_chunk = chunks // 2 * (1 - core)
    else:
        first_chunk = 0

    def row(ref):
        return ref[...].reshape(1, -1)

    def of_half(part, which):
        return pl.ds(pl.multiple_of(part * 2 * half + which * half, LANES), half)

    def own_copy(pg):
        return pltpu.make_async_copy(
            dctx_own.at[pg, :, of_half(0, core)], dctx.at[pg, core], own_sem.at[pg]
        )

    def mate_copy(pg):
        return remote(
            dctx_own.at[pg, :, of_half(0, 1 - core)], dctx.at[pg, core], mate_send.at[pg],
            mate_recv.at[pg], mate,
        )

    def send_dctx():
        for pg in range(pages):
            mate_copy(pg).start()
            own_copy(pg).start()

    moves = {}
    if summed:
        for name, chain in (("D", down), ("E", early)):
            for at in range(6):
                moves["%ss%d" % (name, at)] = functools.partial(chain.send, at)
                moves["%sr%d" % (name, at)] = functools.partial(chain.receive, at)
            for at in range(4):
                moves["%sc%d" % (name, at)] = functools.partial(chain.add_core, at)
            moves[name + "sh"], moves[name + "ho"], moves[name + "fin"] = chain.share, chain.hand_over, chain.end
        for name, chain in (("S", small), ("T", tiny)):
            moves[name + "s"] = chain.start
            for at in range(5):
                moves["%sa%d" % (name, at)] = functools.partial(chain.advance, at)

    def at_place(place):
        if summed:
            for name in PLAN.get(place, ()):
                moves[name]()

    def at_step(step, places):
        for at, place in enumerate(places):
            if place in PLAN and summed:
                pl.when(step == at)(functools.partial(at_place, place))

    def feed_loads(cotangent, w_out, w_up, w_down, w_sem, up_sem, down_sem):
        rows_in = pltpu.make_async_copy(cotangent_in, cotangent, w_sem.at[0])
        out_load = pltpu.make_async_copy(out_w, w_out, w_sem.at[1])

        def up_load(j):
            return pltpu.make_async_copy(
                up_w.at[:, pl.ds(pl.multiple_of(j * chunk, LANES), chunk)], w_up.at[j], up_sem.at[j]
            )

        def down_load(j):
            return pltpu.make_async_copy(
                down_w.at[pl.ds(pl.multiple_of(j * chunk, LANES), chunk)], w_down.at[j], down_sem.at[j]
            )

        return rows_in, out_load, up_load, down_load

    def attend_phase(
        start_loads, x_t, w_q, w_kv, q, k, v, sc, probs, ctx, box2, own_load, w_sem, out_sem, p_sem, ctx_sem
    ):
        loads = [
            pltpu.make_async_copy(qkv_w.at[:, of_half(0, core)], w_q, w_sem.at[0]),
            pltpu.make_async_copy(qkv_w.at[:, of_half(1, core)], w_kv.at[:, :half], w_sem.at[1]),
            pltpu.make_async_copy(qkv_w.at[:, of_half(2, core)], w_kv.at[:, half:], w_sem.at[2]),
        ]
        own = []
        for pg in range(pages):
            own.append(pltpu.make_async_copy(tokens_in.at[pg], x.at[pg, core], own_load.at[pg, 0]))
            own.append(pltpu.make_async_copy(boxes.at[pg], box.at[pg, core], own_load.at[pg, 1]))
        for copy in own:
            copy.start()
        for copy in loads:
            copy.start()
        to_mate, to_side = [], []
        for pg in range(pages):
            for which, (src, dst) in enumerate(((tokens_in, x), (boxes, box))):
                to_side.append(
                    remote(src.at[pg], dst.at[pg, 2 + core], x_side_send.at[pg, which], x_side_recv.at[pg, which], side)
                )
                to_side[-1].start()
                to_mate.append(
                    remote(src.at[pg], dst.at[pg, core], x_mate_send.at[pg, which], x_mate_recv.at[pg, which], mate)
                )
                to_mate[-1].start()
        start_loads()
        saved = ((x_t, x_t_hbm), (sc, sc_hbm), (q, q_hbm), (k, k_hbm), (v, v_hbm))
        zero = jnp.zeros_like(box_w)
        box2[...] = jnp.concatenate(
            [jnp.concatenate([box_w[...], zero], 1), jnp.concatenate([zero, box_w[...]], 1)], 0
        )

        def bias_of(part):
            both = [
                qkv_b[(2 * part + which) * half : (2 * part + which + 1) * half].reshape(1, half)
                for which in range(2)
            ]
            return jnp.where(core == 0, both[0], both[1])

        for copy in loads:
            copy.wait()

        both_in = ((tokens_in, x), (boxes, box))

        def sines(pg, side_place):
            for at in (2 * side_place, 2 * side_place + 1):
                rows = box[pg, at]
                spread = [
                    jnp.broadcast_to(rows[c : c + 1], (freq.shape[0] // 4, LANES)) for c in range(4)
                ]
                sine, cosine = sin_cos(jnp.concatenate(spread, 0) * freq[...])
                sc[pg, at * LANES : (at + 1) * LANES] = jnp.concatenate([sine, cosine], 0).T

        def project(pg, side_place):
            rows = slice(side_place * chip, (side_place + 1) * chip)
            part = x[pg, 2 * side_place : 2 * side_place + 2].reshape(chip, width)
            x_t[pg, :, rows] = part.T
            bias = jnp.concatenate([bias_of(1), bias_of(2)], 1)
            kv_part = (dot(part, w_kv[...]) + bias).astype(low)
            for hp in range(pairs):
                k[pg, hp, rows] = kv_part[:, hp * LANES : (hp + 1) * LANES]
                v[pg, hp, rows] = kv_part[:, half + hp * LANES : half + (hp + 1) * LANES]
            if side_place == 0:
                q_part = (dot(part, w_q[...]) + bias_of(0)).astype(low)
                for hp in range(pairs):
                    q[pg, hp] = q_part[:, hp * LANES : (hp + 1) * LANES]
            sines(pg, side_place)

        @pl.loop(0, pages)
        def _(pg):
            for which, (src, dst) in enumerate(both_in):
                pltpu.make_async_copy(src.at[pg], dst.at[pg, core], own_load.at[pg, which]).wait()
                remote(
                    src.at[pg], dst.at[pg, core], x_mate_send.at[pg, which], x_mate_recv.at[pg, which], mate
                ).wait_recv()
            project(pg, 0)

        @pl.loop(0, pages)
        def _(pg):
            passed = []
            for which, (src, dst) in enumerate(both_in):
                remote(
                    src.at[pg], dst.at[pg, 2 + core], x_side_send.at[pg, which], x_side_recv.at[pg, which], side
                ).wait_recv()
                copy = remote(
                    dst.at[pg, 2 + core], dst.at[pg, 2 + core], x_pass_send.at[pg, which],
                    x_pass_recv.at[pg, which], mate,
                )
                copy.start()
                passed.append(copy)
            for copy in passed:
                copy.wait_recv()
            project(pg, 1)
            for which, (src, dst) in enumerate(saved):
                pltpu.make_async_copy(src.at[pg], dst.at[pg], out_sem.at[pg, which]).start()
            place = lax.broadcasted_iota(jnp.int32, (keys, chip), 0) + ways.half * chip
            place = jnp.where(place >= keys, place - keys, place)
            valid = place < lengths[pg]

            @pl.loop(0, pairs)
            def _(hp):
                both = sc[pg]
                cosine2, sine2 = turned(both)
                basis = both.astype(low)
                basis_q = (both[:chip] * scale).astype(low)
                left = lane_halves((chip, LANES))
                cosine_q = jnp.where(left, -cosine2[:chip], cosine2[:chip]) * scale
                sine_q = jnp.where(left, sine2[:chip], -sine2[:chip]) * scale
                q_pair, k_pair = q[pg, hp], k[pg, hp]
                q_proj = dot(q_pair, box2[...])
                k_proj = dot(k_pair, box2[...])
                v_t = v[pg, hp].T
                outs = []
                for e in range(2):
                    at = slice(e * LANES, (e + 1) * LANES)
                    q_pos = rotate_key(q_proj[:, at], cosine_q, sine_q).astype(low)
                    k_pos = rotate_key(k_proj[:, at], cosine2, sine2).astype(low)
                    mine = left if e == 0 else jnp.logical_not(left)
                    q_own = jnp.where(mine, q_pair.astype(f32) * scale, 0.0).astype(low)
                    scores = dot_nt(
                        jnp.concatenate([basis, k_pos], 1), jnp.concatenate([q_pos, basis_q], 1)
                    )
                    scores = scores + dot_nt(k_pair, q_own)
                    scores = jnp.where(valid, scores, -1e30)
                    top = jnp.max(scores, axis=0, keepdims=True)
                    grown = jnp.exp(scores - top)
                    total = jnp.sum(grown, axis=0, keepdims=True)
                    p = (grown * (1.0 / total)).astype(low)
                    probs[pg, hp, e] = p
                    outs.append(dot(v_t[e * LANES // 2 : (e + 1) * LANES // 2], p))
                pltpu.make_async_copy(probs.at[pg, hp], p_hbm.at[pg, hp], p_sem.at[pg, hp]).start()
                context = jnp.concatenate(outs, 0).T.astype(low)
                lanes = pl.ds(pl.multiple_of(hp * LANES, LANES), LANES)
                ctx[pg, 0, :, lanes] = context[: chip // 2]
                ctx[pg, 1, :, lanes] = context[chip // 2 :]

            mine = pl.ds(pl.multiple_of(core * half, LANES), half)
            pltpu.make_async_copy(ctx.at[pg, core], ctx_own.at[pg, :, mine], ctx_sem.at[pg]).start()
            remote(
                ctx.at[pg, 1 - core], ctx_own.at[pg, :, mine], ctx_send.at[pg], ctx_recv.at[pg], mate
            ).start()
            for copy in passed:
                copy.wait_send()

        mine = pl.ds(pl.multiple_of(core * half, LANES), half)
        for pg in range(pages):
            for which, (src, dst) in enumerate(saved):
                pltpu.make_async_copy(src.at[pg], dst.at[pg], out_sem.at[pg, which]).wait()
            for hp in range(pairs):
                pltpu.make_async_copy(probs.at[pg, hp], p_hbm.at[pg, hp], p_sem.at[pg, hp]).wait()
            pltpu.make_async_copy(ctx.at[pg, core], ctx_own.at[pg, :, mine], ctx_sem.at[pg]).wait()
            remote(
                ctx.at[pg, 1 - core], ctx_own.at[pg, :, mine], ctx_send.at[pg], ctx_recv.at[pg], mate
            ).wait_send()
        for copy in to_side + to_mate:
            copy.wait_send()

    def feed_phase(
        cotangent, w_out, w_up, w_down, w_sem, up_sem, down_sem, output, act, slope, norm1, inverse1, hidden, hidden_t,
        grow, staged, up_rows, out_sem,
    ):
        rows_in, out_load, up_load, down_load = feed_loads(cotangent, w_out, w_up, w_down, w_sem, up_sem, down_sem)
        g_rows[...] = jnp.zeros_like(g_rows)
        for j in range(chunks):
            up_rows[j : j + 1] = up_b[j * chunk : (j + 1) * chunk].reshape(1, chunk)
        out_load.wait()
        rows_in.wait()
        for pg in range(pages):
            other = pl.ds(pl.multiple_of((1 - core) * (width // 2), LANES), width // 2)
            part = ctx_own.at[pg, :, other]
            remote(part, part, ctx_send.at[pg], ctx_recv.at[pg], mate).wait_recv()
        ctx = ctx_own[...].reshape(pages * block, width)
        tokens = jnp.concatenate([x[pg, core] for pg in range(pages)], 0)
        resid = tokens.astype(f32) + dot(ctx, w_out[...]) + row(out_b)
        normed, inverse = norm_of(resid)
        norm1[...] = normed
        inverse1[...] = jnp.broadcast_to(inverse, inverse1.shape)
        first = normed * row(gain1) + row(shift1)
        hidden[...] = first.astype(low)
        hidden_t[...] = first.astype(low).T
        grow[...] = first + row(down_b)

        @pl.loop(0, chunks)
        def _(j):
            up_load(j).wait()
            upper = dot(hidden[...], w_up[j]) + up_rows[pl.ds(j, 1)]
            cdf = 0.5 + 0.5 * lax.erf(upper * 0.7071067811865476)
            act_low = (upper * cdf).astype(low)
            act[j] = act_low
            slope[j] = (cdf + upper * (jnp.exp(upper * upper * -0.5) * 0.3989422804014327)).astype(low)
            down_load(j).wait()
            grow[...] += dot(act_low, w_down[j])

        normed2, inverse2 = norm_of(grow[...])
        output[...] = (normed2 * row(gain2) + row(shift2)).astype(low)
        output_copy = pltpu.make_async_copy(output, layer_out, out_sem)
        output_copy.start()
        cot = cotangent[...].astype(f32)
        g_rows[0:1] = column_sum(cot * normed2)
        g_rows[1:2] = column_sum(cot)
        dresid2 = norm_back(cot * row(gain2), normed2, inverse2)
        dffn = dresid2.astype(low)
        g_rows[2:3] = column_sum(dffn.astype(f32))
        grow[...] = dresid2
        staged[...] = dffn

        @pl.loop(0, chunks)
        def _(j):
            grad_down = dot_tn(act[j], staged[...]).astype(low)
            for piece in range(up_pieces):
                at = j * up_pieces + piece
                per = up_pieces * chunks // 8
                rows = pl.ds(pl.multiple_of((at % per) * LANES, LANES), LANES)
                for column in range(6):
                    packed_down[column, at // per, rows] = grad_down[
                        piece * LANES : (piece + 1) * LANES, column * LANES : (column + 1) * LANES
                    ]

        if summed:
            down.swap(range(3))
        up_end = up_pieces * shard // 2
        per_half = up_end + shard // 2

        @pl.loop(0, chunks)
        def _(step):
            at_step(step, ["f%d" % at for at in range(chunks)])
            j = lax.rem(step + first_chunk, chunks)
            dffn = staged[...]
            dupper = (dot_nt(dffn, w_down[j]) * slope[j].astype(f32)).astype(low)
            g_rows[pl.ds(8 + j, 1), :chunk] = column_sum(dupper.astype(f32))
            grow[...] += dot_nt(dupper, w_up[j])
            grad_up = dot(hidden_t[...], dupper).astype(low)
            for piece in range(up_pieces):
                part = grad_up[:, piece * LANES : (piece + 1) * LANES].reshape(8, shard, LANES)
                at = piece // (up_pieces // 2) * per_half + piece % (up_pieces // 2) * shard
                packed[j, :, at : at + shard] = part
            if summed:

                for order in range(3):

                    @pl.when(step == order)
                    def _(order=order):
                        early.swap([order], 0, up_end)

        dhidden = grow[...]
        normed = norm1[...]
        g_rows[3:4] = column_sum(dhidden * normed)
        g_rows[4:5] = column_sum(dhidden)
        back = norm_back(dhidden * row(gain1), normed, inverse1[:, :1])
        dresid1[...] = back.reshape(dresid1.shape)
        dattn = back.astype(low)
        g_rows[5:6] = column_sum(dattn.astype(f32))
        dctx_own[...] = dot_nt(dattn, w_out[...]).astype(low).reshape(dctx_own.shape)
        send_dctx()
        at_place("fe")
        grad_out = dot_tn(ctx_own[...].reshape(pages * block, width), dattn).astype(low)
        for column in range(6):
            part = grad_out[:, column * LANES : (column + 1) * LANES].reshape(8, shard, LANES)
            for half in range(2):
                at = half * per_half + up_end
                packed[column, :, at : at + shard // 2] = part[:, half * shard // 2 : (half + 1) * shard // 2]
        if summed:
            early.swap(range(3), up_end, per_half)
        at_place("fw")
        output_copy.wait()

    def back_phase(
        x_t, q, k, v, sc, probs, dq, dkv, w_c, dx, box_t, g_box, g_bias, late_packed, late_held, in_sem, p_sem, w_sem
    ):
        def loads(pg):
            names = ((q_hbm, q), (k_hbm, k), (v_hbm, v), (sc_hbm, sc))
            copies = [
                pltpu.make_async_copy(src.at[pg], dst.at[pg], in_sem.at[pg, at])
                for at, (src, dst) in enumerate(names)
            ]
            at = pl.ds(pl.multiple_of(pg * keys, LANES), keys)
            copies.append(pltpu.make_async_copy(x_t_hbm.at[pg], x_t.at[:, at], in_sem.at[pg, 4]))
            return copies

        def p_load(hp, pg):
            return pltpu.make_async_copy(p_hbm.at[pg, hp], probs.at[pg, hp], p_sem.at[pg, hp])

        w_loads = [
            pltpu.make_async_copy(qkv_w.at[:, of_half(part, core)], w_c.at[part], w_sem.at[part])
            for part in range(3)
        ]
        for pg in range(pages):
            for copy in loads(pg):
                copy.start()
            for hp in range(pairs):
                p_load(hp, pg).start()
        for copy in w_loads:
            copy.start()

        def late(hp):
            return LateSum(ways, LATE_ORDERS, hp, late_packed, late_held, late_got, late_out, late_sems)

        for e in range(2):
            box_t[e] = jnp.zeros_like(box_t[e])
            box_t[e, :, e * head : (e + 1) * head] = box_w[...].astype(f32).T.astype(low)
        g_box[...] = jnp.zeros_like(g_box)

        def take(pg):
            for copy in loads(pg):
                copy.wait()
            own_copy(pg).wait()
            mate_copy(pg).wait_recv()

        def one_pair(pg, hp):
            lanes = pl.ds(pl.multiple_of(hp * LANES, LANES), LANES)
            p_load(hp, pg).wait()
            both = sc[pg]
            cosine2, sine2 = turned(both)
            flat = both.T
            sine_t, cosine_t = flat[:head, :chip], flat[head:, :chip]
            basis = both.astype(low)
            basis_t = flat.astype(low)
            q_pair, k_pair, v_pair = q[pg, hp], k[pg, hp], v[pg, hp]
            q_t, k_t = q_pair.T, k_pair.T
            dc = dctx[pg, :, :, lanes].reshape(chip, LANES)
            left = lane_halves((chip, LANES))
            zero = jnp.zeros_like(dc)
            dk, dv, dqs = 0.0, 0.0, []
            for e in range(2):
                mine = left if e == 0 else jnp.logical_not(left)
                own_rows = slice(e * head, (e + 1) * head)
                p = probs[pg, hp, e]
                dc_own = jnp.where(mine, dc, zero)
                q_own = jnp.where(mine, q_pair, zero)
                dp = dot_nt(v_pair, dc_own)
                p_wide = p.astype(f32)
                delta = jnp.sum(p_wide * dp, axis=0, keepdims=True)
                ds = (p_wide * (dp - delta)).astype(low)
                dv = dv + dot(p, dc_own)
                dk_feat = dot(ds, jnp.concatenate([q_own, basis[:chip]], 1)) * scale
                dq_feat = dot(jnp.concatenate([k_t[own_rows], basis_t], 0), ds) * scale
                dk_proj = rotate_key(dk_feat[:, LANES:], cosine2, sine2).astype(low)
                a, b = dq_feat[head : 2 * head], dq_feat[2 * head :]
                dq_proj = jnp.concatenate(
                    [a * cosine_t - b * sine_t, a * sine_t + b * cosine_t], 0
                ).astype(low)
                dk = dk + dk_feat[:, :LANES] + dot(dk_proj, box_t[e])
                dqs.append(dq_feat[:head] + dot(box_w[...], dq_proj))
                g_box[...] += dot(k_t[own_rows], dk_proj) + dot_nt(q_t[own_rows], dq_proj)
            at = pl.ds(pl.multiple_of(pg * keys, LANES), keys)
            at_q = pl.ds(pl.multiple_of(pg * chip, LANES), chip)
            dq[hp, at_q] = jnp.concatenate(dqs, 0).T.astype(low)
            dkv[hp, at, :LANES] = dk.astype(low)
            dkv[hp, at, LANES:] = dv.astype(low)

        def pair_grads(hp):
            dkv_all = dkv[hp]
            dq_all = dq[hp]
            g_kv = column_sum(dkv_all.astype(f32))
            g_bias[pl.ds(hp, 1)] = column_sum(dq_all.astype(f32))
            g_bias[pl.ds(hp + pairs, 1)] = g_kv[:, :LANES]
            g_bias[pl.ds(hp + 2 * pairs, 1)] = g_kv[:, LANES:]
            grad = dot(x_t[...], dkv_all).astype(low)
            x_q = jnp.concatenate([x_t[:, pg * keys : pg * keys + chip] for pg in range(pages)], 1)
            grad_q = dot(x_q, dq_all).astype(low)
            late_packed[hp, 0] = grad_q.reshape(8, shard, LANES)
            late_packed[hp, 1] = grad[:, :LANES].reshape(8, shard, LANES)
            late_packed[hp, 2] = grad[:, LANES:].reshape(8, shard, LANES)

        def core_copy(pg, at):
            return remote(
                dx.at[pg, at, 1 - core], dx_mate.at[pg, at], core_send.at[pg, at], core_recv.at[pg, at],
                mate,
            )

        def side_copy(pg):
            return remote(dx.at[pg, 1, core], dx_side.at[pg], side_send.at[pg], side_recv.at[pg], side)

        def input_part(pg):
            for at in (1, 0):
                rows = pl.ds(pl.multiple_of(pg * keys + at * chip, LANES), chip)
                dks = jnp.concatenate([dkv[hp, rows, :LANES] for hp in range(pairs)], 1)
                dvs = jnp.concatenate([dkv[hp, rows, LANES:] for hp in range(pairs)], 1)
                total = dot_nt(dks, w_c[1]) + dot_nt(dvs, w_c[2])
                if at == 0:
                    rows_q = pl.ds(pl.multiple_of(pg * chip, LANES), chip)
                    dqs = jnp.concatenate([dq[hp, rows_q] for hp in range(pairs)], 1)
                    total = total + dot_nt(dqs, w_c[0])
                dx[pg, at] = total.astype(low).reshape(2, block, width)
                core_copy(pg, at).start()

        def pass_input(pg):
            core_copy(pg, 1).wait_recv()
            dx[pg, 1, core] = dx[pg, 1, core] + dx_mate[pg, 1]
            side_copy(pg).start()

        def bias_rows():
            for part in range(3):
                for which in range(2):
                    own = jnp.where(core == which, 1.0, 0.0)
                    for hp in range(pairs):
                        at = part * pairs + hp
                        yield 64 + (2 * part + which) * pairs + hp, g_bias[at : at + 1] * own

        def finish_input(pg):
            core_copy(pg, 0).wait_recv()
            side_copy(pg).wait_recv()
            total = dx[pg, 0, core].astype(f32) + dx_mate[pg, 0].astype(f32) + dx_side[pg].astype(f32)
            dx_out[pg] = (total + dresid1[pg]).astype(low)

        for pg in range(pages):
            moves["X%dp" % pg] = functools.partial(pass_input, pg)
            moves["X%dfin" % pg] = functools.partial(finish_input, pg)
        if summed:
            for hp in range(pairs):
                chain = late(hp)
                moves["L%ds" % hp], moves["L%dfin" % hp] = chain.start, chain.finish
                for at in range(4):
                    moves["L%da%d" % (hp, at)] = functools.partial(chain.advance, at)

        @pl.loop(0, pages - 1)
        def _(pg):
            take(pg)

            @pl.loop(0, pairs)
            def _(hp):
                at_step(pg * pairs + hp, ["b%d" % at for at in range(6)])
                one_pair(pg, hp)

            at_step(pg, ["p0", "p1"])

            @pl.when(pg == 0)
            def _():
                for copy in w_loads:
                    copy.wait()

            input_part(pg)
            at_step(pg, ["q0", "q1"])

        last = pages - 1
        take(last)

        @pl.loop(0, pairs)
        def _(hp):
            at_step(hp, ["b6", "b7", "b8"])
            one_pair(last, hp)
            pair_grads(hp)
            at_step(hp, ["g0", "g1"])

        if summed:
            tiny_value[0, : 8 * 8] = g_box[...]
            tiny_value[0, 64:] = jnp.zeros((24, LANES), f32)
            for at, row in bias_rows():
                tiny_value[0, at : at + 1] = row
        at_place("p2")
        input_part(last)
        at_place("tail")
        if not summed:
            for pg in range(pages):
                pass_input(pg)
            for pg in range(pages):
                finish_input(pg)
        for pg in range(pages):
            for at in range(2):
                core_copy(pg, at).wait_send()
            side_copy(pg).wait_send()
            mate_copy(pg).wait_send()
        if summed:
            small_out[...] = small_value[5]
            tiny_out[...] = tiny_value[5]
            small.finish()
            tiny.finish()
        else:
            late_out[...] = late_packed[...]
            tiny_out[:64] = g_box[...]
            tiny_out[64:] = jnp.zeros((24, LANES), f32)
            for at, row in bias_rows():
                tiny_out[at : at + 1] = row

    vmem, dma = pltpu.VMEM, pltpu.SemaphoreType.DMA
    rows = pages * block
    def forward(*weights):
        rows_in, out_load, up_load, down_load = feed_loads(*weights)

        def start_loads():
            out_load.start()
            rows_in.start()
            for j in range(chunks):
                up_load(j).start()
                down_load(j).start()

        pl.run_scoped(
            functools.partial(attend_phase, start_loads),
            vmem((pages, width, keys), low),
            vmem((width, half), low),
            vmem((width, 2 * half), low),
            vmem((pages, pairs, chip, LANES), low),
            vmem((pages, pairs, keys, LANES), low),
            vmem((pages, pairs, keys, LANES), low),
            vmem((pages, keys, LANES), f32),
            vmem((pages, pairs, 2, keys, chip), low),
            vmem((pages, 2, block, half), low),
            vmem((2 * box_w.shape[0], 2 * box_w.shape[1]), low),
            dma((pages, 2)), dma((3,)), dma((pages, 5)), dma((pages, pairs)), dma((pages,)),
        )
        pl.run_scoped(
            functools.partial(feed_phase, *weights),
            vmem((rows, width), low),
            vmem((chunks, rows, chunk), low),
            vmem((chunks, rows, chunk), low),
            vmem((rows, width), f32),
            vmem((rows, LANES), f32),
            vmem((rows, width), low),
            vmem((width, rows), low),
            vmem((rows, width), f32),
            vmem((rows, width), low),
            vmem((chunks, chunk), f32),
            dma,
        )

    pl.run_scoped(
        forward,
        vmem((rows, width), low),
        vmem((width, width), low),
        vmem((chunks, width, chunk), low),
        vmem((chunks, chunk, width), low),
        dma((2,)), dma((chunks,)), dma((chunks,)),
    )
    late_shape = (pairs, 3, 8, shard, LANES)
    pl.run_scoped(
        back_phase,
        vmem((width, pages * keys), low),
        vmem((pages, pairs, chip, LANES), low),
        vmem((pages, pairs, keys, LANES), low),
        vmem((pages, pairs, keys, LANES), low),
        vmem((pages, keys, LANES), f32),
        vmem((pages, pairs, 2, keys, chip), low),
        vmem((pairs, pages * chip, LANES), low),
        vmem((pairs, pages * keys, 2 * LANES), low),
        vmem((3, width, half), low),
        vmem((pages, 2, 2, block, width), low),
        vmem((2, LANES, LANES), low),
        vmem(box_w.shape, f32),
        vmem((3 * pairs, LANES), f32),
        vmem(late_shape, low),
        vmem((pairs, 3, 8, shard // 2, LANES), low),
        dma((pages, 5)), dma((pages, pairs)), dma((3,)),
    )


def layer(tokens, boxes, lengths, cotangent, weights, vectors, qkv_w, qkv_b, box_w, summed):
    pages, block, width = tokens.shape
    head_dim, pos = box_w.shape
    count = pos // 8
    freqs = 10000.0 ** (-np.arange(count) / count)
    freq = jnp.asarray(np.tile(np.tile(freqs, 4)[:, None], (1, LANES)), f32)
    boxes_t = boxes.astype(f32).transpose(0, 2, 1)
    chip, keys = 2 * block, 4 * block
    rows = pages * block
    half = width // 2
    pairs = half // LANES
    shard = width // 8
    hidden_width = weights[1].shape[1]
    down_rows = hidden_width // 8
    packed_rows = down_rows + shard
    tiny_rows = 88
    small = (16, width)
    struct = jax.ShapeDtypeStruct
    vmem, dma = pltpu.VMEM, pltpu.SemaphoreType.DMA
    outs = [
        struct((pages, width, keys), low),
        struct((pages, pairs, chip, LANES), low),
        struct((pages, pairs, keys, LANES), low),
        struct((pages, pairs, keys, LANES), low),
        struct((pages, keys, LANES), f32),
        struct((pages, pairs, 2, keys, chip), low),
        struct((rows, width), low),
        struct((pages, block, width), low),
    ]
    scratch = [
        vmem((pages, 4, block, width), low),
        vmem((pages, 4, 4, LANES), f32),
        vmem((pages, block, width), low),
        vmem((pages, block, width), f32),
        vmem((pages, block, width), low),
        vmem((pages, 2, block, half), low),
        vmem((pages, 2, block, width), low),
        vmem((pages, block, width), low),
        *[dma((pages, 2))] * 6, dma((pages,)), dma((pages,)),
        dma((pages,)), dma((pages,)), dma((pages,)), dma((pages, 2)), dma((pages, 2)), dma((pages,)), dma((pages,)),
    ]
    if summed:
        outs += [
            struct((2, 3, 2, packed_rows // 2, LANES), low),
            struct((2, 3, 2, down_rows // 2, LANES), low),
            struct((2, pairs, 2, 3, shard // 2, LANES), low),
            struct(small, f32),
            struct((tiny_rows, LANES), f32),
        ]
        scratch += [
            vmem((6, 8, down_rows, LANES), low),
            vmem((6, 8, packed_rows, LANES), low),
            vmem((3, 16, down_rows // 2, LANES), low),
            vmem((3, 16, packed_rows // 2, LANES), low),
            vmem((3, 15, down_rows // 2, LANES), low),
            vmem((3, 15, packed_rows // 2, LANES), low),
            vmem((pairs, 3, 15, shard // 2, LANES), low),
            vmem((6,) + small, f32),
            vmem((5,) + small, f32),
            vmem((6, tiny_rows, LANES), f32),
            vmem((5, tiny_rows, LANES), f32),
        ]
        groups = len(GROUPS)
        scratch += ([dma((3, 4))] * 2 + [dma((3, groups))] * 2 + [dma((3,))] * 4) * 2
        scratch += [dma((pairs, 3))] * 2 + [dma((pairs, 3, 3))] * 2 + [dma((pairs, 3))] * 2
        scratch += [dma((5,))] * 4
    else:
        outs += [
            struct((6, 8, down_rows, LANES), low),
            struct((6, 8, packed_rows, LANES), low),
            struct((pairs, 3, 8, shard, LANES), low),
            struct(small, f32),
            struct((tiny_rows, LANES), f32),
        ]
    return pl.pallas_call(
        functools.partial(layer_kernel, summed),
        out_shape=tuple(outs),
        in_specs=[any_spec()] * 7 + [pl.BlockSpec(memory_space=pltpu.SMEM)] + [vmem_spec()] * 10,
        out_specs=(any_spec(),) * 7 + (vmem_spec(),) * 6,
        scratch_shapes=scratch,
        compiler_params=pltpu.CompilerParams(
            collective_id=2, has_side_effects=True, vmem_limit_bytes=63 * 2**20
        ),
        name="layer",
    )(
        tokens, boxes_t, cotangent.reshape(rows, width), *weights, qkv_w, lengths, freq, *vectors, qkv_b, box_w
    )[6:]


def finish_kernel(
    early_in, rest_in, late_in, small_in, tiny_in, dx_in, layer_in,
    up_out, down_out, out_out, qkv_out, qkv_b, box, out_b, gain1, shift1, up_b, down_b, gain2, shift2, input_grad,
    layer_out, early, rest, late, small, tiny, up, down, out, qkv, sems, out_sems,
):
    page = lax.axis_index("page")
    shard = out.shape[0]
    pieces = up.shape[1] // (6 * LANES)
    pairs = (
        (early_in, early), (rest_in, rest), (late_in, late), (small_in, small), (tiny_in, tiny), (dx_in, input_grad),
        (layer_in, layer_out),
    )
    copies = [pltpu.make_async_copy(src, dst, sems.at[at]) for at, (src, dst) in enumerate(pairs)]
    for copy in copies:
        copy.start()
    results = ((up, up_out), (down, down_out), (out, out_out), (qkv, qkv_out))
    done = [pltpu.make_async_copy(src, dst, out_sems.at[at]) for at, (src, dst) in enumerate(results)]
    columns = [(which, order) for which in range(2) for order in range(3)]
    per = pieces // 2
    copies[0].wait()
    for column, (which, order) in enumerate(columns):
        rows = early[which, order].astype(f32)
        at = column * LANES
        for half in range(2):
            for piece in range(per):
                up_at = (column * pieces + half * per + piece) * LANES
                up[:, up_at : up_at + LANES] = rows[half, piece * shard : (piece + 1) * shard]
            out[half * shard // 2 : (half + 1) * shard // 2, at : at + LANES] = rows[half, per * shard :]
    done[0].start()
    done[2].start()
    copies[1].wait()
    for column, (which, order) in enumerate(columns):
        at = column * LANES
        down[:, at : at + LANES] = rest[which, order].astype(f32).reshape(-1, LANES)
    done[1].start()
    copies[2].wait()
    for column, (which, order) in enumerate(columns):
        for part in range(3):
            at = (part * 6 + column) * LANES
            qkv[:, at : at + LANES] = late[which, order, :, part].astype(f32).reshape(shard, LANES)
    done[3].start()
    copies[3].wait()
    copies[4].wait()
    rows = pltpu.roll(small[:8], lax.rem(8 * shard - page * shard, 8 * shard), 1)
    for at, ref in enumerate((gain2, shift2, down_b, gain1, shift1, out_b)):
        ref[...] = rows[at, :shard]
    flat = jnp.concatenate([small[8 + at : 9 + at, : pieces * LANES] for at in range(6)], 1)
    every = flat.shape[1]
    flat = pltpu.roll(flat, lax.rem(every - page * up_b.shape[0], every), 1)
    up_b[...] = flat[0, : up_b.shape[0]]
    box[...] = tiny[pl.ds(pl.multiple_of(page * 8, 8), 8)]
    count = qkv_b.shape[0]
    first = page * count
    parts = [tiny[pl.ds(64 + first // LANES + piece, 1)] for piece in range(4)]
    rest = lax.rem(first, LANES)
    row = pltpu.roll(jnp.concatenate(parts, 1), lax.rem(4 * LANES - rest, 4 * LANES), 1)
    qkv_b[...] = row[0, :count]
    for copy in copies[5:] + done:
        copy.wait()


def finish(early, rest, late, small, tiny, dx, layer):
    struct = jax.ShapeDtypeStruct
    shapes = (
        (96, 3072), (384, 768), (96, 768), (96, 2304), (288,), (8, LANES), (96,), (96,), (96,), (384,), (96,), (96,), (96,),
    )
    operands = (early, rest, late, small, tiny, dx, layer)
    return pl.pallas_call(
        finish_kernel,
        out_shape=tuple(struct(shape, f32) for shape in shapes) + (struct(dx.shape, low), struct(layer.shape, low)),
        in_specs=[any_spec()] * 7,
        out_specs=(any_spec(),) * 4 + (vmem_spec(),) * 11,
        scratch_shapes=[pltpu.VMEM(operand.shape, operand.dtype) for operand in operands[:5]]
        + [pltpu.VMEM(shape, f32) for shape in shapes[:4]]
        + [pltpu.SemaphoreType.DMA((7,)), pltpu.SemaphoreType.DMA((4,))],
        compiler_params=pltpu.CompilerParams(vmem_limit_bytes=63 * 2**20),
        name="finish",
    )(*operands)


def reduce_by_collectives(packed, packed_down, packed_qkv, vectors):
    core = lax.axis_index("blk") % 2
    packed = packed.reshape(6, 8, 2, 240, LANES)
    up = packed[:, :, :, :192].reshape(6, 8, 4, 96, LANES).transpose(1, 3, 0, 2, 4).reshape(768, 3072)
    down = packed_down.transpose(1, 2, 0, 3).reshape(3072, 768)
    out = packed[:, :, :, 192:].transpose(1, 2, 3, 0, 4).reshape(768, 768)
    own = packed_qkv.transpose(2, 3, 1, 0, 4).reshape(768, 3, 384)
    qkv = jnp.zeros((768, 3, 2, 384), low)
    qkv = lax.dynamic_update_slice(qkv, own[:, :, None], (0, 0, core, 0)).reshape(768, 2304)
    grads = jax.tree.map(lambda g: g.astype(f32), (qkv, out, up, down, *vectors))
    page_sums = tuple(
        lax.psum_scatter(grad, "page", scatter_dimension=0, tiled=True) for grad in grads
    )
    return jax.tree.map(
        lambda part: part.astype(f32), lax.psum(jax.tree.map(lambda g: g.astype(low), page_sums), "blk")
    )


def local(
    tokens, lengths, boxes, qkv_weight, qkv_bias, box_weight, out_weight, out_bias, norm1_gain,
    norm1_bias, up_weight, up_bias, down_weight, down_bias, norm2_gain, norm2_bias, cotangent,
):
    pages, block, width = tokens.shape
    rows = pages * block
    summed = lax.axis_size("page") == 8
    output, input_grad, *parts = layer(
        tokens, boxes, lengths, cotangent, (out_weight, up_weight, down_weight),
        (out_bias, norm1_gain, norm1_bias, up_bias, down_bias, norm2_gain, norm2_bias),
        qkv_weight, qkv_bias, box_weight, summed,
    )
    if summed:
        early, rest, late, small, tiny = parts
        (
            up_w, down_w, out_w, qkv_w, qkv_b, box, out_b, gain1, shift1, up_b, down_b, gain2, shift2, input_grad,
            output,
        ) = finish(early, rest, late, small, tiny, input_grad, output)
        box = box.reshape(-1)
    else:
        down, packed, packed_qkv, small, tiny = parts
        vectors = (
            tiny[64:82].reshape(-1), tiny[:64].reshape(-1), small[5], small[3], small[4],
            small[8:14, :512].reshape(-1), small[2], small[0], small[1],
        )
        (
            qkv_w, out_w, up_w, down_w, qkv_b, box, out_b, gain1, shift1, up_b, down_b, gain2, shift2,
        ) = reduce_by_collectives(packed, down, packed_qkv, vectors)
    return (
        output.reshape(pages, block, width), input_grad, qkv_w, qkv_b, box, out_w, out_b, gain1, shift1, up_w, up_b, down_w, down_b, gain2, shift2,
    )


def solution(mesh):
    return jax.shard_map(
        local,
        mesh=mesh,
        in_specs=(
            P("page", "blk", None),
            P("page"),
            P("page", "blk", None),
            P(),
            P(),
            P(),
            P(),
            P(),
            P(),
            P(),
            P(),
            P(),
            P(),
            P(),
            P(),
            P(),
            P("page", "blk", None),
        ),
        out_specs=(
            P("page", "blk", None),
            P("page", "blk", None),
            P("page", None),
            P("page"),
            P("page"),
            P("page", None),
            P("page"),
            P("page"),
            P("page"),
            P("page", None),
            P("page"),
            P("page", None),
            P("page"),
            P("page"),
            P("page"),
        ),
        check_vma=False,
    )
```

time: 143 us -> 130 us (0.909)
  Pallas kernels: 139 us -> 126 us
    pallas_call x2 -> x1, Pallas kernels: 135 us -> 122 us  [layer(): pl.pallas_call(functools.partial(layer_kernel, summed), out_shape=tuple(o...]
where the time goes in v4:
time: 130 us; the launch traced here: 128 us
  Pallas kernels  126 us (97%)
    pallas_call x1, Pallas kernels, layer(): pl.pallas_call(functools.partial(layer_kernel, summed), out_shape=tuple(o...  122 us
    pallas_call x1, Pallas kernels, finish(): pl.pallas_call(finish_kernel, out_shape=tuple((struct(shape, f32) for sha...  4.16 us

profile of v4, /device:TPU:9, one launch (start us, length us, event | category | flops | bytes accessed | tf_op | source)
XLA Modules:
  0.0 128.0 jit_solution(1806650726327875372)
XLA Ops:
  0.6 1.3 %convert_bitcast_fusion.boxes = f32[3,4,128]{2,1,0:T(4,128)} fusion(s32[3,128,4]{1,2,0:T(4,128)} %param.20), kind=kLoop, calls=%fused_computation | loop fusion | flops 1536 | bytes 12288 | tf_op jit(solution)/shard_map/transpose | solution.py:1033
  1.9 121.7 %layer.1 = (bf16[3,768,512]{2,1,0:T(8,128)(2,1)}, bf16[3,3,256,128]{3,2,1,0:T(8,128)(2,1)}, bf16[3,3,512,128]{3,2,1,0:T(8,128)(2,1)}, bf16[3,3,512,128]{3,2,1,0:...) custom-call(bf16[3,128,768]{2,1,0:T(8,128)(2,1)} %tokens_in.1, ...), custom_call_target="tpu_custom_call" | custom-call | tf_op jit(solution)/shard_map/layer/pallas_call | solution.py:1101
  123.6 4.2 %finish.1 = (f32[96,3072]{1,0:T(8,128)}, f32[384,768]{1,0:T(8,128)}, f32[96,768]{1,0:T(8,128)}, f32[96,2304]{1,0:T(8,128)}, f32[288]{0:T(512)}, /*index=5*/f32[8...) custom-call(bf16[2,3,2,240,128]{4,3,2,1,0:T(8,128)(2,1)} %get-tuple-, ...), custom_call_target="tpu_custom_call" | custom-call | tf_op jit(solution)/shard_map/finish/pallas_call | solution.py:1183

commit v5 on v4

--- a/solution.py
+++ b/solution.py
@@ -102,23 +102,23 @@
     return ((z + 2) % 4) * 2 + x
 
 
-DOWN_ORDERS = ("xyam", "axym", "yaxm")
+DOWN_ORDERS = ("xaym", "ayxm", "yxam")
 EARLY_ORDERS = ("xaym", "axym", "yxam")
-LATE_ORDERS = ("xyam", "xyam", "axym")
+LATE_ORDERS = ("xyam", "axym", "xyam")
 PLAN = {
-    "f2": ("Dc0", "Ds0", "Dc1", "Ds1"),
-    "f3": ("Dc2", "Dc3"),
-    "fe": ("Dr0", "Ds3", "Ds2"),
+    "f0": ("Dc0", "Ds0"),
+    "f1": ("Dc1", "Ds1", "Dc2"),
+    "f2": ("Dc3",),
+    "fe": ("Dr0", "Ds2", "Ds3"),
     "fw": ("Ss",),
-    "b0": ("Ec2", "Ec3", "Ec0", "Es0", "Ec1", "Es1", "Dr3", "Dr1"),
-    "b1": ("Dr2",),
-    "b2": ("Sa0",),
+    "b0": ("Ec2", "Ec0", "Es0", "Ec3", "Ec1", "Es1", "Dr1", "Dr2"),
+    "b2": ("Sa0", "Dr3"),
     "b4": ("Er0", "Es2", "Ds4", "Es3", "X0p"),
     "q1": ("Sa1", "Er1"),
-    "g0": ("L0s", "X1p"),
-    "g1": ("Er2", "X0fin", "Es4"),
-    "p2": ("Dr4", "Ds5", "Sa2", "X1fin", "Ts"),
-    "tail": ("Er3", "L1s", "X2p", "Er4", "L2s", "Es5", "Sa3", "L0a0", "Sa4", "Ta0", "Dsh", "X2fin", "L1a0", "Dho", "L2a0", "L0a1", "Dfin", "L1a1", "Ta1", "L2a1", "Esh", "L0a2", "L1a2", "L2a2", "Ta2", "L0a3", "Eho", "L1a3", "Ta3", "Efin", "L2a3", "Ta4", "L0fin", "L1fin", "L2fin"),
+    "g0": ("X1p",),
+    "g1": ("L1s", "X0fin", "Er2", "Es4"),
+    "p2": ("Dr4", "Ts", "Ds5", "L2s", "X1fin", "Sa2"),
+    "tail": ("Er3", "X2p", "Er4", "L0s", "Es5", "Sa3", "L1a0", "Sa4", "Ta0", "Dsh", "X2fin", "L2a0", "Dho", "L0a0", "L1a1", "Dfin", "L2a1", "Ta1", "L0a1", "Esh", "L1a2", "L2a2", "L0a2", "Ta2", "L1a3", "Eho", "L2a3", "Ta3", "Efin", "L0a3", "Ta4", "L1fin", "L2fin", "L0fin"),
 }
 
 
@@ -478,7 +478,7 @@
         return rows_in, out_load, up_load, down_load
 
     def attend_phase(
-        start_loads, x_t, w_q, w_kv, q, k, v, sc, probs, ctx, box2, own_load, w_sem, out_sem, p_sem, ctx_sem
+        start_loads, x_t, w_q, w_kv, q, k, v, sc, probs, ctx, box2, raw, own_load, w_sem, out_sem, p_sem, ctx_sem
     ):
         loads = [
             pltpu.make_async_copy(qkv_w.at[:, of_half(0, core)], w_q, w_sem.at[0]),
@@ -525,7 +525,7 @@
 
         def sines(pg, side_place):
             for at in (2 * side_place, 2 * side_place + 1):
-                rows = box[pg, at]
+                rows = box[pg, at].astype(f32)
                 spread = [
                     jnp.broadcast_to(rows[c : c + 1], (freq.shape[0] // 4, LANES)) for c in range(4)
                 ]
@@ -578,20 +578,17 @@
             place = jnp.where(place >= keys, place - keys, place)
             valid = place < lengths[pg]
 
-            @pl.loop(0, pairs)
-            def _(hp):
-                both = sc[pg]
-                cosine2, sine2 = turned(both)
-                basis = both.astype(low)
-                basis_q = (both[:chip] * scale).astype(low)
-                left = lane_halves((chip, LANES))
-                cosine_q = jnp.where(left, -cosine2[:chip], cosine2[:chip]) * scale
-                sine_q = jnp.where(left, sine2[:chip], -sine2[:chip]) * scale
+            both = sc[pg]
+            cosine2, sine2 = turned(both)
+            basis = both.astype(low)
+            basis_q = (both[:chip] * scale).astype(low)
+            left = lane_halves((chip, LANES))
+            cosine_q = jnp.where(left, -cosine2[:chip], cosine2[:chip]) * scale
+            sine_q = jnp.where(left, sine2[:chip], -sine2[:chip]) * scale
+            for hp in range(pairs):
                 q_pair, k_pair = q[pg, hp], k[pg, hp]
                 q_proj = dot(q_pair, box2[...])
                 k_proj = dot(k_pair, box2[...])
-                v_t = v[pg, hp].T
-                outs = []
                 for e in range(2):
                     at = slice(e * LANES, (e + 1) * LANES)
                     q_pos = rotate_key(q_proj[:, at], cosine_q, sine_q).astype(low)
@@ -602,16 +599,20 @@
                         jnp.concatenate([basis, k_pos], 1), jnp.concatenate([q_pos, basis_q], 1)
                     )
                     scores = scores + dot_nt(k_pair, q_own)
-                    scores = jnp.where(valid, scores, -1e30)
+                    raw[2 * hp + e] = jnp.where(valid, scores, -1e30)
+            for hp in range(pairs):
+                for e in range(2):
+                    scores = raw[2 * hp + e]
                     top = jnp.max(scores, axis=0, keepdims=True)
                     grown = jnp.exp(scores - top)
                     total = jnp.sum(grown, axis=0, keepdims=True)
-                    p = (grown * (1.0 / total)).astype(low)
-                    probs[pg, hp, e] = p
-                    outs.append(dot(v_t[e * LANES // 2 : (e + 1) * LANES // 2], p))
+                    probs[pg, hp, e] = (grown * (1.0 / total)).astype(low)
                 pltpu.make_async_copy(probs.at[pg, hp], p_hbm.at[pg, hp], p_sem.at[pg, hp]).start()
+            for hp in range(pairs):
+                v_t = v[pg, hp].T
+                outs = [dot(v_t[e * head : (e + 1) * head], probs[pg, hp, e]) for e in range(2)]
                 context = jnp.concatenate(outs, 0).T.astype(low)
-                lanes = pl.ds(pl.multiple_of(hp * LANES, LANES), LANES)
+                lanes = slice(hp * LANES, (hp + 1) * LANES)
                 ctx[pg, 0, :, lanes] = context[: chip // 2]
                 ctx[pg, 1, :, lanes] = context[chip // 2 :]
 
@@ -661,16 +662,21 @@
         hidden_t[...] = first.astype(low).T
         grow[...] = first + row(down_b)
 
-        @pl.loop(0, chunks)
-        def _(j):
+        for j in range(chunks):
             up_load(j).wait()
-            upper = dot(hidden[...], w_up[j]) + up_rows[pl.ds(j, 1)]
-            cdf = 0.5 + 0.5 * lax.erf(upper * 0.7071067811865476)
-            act_low = (upper * cdf).astype(low)
-            act[j] = act_low
-            slope[j] = (cdf + upper * (jnp.exp(upper * upper * -0.5) * 0.3989422804014327)).astype(low)
             down_load(j).wait()
-            grow[...] += dot(act_low, w_down[j])
+
+        @pl.loop(0, chunks // 2)
+        def _(step):
+            for j in (2 * step, 2 * step + 1):
+                upper = dot(hidden[...], w_up[j]) + up_rows[pl.ds(j, 1)]
+                cdf = 0.5 + 0.5 * lax.erf(upper * 0.7071067811865476)
+                act[j] = (upper * cdf).astype(low)
+                slope[j] = (cdf + upper * (jnp.exp(upper * upper * -0.5) * 0.3989422804014327)).astype(low)
+
+        @pl.loop(0, chunks // 2)
+        def _(step):
+            grow[...] += dot(act[2 * step], w_down[2 * step]) + dot(act[2 * step + 1], w_down[2 * step + 1])
 
         normed2, inverse2 = norm_of(grow[...])
         output[...] = (normed2 * row(gain2) + row(shift2)).astype(low)
@@ -702,12 +708,17 @@
         up_end = up_pieces * shard // 2
         per_half = up_end + shard // 2
 
+        @pl.loop(0, chunks // 2)
+        def _(step):
+            dffn = staged[...]
+            for j in (2 * step, 2 * step + 1):
+                act[j] = (dot_nt(dffn, w_down[j]) * slope[j].astype(f32)).astype(low)
+
         @pl.loop(0, chunks)
         def _(step):
             at_step(step, ["f%d" % at for at in range(chunks)])
             j = lax.rem(step + first_chunk, chunks)
-            dffn = staged[...]
-            dupper = (dot_nt(dffn, w_down[j]) * slope[j].astype(f32)).astype(low)
+            dupper = act[j]
             g_rows[pl.ds(8 + j, 1), :chunk] = column_sum(dupper.astype(f32))
             grow[...] += dot_nt(dupper, w_up[j])
             grad_up = dot(hidden_t[...], dupper).astype(low)
@@ -977,6 +988,7 @@
             vmem((pages, pairs, 2, keys, chip), low),
             vmem((pages, 2, block, half), low),
             vmem((2 * box_w.shape[0], 2 * box_w.shape[1]), low),
+            vmem((2 * pairs, keys, chip), f32),
             dma((pages, 2)), dma((3,)), dma((pages, 5)), dma((pages, pairs)), dma((pages,)),
         )
         pl.run_scoped(
@@ -1030,7 +1042,7 @@
     count = pos // 8
     freqs = 10000.0 ** (-np.arange(count) / count)
     freq = jnp.asarray(np.tile(np.tile(freqs, 4)[:, None], (1, LANES)), f32)
-    boxes_t = boxes.astype(f32).transpose(0, 2, 1)
+    boxes_t = boxes.transpose(0, 2, 1)
     chip, keys = 2 * block, 4 * block
     rows = pages * block
     half = width // 2
@@ -1055,7 +1067,7 @@
     ]
     scratch = [
         vmem((pages, 4, block, width), low),
-        vmem((pages, 4, 4, LANES), f32),
+        vmem((pages, 4, 4, LANES), jnp.int32),
         vmem((pages, block, width), low),
         vmem((pages, block, width), f32),
         vmem((pages, block, width), low),

time: 130 us -> 120 us (0.923)
  Pallas kernels: 126 us -> 117 us
    pallas_call x1, Pallas kernels: 122 us -> 113 us  [layer(): pl.pallas_call(functools.partial(layer_kernel, summed), out_shape=tuple(o...]
where the time goes in v5:
time: 120 us; the launch traced here: 118 us
  Pallas kernels  117 us (98%)
    pallas_call x1, Pallas kernels, layer(): pl.pallas_call(functools.partial(layer_kernel, summed), out_shape=tuple(o...  113 us
    pallas_call x1, Pallas kernels, finish(): pl.pallas_call(finish_kernel, out_shape=tuple((struct(shape, f32) for sha...  4.16 us

profile of v5, /device:TPU:9, one launch (start us, length us, event | category | flops | bytes accessed | tf_op | source)
XLA Modules:
  0.0 118.2 jit_solution(4795967992438971981)
XLA Ops:
  0.7 113.3 %layer.1 = (bf16[3,768,512]{2,1,0:T(8,128)(2,1)}, bf16[3,3,256,128]{3,2,1,0:T(8,128)(2,1)}, bf16[3,3,512,128]{3,2,1,0:T(8,128)(2,1)}, bf16[3,3,512,128]{3,2,1,0:...) custom-call(bf16[3,128,768]{2,1,0:T(8,128)(2,1)} %tokens_in.1, ...), custom_call_target="tpu_custom_call" | custom-call | tf_op jit(solution)/shard_map/layer/pallas_call | solution.py:1113
  113.9 4.2 %finish.1 = (f32[96,3072]{1,0:T(8,128)}, f32[384,768]{1,0:T(8,128)}, f32[96,768]{1,0:T(8,128)}, f32[96,2304]{1,0:T(8,128)}, f32[288]{0:T(512)}, /*index=5*/f32[8...) custom-call(bf16[2,3,2,240,128]{4,3,2,1,0:T(8,128)(2,1)} %get-tuple-, ...), custom_call_target="tpu_custom_call" | custom-call | tf_op jit(solution)/shard_map/finish/pallas_call | solution.py:1195

commit v6 on v5

--- a/solution.py
+++ b/solution.py
@@ -111,7 +111,7 @@
     "f2": ("Dc3",),
     "fe": ("Dr0", "Ds2", "Ds3"),
     "fw": ("Ss",),
-    "b0": ("Ec2", "Ec0", "Es0", "Ec3", "Ec1", "Es1", "Dr1", "Dr2"),
+    "b0": ("Dr1", "Dr2"),
     "b2": ("Sa0", "Dr3"),
     "b4": ("Er0", "Es2", "Ds4", "Es3", "X0p"),
     "q1": ("Sa1", "Er1"),
@@ -119,6 +119,7 @@
     "g1": ("L1s", "X0fin", "Er2", "Es4"),
     "p2": ("Dr4", "Ts", "Ds5", "L2s", "X1fin", "Sa2"),
     "tail": ("Er3", "X2p", "Er4", "L0s", "Es5", "Sa3", "L1a0", "Sa4", "Ta0", "Dsh", "X2fin", "L2a0", "Dho", "L0a0", "L1a1", "Dfin", "L2a1", "Ta1", "L0a1", "Esh", "L1a2", "L2a2", "L0a2", "Ta2", "L1a3", "Eho", "L2a3", "Ta3", "Efin", "L0a3", "Ta4", "L1fin", "L2fin", "L0fin"),
+    "bs": ("Ec2", "Ec0", "Es0", "Ec3", "Ec1", "Es1"),
 }
 
 
@@ -666,17 +667,17 @@
             up_load(j).wait()
             down_load(j).wait()
 
-        @pl.loop(0, chunks // 2)
+        @pl.loop(0, chunks // 3)
         def _(step):
-            for j in (2 * step, 2 * step + 1):
+            for j in (3 * step, 3 * step + 1, 3 * step + 2):
                 upper = dot(hidden[...], w_up[j]) + up_rows[pl.ds(j, 1)]
                 cdf = 0.5 + 0.5 * lax.erf(upper * 0.7071067811865476)
                 act[j] = (upper * cdf).astype(low)
                 slope[j] = (cdf + upper * (jnp.exp(upper * upper * -0.5) * 0.3989422804014327)).astype(low)
 
-        @pl.loop(0, chunks // 2)
+        @pl.loop(0, chunks // 3)
         def _(step):
-            grow[...] += dot(act[2 * step], w_down[2 * step]) + dot(act[2 * step + 1], w_down[2 * step + 1])
+            grow[...] += sum(dot(act[3 * step + at], w_down[3 * step + at]) for at in range(3))
 
         normed2, inverse2 = norm_of(grow[...])
         output[...] = (normed2 * row(gain2) + row(shift2)).astype(low)
@@ -691,17 +692,19 @@
         grow[...] = dresid2
         staged[...] = dffn
 
-        @pl.loop(0, chunks)
-        def _(j):
-            grad_down = dot_tn(act[j], staged[...]).astype(low)
-            for piece in range(up_pieces):
-                at = j * up_pieces + piece
-                per = up_pieces * chunks // 8
-                rows = pl.ds(pl.multiple_of((at % per) * LANES, LANES), LANES)
-                for column in range(6):
-                    packed_down[column, at // per, rows] = grad_down[
-                        piece * LANES : (piece + 1) * LANES, column * LANES : (column + 1) * LANES
-                    ]
+        @pl.loop(0, chunks // 2)
+        def _(step):
+            dffn = staged[...]
+            for j in (2 * step, 2 * step + 1):
+                grad_down = dot_tn(act[j], dffn).astype(low)
+                for piece in range(up_pieces):
+                    at = j * up_pieces + piece
+                    per = up_pieces * chunks // 8
+                    rows = pl.ds(pl.multiple_of((at % per) * LANES, LANES), LANES)
+                    for column in range(6):
+                        packed_down[column, at // per, rows] = grad_down[
+                            piece * LANES : (piece + 1) * LANES, column * LANES : (column + 1) * LANES
+                        ]
 
         if summed:
             down.swap(range(3))
@@ -783,6 +786,7 @@
                 p_load(hp, pg).start()
         for copy in w_loads:
             copy.start()
+        at_place("bs")
 
         def late(hp):
             return LateSum(ways, LATE_ORDERS, hp, late_packed, late_held, late_got, late_out, late_sems)

time: 120 us -> 119 us (level)
  no operation moved by 1% of the time
where the time goes in v6:
time: 119 us; the launch traced here: 117 us
  Pallas kernels  116 us (97%)
    pallas_call x1, Pallas kernels, layer(): pl.pallas_call(functools.partial(layer_kernel, summed), out_shape=tuple(o...  112 us
    pallas_call x1, Pallas kernels, finish(): pl.pallas_call(finish_kernel, out_shape=tuple((struct(shape, f32) for sha...  4.16 us

profile of v6, /device:TPU:9, one launch (start us, length us, event | category | flops | bytes accessed | tf_op | source)
XLA Modules:
  0.0 117.3 jit_solution(859453258595637754)
XLA Ops:
  0.7 112.3 %layer.1 = (bf16[3,768,512]{2,1,0:T(8,128)(2,1)}, bf16[3,3,256,128]{3,2,1,0:T(8,128)(2,1)}, bf16[3,3,512,128]{3,2,1,0:T(8,128)(2,1)}, bf16[3,3,512,128]{3,2,1,0:...) custom-call(bf16[3,128,768]{2,1,0:T(8,128)(2,1)} %tokens_in.1, ...), custom_call_target="tpu_custom_call" | custom-call | tf_op jit(solution)/shard_map/layer/pallas_call | solution.py:1117
  113.0 4.2 %finish.1 = (f32[96,3072]{1,0:T(8,128)}, f32[384,768]{1,0:T(8,128)}, f32[96,768]{1,0:T(8,128)}, f32[96,2304]{1,0:T(8,128)}, f32[288]{0:T(512)}, /*index=5*/f32[8...) custom-call(bf16[2,3,2,240,128]{4,3,2,1,0:T(8,128)(2,1)} %get-tuple-, ...), custom_call_target="tpu_custom_call" | custom-call | tf_op jit(solution)/shard_map/finish/pallas_call | solution.py:1199
